TPU v7x, 32 devices: a whole 2x2x4 slice. The times are simulated.
32 devices in a mesh: groups: 2 (over y), tm: 4 (over x, core), space: 4 (over z).
Axes of the slice: x: 2, y: 2, z: 4, core: 2. Of those that a mesh axis runs over, the one named last changes fastest.
Arguments:
- query: bfloat16 [8192, 1536], P(('groups', 'tm', 'space')), parts along dimension 0, may hold values from -24 to 24
- key_in: bfloat16 [8192, 1536], P(('groups', 'tm', 'space')), parts along dimension 0, may hold values from -24 to 24
- value_in: bfloat16 [8192, 1536], P(('groups', 'tm', 'space')), parts along dimension 0, may hold values from -12 to 12
- grad_out: bfloat16 [8192, 1536], P(('groups', 'tm', 'space')), parts along dimension 0, may hold values from -48 to 48
- frame_ids: int32 [8192], P(('groups', 'tm', 'space')), parts along dimension 0, may hold values from 0 to 15, as said below
- time_ids: int32 [8192], P(('groups', 'tm', 'space')), parts along dimension 0, may hold values from 0 to 3, as said below
- tile_valid: int32 [8, 4], P(('groups', 'tm'), 'space'), parts along dimension 0, may hold values from 128 to 256
Outputs:
- query_grad: bfloat16 [8192, 1536], P(('groups', 'tm', 'space')), parts along dimension 0
- key_grad: bfloat16 [8192, 1536], P(('groups', 'tm', 'space')), parts along dimension 0
- value_grad: bfloat16 [8192, 1536], P(('groups', 'tm', 'space')), parts along dimension 0
There are 2 independent parts, one for each index of `groups`. A program takes and returns all parts, laid end to end along the dimension named above; each array names one. Nothing has to cross between parts.
Inputs may be any that keep to these rules, and one draw needn't show every extreme that they name: `frame_ids`: in every block the first 16 rows carry the ids 0 to 15 in order. `time_ids`: in every block the first 4 rows carry the ids 0 to 3 in order.
All inputs are finite; a program needn't handle non-finite values.
Results may differ from a plain program's by a relative error of at most 0.0072.
Values may be sent and summed in bfloat16 or wider, within the bound.
No kernel may reach another device: no remote copies, remote signals or barrier semaphores. Data moves between devices by JAX's collectives and lax.ppermute only.
A program may use at most 64 MiB of HBM per device.

v0:
```python
import jax
import jax.numpy as jnp
from jax import lax
from jax.sharding import PartitionSpec as P

HD = 128
WIN = 64
WIN_FRAME = 4
KF = 16
KT = 4


MASK_FILL = -1e30


def member_table(labels_in, live_rows, groups):
    labels = lax.iota(jnp.int32, groups)
    return (labels_in[:, None] == labels[None, :]) & live_rows[:, None]


def pooled_pair(member, key_in, value_in):
    table = member.astype(jnp.bfloat16)
    counts = jnp.sum(member.astype(jnp.float32), axis=0)
    sums_k = jnp.einsum("tc,tf->cf", table, key_in, preferred_element_type=jnp.float32)
    sums_v = jnp.einsum("tc,tf->cf", table, value_in, preferred_element_type=jnp.float32)
    return (
        (sums_k / counts[:, None]).astype(jnp.bfloat16),
        (sums_v / counts[:, None]).astype(jnp.bfloat16),
        counts,
    )


def attend(query, key_in, value_in, masked_grad, live_rows, coarse_k, coarse_v):
    length, features = query.shape
    windows = length // WIN
    head_count = features // HD
    factor = HD ** (-0.5)
    query_heads = query.reshape(windows, WIN, head_count, HD)
    key_heads = key_in.reshape(windows, WIN, head_count, HD)
    value_heads = value_in.reshape(windows, WIN, head_count, HD)
    grad_heads = masked_grad.reshape(windows, WIN, head_count, HD)
    coarse_kh = coarse_k.reshape(-1, head_count, HD)
    coarse_vh = coarse_v.reshape(-1, head_count, HD)
    window_score = (
        jnp.einsum("wqhd,wkhd->wqhk", query_heads, key_heads, preferred_element_type=jnp.float32)
        * factor
    )
    window_score = jnp.where(live_rows.reshape(windows, 1, 1, WIN), window_score, MASK_FILL)
    coarse_score = (
        jnp.einsum("wqhd,khd->wqhk", query_heads, coarse_kh, preferred_element_type=jnp.float32)
        * factor
    )
    row_max = jnp.maximum(jnp.max(window_score, axis=-1), jnp.max(coarse_score, axis=-1))[..., None]
    window_exp = jnp.exp(window_score - row_max)
    coarse_exp = jnp.exp(coarse_score - row_max)
    row_sum = (jnp.sum(window_exp, axis=-1) + jnp.sum(coarse_exp, axis=-1))[..., None]
    window_weight = window_exp / row_sum
    coarse_weight = coarse_exp / row_sum
    window_wb = window_weight.astype(jnp.bfloat16)
    coarse_wb = coarse_weight.astype(jnp.bfloat16)
    attended = jnp.einsum(
        "wqhk,wkhd->wqhd", window_wb, value_heads, preferred_element_type=jnp.float32
    )
    attended = attended + jnp.einsum(
        "wqhk,khd->wqhd", coarse_wb, coarse_vh, preferred_element_type=jnp.float32
    )
    delta = jnp.sum(grad_heads.astype(jnp.float32) * attended, axis=-1, keepdims=True)
    window_dp = jnp.einsum(
        "wqhd,wkhd->wqhk", grad_heads, value_heads, preferred_element_type=jnp.float32
    )
    coarse_dp = jnp.einsum(
        "wqhd,khd->wqhk", grad_heads, coarse_vh, preferred_element_type=jnp.float32
    )
    window_ds = (factor * window_weight * (window_dp - delta)).astype(jnp.bfloat16)
    coarse_ds = (factor * coarse_weight * (coarse_dp - delta)).astype(jnp.bfloat16)
    query_grad = jnp.einsum(
        "wqhk,wkhd->wqhd", window_ds, key_heads, preferred_element_type=jnp.float32
    )
    query_grad = query_grad + jnp.einsum(
        "wqhk,khd->wqhd", coarse_ds, coarse_kh, preferred_element_type=jnp.float32
    )
    window_kg = jnp.einsum(
        "wqhk,wqhd->wkhd", window_ds, query_heads, preferred_element_type=jnp.float32
    )
    window_vg = jnp.einsum(
        "wqhk,wqhd->wkhd", window_wb, grad_heads, preferred_element_type=jnp.float32
    )
    return (
        query_grad.reshape(length, features),
        window_kg.reshape(length, features),
        window_vg.reshape(length, features),
        coarse_ds,
        coarse_wb,
        query_heads,
        grad_heads,
    )


def coarse_terms(coarse_ds, coarse_wb, query_heads, grad_heads, offset, amount):
    ds_part = lax.dynamic_slice_in_dim(coarse_ds, offset, amount, 3)
    wb_part = lax.dynamic_slice_in_dim(coarse_wb, offset, amount, 3)
    grad_k = jnp.einsum("wqhk,wqhd->khd", ds_part, query_heads, preferred_element_type=jnp.float32)
    grad_v = jnp.einsum("wqhk,wqhd->khd", wb_part, grad_heads, preferred_element_type=jnp.float32)
    return jnp.concatenate([grad_k.reshape(amount, -1), grad_v.reshape(amount, -1)], axis=1)


def spread(member, counts, grads):
    share = grads / counts[:, None]
    return jnp.dot(member.astype(jnp.float32), share, precision=lax.Precision.HIGHEST)


def body(query, key_in, value_in, grad_out, frame_ids, time_ids, tile_valid):
    length, features = query.shape
    tile_span = WIN_FRAME * WIN
    live_rows = lax.iota(jnp.int32, length) % tile_span < tile_valid.reshape(())
    frame_member = member_table(frame_ids, live_rows, KF)
    time_member = member_table(time_ids, live_rows, KT)
    frame_k, frame_v, frame_count = pooled_pair(frame_member, key_in, value_in)
    time_k, time_v, time_count = pooled_pair(time_member, key_in, value_in)
    frame_k_all, frame_v_all = (
        lax.all_gather(frame_k, "tm", axis=0, tiled=True),
        lax.all_gather(frame_v, "tm", axis=0, tiled=True),
    )
    time_k_all, time_v_all = (
        lax.all_gather(time_k, "space", axis=0, tiled=True),
        lax.all_gather(time_v, "space", axis=0, tiled=True),
    )
    coarse_k = jnp.concatenate([frame_k_all, time_k_all], axis=0)
    coarse_v = jnp.concatenate([frame_v_all, time_v_all], axis=0)
    masked_grad = grad_out * live_rows[:, None].astype(jnp.bfloat16)
    query_grad, window_kg, window_vg, coarse_ds, coarse_wb, query_heads, grad_heads = attend(
        query, key_in, value_in, masked_grad, live_rows, coarse_k, coarse_v
    )
    frame_rows = frame_k_all.shape[0]
    frame_terms = coarse_terms(coarse_ds, coarse_wb, query_heads, grad_heads, 0, frame_rows)
    frame_grads = lax.psum_scatter(
        frame_terms.astype(jnp.bfloat16), "tm", scatter_dimension=0, tiled=True
    ).astype(jnp.float32)
    time_terms = coarse_terms(
        coarse_ds, coarse_wb, query_heads, grad_heads, frame_rows, time_k_all.shape[0]
    )
    time_grads = lax.psum_scatter(
        time_terms.astype(jnp.bfloat16), "space", scatter_dimension=0, tiled=True
    ).astype(jnp.float32)
    back = spread(frame_member, frame_count, frame_grads) + spread(
        time_member, time_count, time_grads
    )
    key_grad = (window_kg + back[:, :features]).astype(jnp.bfloat16)
    value_grad = (window_vg + back[:, features:]).astype(jnp.bfloat16)
    return (query_grad.astype(jnp.bfloat16), key_grad, value_grad)


def solution(mesh):
    placed = (
        P(("groups", "tm", "space"), None),
        P(("groups", "tm", "space"), None),
        P(("groups", "tm", "space"), None),
        P(("groups", "tm", "space"), None),
        P(("groups", "tm", "space")),
        P(("groups", "tm", "space")),
        P(("groups", "tm"), "space"),
    )
    return jax.shard_map(
        body,
        mesh=mesh,
        in_specs=placed,
        out_specs=(
            P(("groups", "tm", "space"), None),
            P(("groups", "tm", "space"), None),
            P(("groups", "tm", "space"), None),
        ),
        check_vma=False,
    )
```

profile of v0, /device:TPU:0, one launch (start us, length us, event | category | flops | bytes accessed | tf_op | source)
XLA Modules:
  0.0 123.1 jit_solution(1480777043557902272)
XLA Ops:
  8.1 2.4 %reshape.105 = bf16[4,64,12,128]{3,2,1,0:T(8,128)(2,1)} reshape(bf16[256,1536]{1,0:T(8,128)(2,1)} %param.9) | data formatting | bytes 1572864 | tf_op jit(solution)/shard_map/reshape | solution.py:40
  10.5 1.5 %reshape.101 = bf16[4,64,12,128]{3,2,1,0:T(8,128)(2,1)} reshape(bf16[256,1536]{1,0:T(8,128)(2,1)S(1)} %copy-done.10) | data formatting | bytes 1572864 | tf_op jit(solution)/shard_map/reshape | solution.py:39
  13.1 0.8 fusion.4
  14.5 0.5 reshape.102
  15.1 0.6 fusion.73
  15.9 14.7 %all-gather = bf16[4,4,1536]{2,1,0:T(4,128)(2,1)S(1)} all-gather(bf16[1,4,1536]{2,1,0:T(4,128)(2,1)S(1)} %fusion.5), channel_id=1, replica_groups=mesh['groups'=2,'tm'=4,'space'=4] {'space'}, dimensions={0}, use_global_device_ids=true | all-gather | bytes 61440 | tf_op jit(solution)/shard_map/all_gather | solution.py:125
  30.6 5.6 %all_gather.12 = bf16[64,1536]{1,0:T(8,128)(2,1)S(1)} all-gather(bf16[16,1536]{1,0:T(8,128)(2,1)S(1)} %fusion), channel_id=1, replica_groups=mesh['groups'=2,'tm'=4,'space'=4] {'tm'}, dimensions={0}, use_global_device_ids=true | all-gather | bytes 245760 | tf_op jit(solution)/shard_map/all_gather | solution.py:121
  36.2 0.7 copy-done.14
  37.2 0.5 bitcast_reduce_fusion
  37.8 0.4 copy-done.12
  38.1 0.6 bitcast_reduce_fusion.1
  38.8 0.4 fusion.16
  39.2 0.9 fusion.18
  40.2 0.4 copy-done.19
  40.6 1.7 %fusion.33 = f32[4,12,64,128]{3,2,1,0:T(8,128)} fusion(bf16[4,64,12,128]{3,2,1,0:T(8,128)(2,1)S(1)} %copy-done.19, f32[4,64,12]{1,2,0:T(8,128)S(1)} %copy_add_fusion, f32[4,64,12]{1,2,0:T(8,128)S(1)} %copy_maximum_fusion, f32[4,12,64,64]{3,2,1,0:T(8,128)S(1)} %get-tuple-element.8), kind=kOutput, calls=%fused_computation.56 | convolution fusion | flops 50921472 | bytes 3170304 | tf_op jit(solution)/shard_map/wqhk,wkhd->wqhd/dot_general | solution.py:61
  42.3 1.7 %fusion.44 = bf16[4,64,12,80]{3,1,0,2:T(8,128)(2,1)} fusion(f32[4,64,12]{1,0,2:T(4,128)S(1)} %copy.168, f32[4,64,12]{1,0,2:T(4,128)S(1)} %copy.160, f32[12,80,256]{1,2,0:S(1)} %fusion.47), kind=kLoop, calls=%fused_computation.69 | loop fusion | flops 983040 | bytes 1499136 | tf_op jit(solution)/shard_map/convert_element_type | solution.py:60
  44.1 1.5 %reshape.104 = bf16[4,64,12,128]{3,2,1,0:T(8,128)(2,1)} reshape(bf16[256,1536]{1,0:T(8,128)(2,1)S(1)} %broadcast_multiply_fusion) | data formatting | bytes 1572864 | tf_op jit(solution)/shard_map/reshape | solution.py:41
  45.6 13.1 %all-gather.1 = bf16[4,4,1536]{2,1,0:T(4,128)(2,1)S(1)} all-gather(bf16[1,4,1536]{2,1,0:T(4,128)(2,1)S(1)} %copy-done.22), channel_id=1, replica_groups=mesh['groups'=2,'tm'=4,'space'=4] {'space'}, dimensions={0}, use_global_device_ids=true | all-gather | bytes 61440 | tf_op jit(solution)/shard_map/all_gather | solution.py:126
  58.7 5.6 %all_gather.14 = bf16[64,1536]{1,0:T(8,128)(2,1)S(1)} all-gather(bf16[16,1536]{1,0:T(8,128)(2,1)S(1)} %fusion.1), channel_id=1, replica_groups=mesh['groups'=2,'tm'=4,'space'=4] {'tm'}, dimensions={0}, use_global_device_ids=true | all-gather | bytes 245760 | tf_op jit(solution)/shard_map/all_gather | solution.py:122
  64.3 1.6 %copy.174 = bf16[4,64,12,128]{3,1,0,2:T(8,128)(2,1)S(1)} copy(bf16[4,64,12,128]{3,2,1,0:T(8,128)(2,1)} %reshape.104) | data formatting | bytes 1572864 | tf_op jit(solution)/shard_map/reshape | solution.py:41
  65.9 1.6 %fusion.22 = bf16[12,8,8,128]{3,2,1,0:T(8,128)(2,1)S(1)} fusion(bf16[4,64,12,128]{3,1,0,2:T(8,128)(2,1)S(1)} %copy.174, bf16[4,64,12,80]{3,1,0,2:T(8,128)(2,1)} %fusion.44), kind=kOutput, calls=%fused_computation.42 | convolution fusion | flops 50429952 | bytes 1474560 | tf_op jit(solution)/shard_map/wqhk,wqhd->khd/dot_general | solution.py:103
  67.5 0.7 fusion.10
  68.1 0.3 fusion.45
  68.5 1.6 %multiply_convert_fusion = bf16[4,64,12,80]{3,1,0,2:T(8,128)(2,1)S(1)} fusion(f32[4,64,12,80]{3,1,0,2:T(8,128)S(1)} %bitcast.187, f32[4,64,12]{1,0,2:T(4,128)S(1)} %copy.175, f32[4,64,12]{1,0,2:T(4,128)S(1)} %copy.168, f32[4,64,12]{1,0,2:T(4,128)S(1)} %copy.160, f32[12,80,256]{1,2,0:S(1)} %fusion.47), kind=kLoop, calls=%fused_computation.29 | loop fusion | flops 1720320 | bytes 2494464 | tf_op jit(solution)/shard_map/convert_element_type | solution.py:75
  70.1 0.9 copy-done
  71.0 0.4 fusion.21
  71.4 0.8 pad_maximum_fusion
  72.5 0.8 fusion.25
  73.2 0.8 fusion.26
  74.0 0.6 pad_maximum_fusion.1
  74.7 2.6 %fusion.12 = bf16[4,64,12,64]{1,3,2,0:T(8,128)(2,1)S(1)} fusion(f32[4,64,12]{1,2,0:T(8,128)S(1)} %fusion.10, bf16[4,64,12,128]{3,2,1,0:T(8,128)(2,1)} %reshape.105, f32[4,64,12]{1,2,0:T(8,128)S(1)} %copy_add_fusion, f32[4,64,12]{1,2,0:T(8,128)S(1)} %copy_maximum_fusion, f32[4,12,64,64]{3,2,1,0:T(8,128)} %copy-done.16, bf16[4,64,12,128]{3,2,1,0:T(8,128)(2,1)S(1)} %copy-done.9), kind=kOutput, calls=%fused_computation.22 | convolution fusion | flops 51511296 | bytes 2789376 | tf_op jit(solution)/shard_map/wqhd,wkhd->wqhk/dot_general | solution.py:68
  77.4 0.5 convolution_bitcast_fusion
  77.9 0.7 copy-done.13
  78.6 0.4 fusion.38
  79.0 0.8 copy-done.7
  79.8 0.4 convolution_bitcast_fusion.1
  80.2 0.6 copy-done.15
  80.8 0.4 fusion.8
  81.1 0.5 copy.178
  81.7 1.1 copy.265
  82.8 2.3 %copy.194 = f32[4,64,12,128]{3,2,1,0:T(8,128)} copy(f32[4,64,12,128]{3,1,2,0:T(8,128)S(1)} %convolution_bitcast_fusion) | data formatting | bytes 3145728 | tf_op jit(solution)/shard_map/wqhk,wqhd->wkhd/transpose | solution.py:85
  85.0 2.2 %copy.180 = f32[4,64,12,128]{3,2,1,0:T(8,128)} copy(f32[4,64,12,128]{3,1,2,0:T(8,128)S(1)} %convolution_bitcast_fusion.1) | data formatting | bytes 3145728 | tf_op jit(solution)/shard_map/wqhk,wqhd->wkhd/transpose | solution.py:82
  87.3 0.6 dynamic-slice
  88.5 5.9 %reduce-scatter.2.cloned.1.call-done = bf16[16,3072]{1,0:T(8,128)(2,1)} async-done(((bf16[64,3072]{1,0:T(8,128)(2,1)}), bf16[16,3072]{1,0:T(8,128)(2,1)}) %reduce-scatter.2.cloned.1.call-update) | async-done | bytes 98320 | tf_op jit(solution)/shard_map/reduce_scatter | solution.py:136
  94.5 2.3 %fusion.53 = f32[256,3072]{1,0:T(8,128)S(1)} fusion(bf16[16,3072]{1,0:T(8,128)(2,1)} %reduce-scatter.2.cloned.1.call-done, f32[16]{0:T(128)S(1)} %copy-done.32, s32[256]{0:T(256)S(1)} %copy-done.26, pred[256]{0:T(512)(128)(4,1)S(1)} %copy-done.28), kind=kOutput, calls=%fused_computation.84 | convolution fusion | flops 151101440 | bytes 3245376 | tf_op jit(solution)/shard_map/dot_general | solution.py:109
  96.8 14.1 %all-reduce.3.cloned.1.call-done = bf16[16,3072]{1,0:T(8,128)(2,1)} async-done(((bf16[16,3072]{1,0:T(8,128)(2,1)}), bf16[16,3072]{1,0:T(8,128)(2,1)}) %all-reduce.3.cloned.1.call-update) | async-done | bytes 98320
  110.9 2.5 %convolution_add_fusion = f32[256,3072]{1,0:T(8,128)S(1)} fusion(f32[256,3072]{1,0:T(8,128)S(1)} %fusion.53, pred[256,4]{0,1:T(4,128)(4,1)S(1)} %copy-done.24, bf16[16,3072]{1,0:T(8,128)(2,1)} %all-reduce.3.cloned.1.call-done, u32[]{:T(128)S(6)} %multiply.9, f32[4]{0:T(128)S(1)} %copy-done.30), kind=kOutput, calls=%fused_computation | convolution fusion | flops 38559744 | bytes 6317076 | tf_op jit(solution)/shard_map/dot_general | solution.py:109
  113.4 2.2 %fusion.6 = (bf16[256,1536]{1,0:T(8,128)(2,1)}, bf16[256,1536]{1,0:T(8,128)(2,1)}) fusion(f32[32,8,12,128]{3,2,1,0:T(8,128)S(1)} %bitcast.185, f32[256,3072]{1,0:T(8,128)S(1)} %convolution_add_fusion, f32[32,8,12,128]{3,2,1,0:T(8,128)S(1)} %bitcast.186), kind=kLoop, calls=%fused_computation.12 | loop fusion | flops 1572864 | bytes 7864320 | tf_op jit(solution)/shard_map/convert_element_type | solution.py:149
  (88 shorter events, 2.1 us)
Async XLA Ops:
  8.0 2.5 %copy-start.10 = (bf16[256,1536]{1,0:T(8,128)(2,1)S(1)}, bf16[256,1536]{1,0:T(8,128)(2,1)}, u32[]{:S(2)}) copy-start(bf16[256,1536]{1,0:T(8,128)(2,1)} %param.8) | copy-start | bytes 2359300
  8.0 4.7 %copy-start.33 = (s32[256]{0:T(256)S(1)}, s32[256]{0:T(256)}, u32[]{:S(2)}) copy-start(s32[256]{0:T(256)} %param.12) | copy-start | bytes 3076
  8.0 86.4 %reduce-scatter.2.cloned.1.call-start = ((), (), s32[]{:S(2)}) async-start(), calls=%async_computation.1 | async-start | bytes 491520 | tf_op jit(solution)/shard_map/reduce_scatter | solution.py:136
  10.5 2.6 %copy-start.11 = (bf16[256,1536]{1,0:T(8,128)(2,1)S(1)}, bf16[256,1536]{1,0:T(8,128)(2,1)}, u32[]{:S(2)}) copy-start(bf16[256,1536]{1,0:T(8,128)(2,1)} %param.9) | copy-start | bytes 2359300
  10.5 3.4 %copy-start.25 = (s32[256]{0:T(256)S(1)}, s32[256]{0:T(256)}, u32[]{:S(2)}) copy-start(s32[256]{0:T(256)} %param.11) | copy-start | bytes 3076
  12.7 1.8 %copy-start.27 = (pred[256]{0:T(512)(128)(4,1)}, pred[256]{0:T(512)(128)(4,1)S(1)}, u32[]{:S(2)}) copy-start(pred[256]{0:T(512)(128)(4,1)S(1)} %fusion.74) | copy-start | bytes 772
  12.9 1.4 %copy-start.23 = (pred[256,4]{0,1:T(4,128)(4,1)}, pred[256,4]{0,1:T(4,128)(4,1)S(1)}, u32[]{:S(2)}) copy-start(pred[256,4]{0,1:T(4,128)(4,1)S(1)} %get-tuple-element.4) | copy-start | bytes 3076
  12.9 1.4 %copy-start.29 = (f32[4]{0:T(128)}, f32[4]{0:T(128)S(1)}, u32[]{:S(2)}) copy-start(f32[4]{0:T(128)S(1)} %get-tuple-element.3) | copy-start | bytes 52
  12.9 1.6 %copy-start.20 = (bf16[256,1536]{1,0:T(8,128)(2,1)S(1)}, bf16[256,1536]{1,0:T(8,128)(2,1)}, u32[]{:S(2)}) copy-start(bf16[256,1536]{1,0:T(8,128)(2,1)} %param.7) | copy-start | bytes 2359300
  14.0 1.0 copy-start.31
  15.1 22.7 %copy-start.6 = (bf16[4,64,12,128]{3,2,1,0:T(8,128)(2,1)}, bf16[4,64,12,128]{3,2,1,0:T(8,128)(2,1)S(1)}, u32[]{:S(2)}) copy-start(bf16[4,64,12,128]{3,2,1,0:T(8,128)(2,1)S(1)} %reshape.102) | copy-start | bytes 2359300
  36.2 0.7 copy-start.14
  36.9 1.2 copy-start.12
  36.9 1.2 copy-start.35
  38.8 1.4 %copy-start.16 = (f32[4,12,64,64]{3,2,1,0:T(8,128)}, f32[4,12,64,64]{3,2,1,0:T(8,128)S(1)}, u32[]{:S(2)}) copy-start(f32[4,12,64,64]{3,2,1,0:T(8,128)S(1)} %get-tuple-element.8) | copy-start | bytes 2359300
  38.8 1.8 %copy-start.19 = (bf16[4,64,12,128]{3,2,1,0:T(8,128)(2,1)S(1)}, bf16[4,64,12,128]{3,2,1,0:T(8,128)(2,1)}, u32[]{:S(2)}) copy-start(bf16[4,64,12,128]{3,2,1,0:T(8,128)(2,1)} %reshape.105) | copy-start | bytes 2359300
  42.2 1.7 %copy-start.21 = (bf16[256,1536]{1,0:T(8,128)(2,1)S(1)}, bf16[256,1536]{1,0:T(8,128)(2,1)}, u32[]{:S(2)}) copy-start(bf16[256,1536]{1,0:T(8,128)(2,1)} %param.10) | copy-start | bytes 2359300
  44.0 1.7 %copy-start.22 = (bf16[1,4,1536]{2,1,0:T(4,128)(2,1)S(1)}, bf16[1,4,1536]{2,1,0:T(4,128)(2,1)}, u32[]{:S(2)}) copy-start(bf16[1,4,1536]{2,1,0:T(4,128)(2,1)} %fusion.4) | copy-start | bytes 36868
  64.3 3.1 %copy-start.2 = (bf16[4,64,12,80]{3,1,0,2:T(8,128)(2,1)S(1)}, bf16[4,64,12,80]{3,1,0,2:T(8,128)(2,1)}, u32[]{:S(2)}) copy-start(bf16[4,64,12,80]{3,1,0,2:T(8,128)(2,1)} %fusion.44) | copy-start | bytes 1474564
  64.3 3.1 %copy-start.8 = (bf16[4,64,12,128]{3,2,1,0:T(8,128)(2,1)S(1)}, bf16[4,64,12,128]{3,2,1,0:T(8,128)(2,1)}, u32[]{:S(2)}) copy-start(bf16[4,64,12,128]{3,2,1,0:T(8,128)(2,1)} %reshape.104) | copy-start | bytes 2359300
  64.3 3.1 %copy-start.18 = (f32[4,12,64,128]{3,2,1,0:T(8,128)S(1)}, f32[4,12,64,128]{3,2,1,0:T(8,128)}, u32[]{:S(2)}) copy-start(f32[4,12,64,128]{3,2,1,0:T(8,128)} %fusion.33) | copy-start | bytes 4718596
  70.1 0.9 copy-start
  71.0 1.5 %copy-start.3 = (bf16[4,64,12,80]{3,1,0,2:T(8,128)(2,1)S(1)}, bf16[4,64,12,80]{3,1,0,2:T(8,128)(2,1)}, u32[]{:S(2)}) copy-start(bf16[4,64,12,80]{3,1,0,2:T(8,128)(2,1)} %fusion.44) | copy-start | bytes 1474564
  71.4 1.8 %copy-start.1 = (bf16[4,64,12,80]{3,1,0,2:T(8,128)(2,1)S(1)}, bf16[4,64,12,80]{3,1,0,2:T(8,128)(2,1)}, u32[]{:S(2)}) copy-start(bf16[4,64,12,80]{3,1,0,2:T(8,128)(2,1)} %copy-done) | copy-start | bytes 1474564
  72.2 38.7 %all-reduce.3.cloned.1.call-start = ((), (), s32[]{:S(2)}) async-start(), calls=%async_computation.2 | async-start | bytes 196608
  73.2 1.5 %copy-start.9 = (bf16[4,64,12,128]{3,2,1,0:T(8,128)(2,1)S(1)}, bf16[4,64,12,128]{3,2,1,0:T(8,128)(2,1)}, u32[]{:S(2)}) copy-start(bf16[4,64,12,128]{3,2,1,0:T(8,128)(2,1)} %reshape.104) | copy-start | bytes 2359300
  74.7 2.6 %copy-start.17 = (f32[4,12,64,64]{3,2,1,0:T(8,128)S(1)}, f32[4,12,64,64]{3,2,1,0:T(8,128)}, u32[]{:S(2)}) copy-start(f32[4,12,64,64]{3,2,1,0:T(8,128)} %copy-done.16) | copy-start | bytes 2359300
  77.4 1.2 copy-start.13
  78.6 1.2 %copy-start.7 = (bf16[4,64,12,128]{3,2,1,0:T(8,128)(2,1)S(1)}, bf16[4,64,12,128]{3,2,1,0:T(8,128)(2,1)}, u32[]{:S(2)}) copy-start(bf16[4,64,12,128]{3,2,1,0:T(8,128)(2,1)} %copy-done.6) | copy-start | bytes 2359300
  79.8 0.9 copy-start.15
  85.0 2.3 %copy-start.34 = (u32[32]{0:T(128)S(1)}, u32[32]{0:T(128)}, u32[]{:S(2)}) copy-start(u32[32]{0:T(128)} %constant.36) | copy-start | bytes 388
  85.0 9.4 %copy-start.26 = (s32[256]{0:T(256)S(1)}, s32[256]{0:T(256)}, u32[]{:S(2)}) copy-start(s32[256]{0:T(256)} %param.11) | copy-start | bytes 3076
  85.0 9.4 %copy-start.28 = (pred[256]{0:T(512)(128)(4,1)S(1)}, pred[256]{0:T(512)(128)(4,1)}, u32[]{:S(2)}) copy-start(pred[256]{0:T(512)(128)(4,1)} %copy-done.27) | copy-start | bytes 772
  85.0 9.4 %copy-start.32 = (f32[16]{0:T(128)S(1)}, f32[16]{0:T(128)}, u32[]{:S(2)}) copy-start(f32[16]{0:T(128)} %copy-done.31) | copy-start | bytes 196
  88.5 22.4 %copy-start.24 = (pred[256,4]{0,1:T(4,128)(4,1)S(1)}, pred[256,4]{0,1:T(4,128)(4,1)}, u32[]{:S(2)}) copy-start(pred[256,4]{0,1:T(4,128)(4,1)} %copy-done.23) | copy-start | bytes 3076
  88.5 22.4 %copy-start.30 = (f32[4]{0:T(128)S(1)}, f32[4]{0:T(128)}, u32[]{:S(2)}) copy-start(f32[4]{0:T(128)} %copy-done.29) | copy-start | bytes 52
  110.9 2.5 %copy-start.4 = (f32[4,64,12,128]{3,2,1,0:T(8,128)S(1)}, f32[4,64,12,128]{3,2,1,0:T(8,128)}, u32[]{:S(2)}) copy-start(f32[4,64,12,128]{3,2,1,0:T(8,128)} %copy.194) | copy-start | bytes 4718596
  110.9 2.5 %copy-start.5 = (f32[4,64,12,128]{3,2,1,0:T(8,128)S(1)}, f32[4,64,12,128]{3,2,1,0:T(8,128)}, u32[]{:S(2)}) copy-start(f32[4,64,12,128]{3,2,1,0:T(8,128)} %copy.180) | copy-start | bytes 4718596
Sparse Core Ops, SparseCore 0:
  72.4 22.0 reduce-scatter.1
Sparse Core Ops, SparseCore 1:
  75.6 35.3 all-reduce.2
where the time goes:
time: 123 us
  blocking collectives  39 us (32%)
  waiting for transfers between devices  20.1 us (16%)
  local copies, waits for them, and re-layouts  19.2 us (16%)
  matrix products  17.6 us (14%)
  between operations  17.2 us (14%)
  other arithmetic  9.65 us (8%)
    all_gather x1, blocking collectives, body(): lax.all_gather(time_k, 'space', axis=0, tiled=True)  14.7 us
    unnamed x3, waiting for transfers between devices  14.1 us
    all_gather x1, blocking collectives, body(): lax.all_gather(time_v, 'space', axis=0, tiled=True)  13.1 us
    unnamed x76, local copies, waits for them, and re-layouts  6.24 us
    reduce_scatter x1, waiting for transfers between devices, body(): lax.psum_scatter(frame_terms.astype(jnp.bfloat16), 'tm', scatter_dimensio...  5.92 us
    all_gather x1, blocking collectives, body(): lax.all_gather(frame_v, 'tm', axis=0, tiled=True)  5.61 us
    all_gather x1, blocking collectives, body(): lax.all_gather(frame_k, 'tm', axis=0, tiled=True)  5.61 us
    dot_general x2, matrix products, spread(): jnp.dot(member.astype(jnp.float32), share, precision=lax.Precision.HIGHEST)  4.81 us
  transfers between devices with their start and end apart: 2, of which 2 were waited for; matrix products, arithmetic and copies ran while one was open for 13% of the time, Pallas kernels for 0%

commit v1 on v0

v1 whole, which is shorter than its diff:
```python
import functools
import math

import jax
import jax.numpy as jnp
from jax import lax
from jax.experimental import pallas as pl
from jax.experimental.pallas import tpu as pltpu
from jax.sharding import PartitionSpec as P

HD = 128
WIN = 64
WIN_FRAME = 4
KF = 16
KT = 4
PAIR = 2 * WIN
SPAN = WIN_FRAME * WIN

MASK_FILL = -1e30
FACTOR = HD ** (-0.5)
LIMIT = 24 * 1024 * 1024

VMEM = pl.BlockSpec(memory_space=pltpu.VMEM)
SMEM = pl.BlockSpec(memory_space=pltpu.SMEM)


def dot(a, b, dims):
    return lax.dot_general(a, b, (dims, ((), ())), preferred_element_type=jnp.float32)


NT = ((1,), (1,))
NN = ((1,), (0,))
TN = ((0,), (0,))


def call(kernel, outs, ins, flops, moved):
    return pl.pallas_call(
        kernel,
        out_shape=outs,
        in_specs=[SMEM if i.shape == (1, 1) else VMEM for i in ins],
        out_specs=[VMEM] * len(outs),
        compiler_params=pltpu.CompilerParams(vmem_limit_bytes=LIMIT),
        cost_estimate=pl.CostEstimate(
            flops=flops, bytes_accessed=moved, transcendentals=0
        ),
    )(*ins)


def member_rows(valid, frame, time, length):
    rows = KF + 8
    label = lax.broadcasted_iota(jnp.int32, (rows, length), 0)
    place = lax.broadcasted_iota(jnp.int32, (rows, length), 1) % SPAN
    ids = jnp.where(label < KF, frame, time + KF)
    return jnp.where((ids == label) & (place < valid), 1.0, 0.0)


def pool_kernel(valid_ref, frame_ref, time_ref, k_ref, v_ref, f_ref, t_ref):
    length, features = k_ref.shape
    member = member_rows(valid_ref[0, 0], frame_ref[...], time_ref[...], length)
    share = 1.0 / jnp.maximum(jnp.sum(member, axis=1, keepdims=True), 1.0)
    table = member.astype(jnp.bfloat16)
    for ref, at in ((k_ref, 0), (v_ref, features)):
        pooled = dot(table, ref[...], NN) * share
        f_ref[:, at : at + features] = pooled[:KF].astype(jnp.bfloat16)
        t_ref[:, at : at + features] = pooled[KF : KF + KT].astype(jnp.bfloat16)


def coarse_rows(refs, at):
    parts = [r[:, at : at + HD].astype(jnp.float32) for r in refs]
    return jnp.concatenate(parts, axis=0).astype(jnp.bfloat16)


def weigh_kernel(counts, valid_ref, q_ref, k_ref, v_ref, g_ref, *refs):
    coarse = refs[: counts[0]]
    outs = refs[counts[0] :]
    dsw_ref, ww_ref, dsc_ref = outs[:3]
    term_refs = outs[3:]
    length, features = q_ref.shape
    heads = features // HD
    valid = valid_ref[0, 0]
    live = lax.broadcasted_iota(jnp.int32, (length, HD), 0) % SPAN < valid
    lane = lax.broadcasted_iota(jnp.int32, (WIN, PAIR), 1)
    row = lax.broadcasted_iota(jnp.int32, (WIN, PAIR), 0)
    first = lane < WIN
    place = row + jnp.where(first, 0, WIN)
    scale = FACTOR * math.log2(math.e)
    for h in range(heads):
        at = h * HD
        kc = coarse_rows(coarse, at)
        vc = coarse_rows(coarse, features + at)
        q = q_ref[:, at : at + HD]
        g = jnp.where(live, g_ref[:, at : at + HD], 0)
        ds_parts, w_parts = [], []
        for p in range(length // PAIR):
            rows = slice(p * PAIR, (p + 1) * PAIR)
            keys = jnp.concatenate([k_ref[rows, at : at + HD], kc], axis=0)
            values = jnp.concatenate([v_ref[rows, at : at + HD], vc], axis=0)
            s = dot(keys, q[rows], NT)
            d = dot(values, g[rows], NT)
            sw = jnp.where(first, s[:WIN], s[WIN:PAIR])
            sw = jnp.where((place + p * PAIR) % SPAN < valid, sw, MASK_FILL)
            sc = s[PAIR:]
            dw = jnp.where(first, d[:WIN], d[WIN:PAIR])
            dc = d[PAIR:]
            top = jnp.maximum(
                jnp.max(sw, axis=0, keepdims=True), jnp.max(sc, axis=0, keepdims=True)
            )
            ew = jnp.exp2((sw - top) * scale)
            ec = jnp.exp2((sc - top) * scale)
            total = jnp.sum(ew, axis=0, keepdims=True) + jnp.sum(
                ec, axis=0, keepdims=True
            )
            inv = 1.0 / total
            ww = ew * inv
            wc = ec * inv
            delta = jnp.sum(ww * dw, axis=0, keepdims=True) + jnp.sum(
                wc * dc, axis=0, keepdims=True
            )
            dsw = (FACTOR * ww) * (dw - delta)
            dsc = (FACTOR * wc) * (dc - delta)
            lanes = slice(p * PAIR, (p + 1) * PAIR)
            dsw_ref[h, :, lanes] = dsw.astype(jnp.bfloat16)
            ww_ref[h, :, lanes] = ww.astype(jnp.bfloat16)
            ds_parts.append(dsc.astype(jnp.bfloat16))
            w_parts.append(wc.astype(jnp.bfloat16))
        dsc = jnp.concatenate(ds_parts, axis=1)
        wc = jnp.concatenate(w_parts, axis=1)
        dsc_ref[h] = dsc
        for term, start in (
            (dot(dsc, q, NN), at),
            (dot(wc, g, NN), features + at),
        ):
            begin = 0
            for ref in term_refs:
                amount = ref.shape[0]
                ref[:, start : start + HD] = term[begin : begin + amount].astype(
                    jnp.bfloat16
                )
                begin += amount


def window_kernel(
    counts, valid_ref, q_ref, k_ref, g_ref, dsw_ref, ww_ref, dsc_ref, *refs
):
    coarse = refs[: counts[0]]
    dq_ref, dk_ref, dv_ref = refs[counts[0] :]
    length, features = q_ref.shape
    valid = valid_ref[0, 0]
    live = lax.broadcasted_iota(jnp.int32, (length, HD), 0) % SPAN < valid
    first = lax.broadcasted_iota(jnp.int32, (WIN, PAIR), 1) < WIN
    zero = jnp.zeros((WIN, PAIR), jnp.bfloat16)

    def split(x):
        return jnp.concatenate(
            [jnp.where(first, x, zero), jnp.where(first, zero, x)], axis=0
        )

    for h in range(features // HD):
        at = h * HD
        kc = coarse_rows(coarse, at)
        for p in range(length // PAIR):
            rows = slice(p * PAIR, (p + 1) * PAIR)
            ds = split(dsw_ref[h, :, rows])
            w = split(ww_ref[h, :, rows])
            g = jnp.where(live[rows], g_ref[rows, at : at + HD], 0)
            dk_ref[rows, at : at + HD] = dot(ds, q_ref[rows, at : at + HD], NN)
            dv_ref[rows, at : at + HD] = dot(w, g, NN)
            keys = jnp.concatenate([k_ref[rows, at : at + HD], kc], axis=0)
            all_ds = jnp.concatenate([ds, dsc_ref[h, :, rows]], axis=0)
            dq_ref[rows, at : at + HD] = dot(all_ds, keys, TN).astype(jnp.bfloat16)


def spread_kernel(
    counts, valid_ref, frame_ref, time_ref, dk_ref, dv_ref, *refs
):
    f_refs = refs[: counts[0]]
    t_refs = refs[counts[0] : counts[0] + counts[1]]
    kg_ref, vg_ref = refs[counts[0] + counts[1] :]
    length, features = dk_ref.shape
    member = member_rows(valid_ref[0, 0], frame_ref[...], time_ref[...], length)
    share = 1.0 / jnp.maximum(jnp.sum(member, axis=1, keepdims=True), 1.0)
    both = jnp.concatenate([member, member], axis=0).astype(jnp.bfloat16)
    for out, grad, begin in ((kg_ref, dk_ref, 0), (vg_ref, dv_ref, features)):
        part = slice(begin, begin + features)
        f = functools.reduce(
            lambda a, b: a + b, [r[:, part].astype(jnp.float32) for r in f_refs]
        )
        t = functools.reduce(
            lambda a, b: a + b, [r[:, part].astype(jnp.float32) for r in t_refs]
        )
        pad = jnp.zeros((8 - KT, features), jnp.float32)
        grads = jnp.concatenate([f, t, pad], axis=0) * share
        high = grads.astype(jnp.bfloat16)
        low = (grads - high.astype(jnp.float32)).astype(jnp.bfloat16)
        terms = jnp.concatenate([high.astype(jnp.float32), low.astype(jnp.float32)], 0)
        back = dot(both, terms.astype(jnp.bfloat16), TN)
        out[...] = (grad[...] + back).astype(jnp.bfloat16)


def swap(x, axis, size, mask):
    return lax.ppermute(x, axis, [(i, i ^ mask) for i in range(size)])


def body(tm, space, query, key_in, value_in, grad_out, frame_ids, time_ids, tile_valid):
    length, features = query.shape
    heads = features // HD
    valid = tile_valid.reshape(1, 1)
    frame = frame_ids.reshape(1, length)
    time = time_ids.reshape(1, length)
    bf16, f32 = jnp.bfloat16, jnp.float32
    shape = jax.ShapeDtypeStruct
    size = length * features

    own_f, own_t = call(
        pool_kernel,
        [shape((KF, 2 * features), bf16), shape((KT, 2 * features), bf16)],
        [valid, frame, time, key_in, value_in],
        4 * size * (KF + KT),
        4 * size,
    )

    have_t = own_t
    mask = 1
    while mask < space:
        got = swap(have_t, "space", space, mask)
        mask *= 2
        if mask < space:
            have_t = jnp.concatenate([have_t, got], axis=0)
    time_parts = [have_t, got]
    from_1 = swap(own_f, "tm", tm, 1)
    from_2 = swap(own_f, "tm", tm, 2)
    from_3 = swap(from_2, "tm", tm, 1)
    coarse = [own_f, from_2, from_1, from_3] + time_parts
    total = tm * KF + space * KT

    half = space * KT // 2
    outs = [
        shape((heads, WIN, length), bf16),
        shape((heads, WIN, length), bf16),
        shape((heads, total, length), bf16),
        shape((2 * KF, 2 * features), bf16),
        shape((2 * KF, 2 * features), bf16),
        shape((half, 2 * features), bf16),
        shape((half, 2 * features), bf16),
    ]
    dsw, ww, dsc, f_keep, f_send, t_keep, t_send = call(
        functools.partial(weigh_kernel, (len(coarse),)),
        outs,
        [valid, query, key_in, value_in, grad_out] + coarse,
        4 * size * (PAIR + total) + 4 * size * total,
        8 * size,
    )

    mask = space // 2
    while True:
        got_t = swap(t_send, "space", space, mask)
        if mask == 1:
            break
        summed = (t_keep.astype(f32) + got_t.astype(f32)).astype(bf16)
        amount = summed.shape[0] // 2
        t_keep, t_send = summed[:amount], summed[amount:]
        mask //= 2
    got_f = swap(f_send, "tm", tm, 1)
    summed = (f_keep.astype(f32) + got_f.astype(f32)).astype(bf16)
    f_keep, f_send = summed[:KF], summed[KF:]
    got_f = swap(f_send, "tm", tm, 2)

    query_grad, dk, dv = call(
        functools.partial(window_kernel, (len(coarse),)),
        [
            shape((length, features), bf16),
            shape((length, features), f32),
            shape((length, features), f32),
        ],
        [valid, query, key_in, grad_out, dsw, ww, dsc] + coarse,
        2 * size * (PAIR + total) + 4 * size * PAIR,
        20 * size,
    )
    key_grad, value_grad = call(
        functools.partial(spread_kernel, (2, 2)),
        [shape((length, features), bf16), shape((length, features), bf16)],
        [valid, frame, time, dk, dv, f_keep, got_f, t_keep, got_t],
        8 * size * (KF + KT),
        12 * size,
    )
    return query_grad, key_grad, value_grad


def solution(mesh):
    tm, space = mesh.shape["tm"], mesh.shape["space"]
    rows = P(("groups", "tm", "space"), None)
    ids = P(("groups", "tm", "space"))
    return jax.shard_map(
        functools.partial(body, tm, space),
        mesh=mesh,
        in_specs=(rows, rows, rows, rows, ids, ids, P(("groups", "tm"), "space")),
        out_specs=(rows, rows, rows),
        check_vma=False,
    )
```

time: 123 us -> 35.9 us (0.29)
  blocking collectives: 39 us -> 0 us
  matrix products: 17.6 us -> 0 us
  between operations: 17.2 us -> 1.37 us
  local copies, waits for them, and re-layouts: 19.2 us -> 5.93 us
  waiting for transfers between devices: 20.1 us -> 7.77 us
  starting transfers between devices: 0.26 us -> 12.3 us
  other arithmetic: 9.65 us -> 0.09 us
  Pallas kernels: 0 us -> 8.08 us
    all_gather x4 -> x0, blocking collectives: 39 us -> none  [the longest x1 14.7 us: body(): lax.all_gather(time_k, 'space', axis=0, tiled=True)]
    dot_general x18 -> x0, matrix products: 16.9 us -> none  [the longest x2 4.81 us: spread(): jnp.dot(member.astype(jnp.float32), share, precision=lax.Precision.HIGHEST)]
    unnamed x3 -> x0, waiting for transfers between devices: 14.1 us -> none
    ppermute x0 -> x9, starting transfers between devices: none -> 12.3 us  [swap(): return lax.ppermute(x, axis, [(i, i ^ mask) for i in range(size)])]
    pallas_call x0 -> x4, Pallas kernels: none -> 8.08 us  [call(): pl.pallas_call(kernel, out_shape=outs, in_specs=[SMEM if i.shape == (1, 1...]
    reshape x8 -> x0, local copies, waits for them, and re-layouts: 7.88 us -> none  [the longest x2 3.09 us: attend(): grad_heads = masked_grad.reshape(windows, WIN, head_count, HD)]
    ppermute x0 -> x9, waiting for transfers between devices: none -> 7.77 us  [swap(): return lax.ppermute(x, axis, [(i, i ^ mask) for i in range(size)])]
    reduce_scatter x1 -> x0, waiting for transfers between devices: 5.92 us -> none  [body(): lax.psum_scatter(frame_terms.astype(jnp.bfloat16), 'tm', scatter_dimensio...]
  transfers between devices with their start and end apart: 2 -> 9, of which waited for: 2 -> 4; matrix products, arithmetic and copies ran while one was open for 13% -> 0% of each run, Pallas kernels for 0% -> 5%
where the time goes in v1:
time: 35.9 us; the launch traced here: 35.6 us
  starting transfers between devices  12.3 us (34%)
  Pallas kernels  8.08 us (23%)
  waiting for transfers between devices  7.77 us (22%)
  local copies, waits for them, and re-layouts  5.93 us (17%)
  between operations  1.37 us (4%)
    ppermute x9, starting transfers between devices, swap(): return lax.ppermute(x, axis, [(i, i ^ mask) for i in range(size)])  12.3 us
    pallas_call x4, Pallas kernels, call(): pl.pallas_call(kernel, out_shape=outs, in_specs=[SMEM if i.shape == (1, 1...  8.08 us
    ppermute x9, waiting for transfers between devices, swap(): return lax.ppermute(x, axis, [(i, i ^ mask) for i in range(size)])  7.77 us
    unnamed x20, local copies, waits for them, and re-layouts  5.89 us
  transfers between devices with their start and end apart: 9, of which 4 were waited for; matrix products, arithmetic and copies ran while one was open for 0% of the time, Pallas kernels for 5%

profile of v1, /device:TPU:0, one launch (start us, length us, event | category | flops | bytes accessed | tf_op | source)
XLA Modules:
  0.0 35.6 jit_solution(6929925307582831859)
XLA Ops:
  1.3 0.0 copy-start
  1.3 1.1 %copy-done = bf16[256,1536]{1,0:T(8,128)(2,1)S(1)} copy-done((bf16[256,1536]{1,0:T(8,128)(2,1)S(1)}, bf16[256,1536]{1,0:T(8,128)(2,1)}, u32[]{:S(2)}) %copy-start) | copy-done | bytes 786456
  2.4 0.0 copy-start.4
  2.4 1.1 %copy-done.4 = bf16[256,1536]{1,0:T(8,128)(2,1)S(1)} copy-done((bf16[256,1536]{1,0:T(8,128)(2,1)S(1)}, bf16[256,1536]{1,0:T(8,128)(2,1)}, u32[]{:S(2)}) %copy-start.4) | copy-done | bytes 786456
  3.5 0.0 copy-start.6
  3.5 0.7 %copy-done.6 = s32[256]{0:T(256)S(1)} copy-done((s32[256]{0:T(256)S(1)}, s32[256]{0:T(256)}, u32[]{:S(2)}) %copy-start.6) | copy-done | bytes 1048
  4.2 0.0 copy-start.8
  4.2 0.7 %copy-done.8 = s32[256]{0:T(256)S(1)} copy-done((s32[256]{0:T(256)S(1)}, s32[256]{0:T(256)}, u32[]{:S(2)}) %copy-start.8) | copy-done | bytes 1048
  4.9 0.0 copy-start.1
  4.9 0.0 copy-start.2
  4.9 0.4 %shard_map.94 = (bf16[16,3072]{1,0:T(8,128)(2,1)S(1)}, bf16[4,3072]{1,0:T(4,128)(2,1)S(1)}) custom-call(s32[1,1]{1,0:T(1,128)S(6)} %copy.10.valid_ref, s32[1,256]{1,0:T(1,128)S(1)} %bitcast.2, s32[1,256]{1,0:T(1,128)S(1)} %bitcast.4, bf16[256,1536]{1,0:T(8,128)(2,1)S(1)} %copy-done, bf16[256,1536]{1,0:T(8,128)(2,1)S(1)} %copy-done.4), custom_call_target="tpu_custom_call" | custom-call | flops 31457280 | bytes 1572864 | tf_op jit(solution)/shard_map/pallas_call | solution.py:37
  5.3 3.0 %collective-permute-start = (bf16[16,3072]{1,0:T(8,128)(2,1)S(1)}, bf16[16,3072]{1,0:T(8,128)(2,1)S(1)}, u32[]{:S(2)}, u32[]{:S(2)}) collective-permute-start(bf16[16,3072]{1,0:T(8,128)(2,1)S(1)} %get-tuple-element.17.refs_0_), channel_id=1, source_target_pairs={{0,8},{4,12},{8,0},{12,4},{1,9},{5,13},{9,1},{13,5},{2,10},{6,14},... | collective-permute-start | bytes 294920 | tf_op jit(solution)/shard_map/ppermute | solution.py:201
  8.3 1.6 %collective-permute-start.3 = (bf16[4,3072]{1,0:T(4,128)(2,1)S(1)}, bf16[4,3072]{1,0:T(4,128)(2,1)S(1)}, u32[]{:S(2)}, u32[]{:S(2)}) collective-permute-start(bf16[4,3072]{1,0:T(4,128)(2,1)S(1)} %get-tuple-element.18), channel_id=1, source_target_pairs={{0,1},{1,0},{2,3},{3,2},{4,5},{5,4},{6,7},{7,6},{8,9},{9,8},{10,11... | collective-permute-start | bytes 73736 | tf_op jit(solution)/shard_map/ppermute | solution.py:201
  9.8 0.0 collective-permute-start.1
  9.8 1.2 %collective-permute-done.refs_1_ = bf16[16,3072]{1,0:T(8,128)(2,1)S(1)} collective-permute-done((bf16[16,3072]{1,0:T(8,128)(2,1)S(1)}, bf16[16,3072]{1,0:T(8,128)(2,1)S(1)}, u32[]{:S(2)}, u32[]{:S(2)}) %collective-permute-start) | collective-permute-done | bytes 98336 | tf_op jit(solution)/shard_map/ppermute | solution.py:201
  11.1 0.0 collective-permute-start.2
  11.1 1.0 %collective-permute-done.3 = bf16[4,3072]{1,0:T(4,128)(2,1)S(1)} collective-permute-done((bf16[4,3072]{1,0:T(4,128)(2,1)S(1)}, bf16[4,3072]{1,0:T(4,128)(2,1)S(1)}, u32[]{:S(2)}, u32[]{:S(2)}) %collective-permute-start.3) | collective-permute-done | bytes 24608 | tf_op jit(solution)/shard_map/ppermute | solution.py:201
  12.1 2.7 %collective-permute-start.4 = (bf16[8,3072]{1,0:T(8,128)(2,1)S(1)}, bf16[8,3072]{1,0:T(8,128)(2,1)S(1)}, u32[]{:S(2)}, u32[]{:S(2)}) collective-permute-start(bf16[8,3072]{1,0:T(8,128)(2,1)S(1)} %pad_maximum_fusion.refs_4_), channel_id=1, source_target_pairs={{0,2},{1,3},{2,0},{3,1},{4,6},{5,7},{6,4},{7,5},{8,10},{9,11},{10,... | collective-permute-start | bytes 147464 | tf_op jit(solution)/shard_map/ppermute | solution.py:201
  14.8 2.8 %collective-permute-done.4.refs_5_ = bf16[8,3072]{1,0:T(8,128)(2,1)S(1)} collective-permute-done((bf16[8,3072]{1,0:T(8,128)(2,1)S(1)}, bf16[8,3072]{1,0:T(8,128)(2,1)S(1)}, u32[]{:S(2)}, u32[]{:S(2)}) %collective-permute-start.4) | collective-permute-done | bytes 49184 | tf_op jit(solution)/shard_map/ppermute | solution.py:201
  17.6 0.0 collective-permute-done.1.refs_2_
  17.6 0.0 collective-permute-done.2.refs_3_
  17.6 0.0 copy-done.1
  17.6 0.0 copy-done.2
  17.6 0.0 copy-start.3
  17.6 1.1 %copy-done.3 = bf16[256,1536]{1,0:T(8,128)(2,1)S(1)} copy-done((bf16[256,1536]{1,0:T(8,128)(2,1)S(1)}, bf16[256,1536]{1,0:T(8,128)(2,1)}, u32[]{:S(2)}) %copy-start.3) | copy-done | bytes 786456
  18.7 0.0 copy-start.5
  18.7 1.1 %copy-done.5 = bf16[256,1536]{1,0:T(8,128)(2,1)S(1)} copy-done((bf16[256,1536]{1,0:T(8,128)(2,1)S(1)}, bf16[256,1536]{1,0:T(8,128)(2,1)}, u32[]{:S(2)}) %copy-start.5) | copy-done | bytes 786456
  19.8 4.3 %shard_map.95 = (bf16[12,64,256]{2,1,0:T(8,128)(2,1)S(1)}, bf16[12,64,256]{2,1,0:T(8,128)(2,1)S(1)}, bf16[12,80,256]{2,1,0:T(8,128)(2,1)S(1)}, bf16[32,3072]{1,0...) custom-call(s32[1,1]{1,0:T(1,128)S(6)} %copy.10.valid_ref, ...), custom_call_target="tpu_custom_call" | custom-call | flops 452984832 | bytes 3145728 | tf_op jit(solution)/shard_map/pallas_call | solution.py:37
  24.1 2.3 %collective-permute-start.7 = (bf16[8,3072]{1,0:T(8,128)(2,1)S(1)}, bf16[8,3072]{1,0:T(8,128)(2,1)S(1)}, u32[]{:S(2)}, u32[]{:S(2)}) collective-permute-start(bf16[8,3072]{1,0:T(8,128)(2,1)S(1)} %get-tuple-element.28), channel_id=1, source_target_pairs={{0,2},{1,3},{2,0},{3,1},{4,6},{5,7},{6,4},{7,5},{8,10},{9,11},{10,... | collective-permute-start | bytes 147464 | tf_op jit(solution)/shard_map/ppermute | solution.py:201
  26.4 0.0 collective-permute-start.5
  26.4 2.7 %collective-permute-done.7 = bf16[8,3072]{1,0:T(8,128)(2,1)S(1)} collective-permute-done((bf16[8,3072]{1,0:T(8,128)(2,1)S(1)}, bf16[8,3072]{1,0:T(8,128)(2,1)S(1)}, u32[]{:S(2)}, u32[]{:S(2)}) %collective-permute-start.7) | collective-permute-done | bytes 49184 | tf_op jit(solution)/shard_map/ppermute | solution.py:201
  29.2 0.0 collective-permute-done.5
  29.3 0.6 %collective-permute-start.6 = (bf16[16,3072]{1,0:T(8,128)(2,1)S(1)}, bf16[16,3072]{1,0:T(8,128)(2,1)S(1)}, u32[]{:S(2)}, u32[]{:S(2)}) collective-permute-start(bf16[16,3072]{1,0:T(8,128)(2,1)S(1)} %get-tuple-element.31), channel_id=1, source_target_pairs={{0,8},{4,12},{8,0},{12,4},{1,9},{5,13},{9,1},{13,5},{2,10},{6,14},... | collective-permute-start | bytes 294920 | tf_op jit(solution)/shard_map/ppermute | solution.py:201
  29.8 2.2 %collective-permute-start.8 = (bf16[4,3072]{1,0:T(4,128)(2,1)S(1)}, bf16[4,3072]{1,0:T(4,128)(2,1)S(1)}, u32[]{:S(2)}, u32[]{:S(2)}) collective-permute-start(bf16[4,3072]{1,0:T(4,128)(2,1)S(1)} %get-tuple-element.33), channel_id=1, source_target_pairs={{0,1},{1,0},{2,3},{3,2},{4,5},{5,4},{6,7},{7,6},{8,9},{9,8},{10,11... | collective-permute-start | bytes 73736 | tf_op jit(solution)/shard_map/ppermute | solution.py:201
  32.1 0.0 copy-start.7
  32.1 0.0 copy-start.9
  32.1 1.9 %shard_map.96 = (bf16[256,1536]{1,0:T(8,128)(2,1)}, f32[256,1536]{1,0:T(8,128)S(1)}, f32[256,1536]{1,0:T(8,128)S(1)}) custom-call(s32[1,1]{1,0:T(1,128)S(6)} %copy.10.valid_ref, bf16[256,1536]{1,0:T(8,128)(2,1)S(1)} %copy-done.2, bf16[256,1536]{1,0:T(8,128)(2,1)S(1)} %copy-done.1, bf16[256,1536]{1,0:T(8,128)(2,1)S(1)} %copy-done.3, ...), custom_call_target="tpu_custom_call" | custom-call | flops 364904448 | bytes 7864320 | tf_op jit(solution)/shard_map/pallas_call | solution.py:37
  34.0 0.0 collective-permute-done.8.refs_3_
  34.0 0.0 collective-permute-done.6.refs_1_
  34.0 0.0 copy-done.7
  34.0 0.0 copy-done.9
  34.0 1.6 %shard_map.97 = (bf16[256,1536]{1,0:T(8,128)(2,1)}, bf16[256,1536]{1,0:T(8,128)(2,1)}) custom-call(s32[1,1]{1,0:T(1,128)S(6)} %copy.10.valid_ref, s32[1,256]{1,0:T(1,128)S(1)} %bitcast.3, s32[1,256]{1,0:T(1,128)S(1)} %bitcast.5, f32[256,1536]{1,0:T(8,128)S(1)} %get-tuple-element.23.dk_ref, f32[256,1536]{1,0:T(8,128)S(1)} %get-tuple-element.24.dv_ref, ...), custom_call_target="tpu_custom_call" | custom-call | flops 62914560 | bytes 4718592 | tf_op jit(solution)/shard_map/pallas_call | solution.py:37
  (5 shorter events, 0.1 us)
Async XLA Ops:
  1.3 1.1 %copy-start = (bf16[256,1536]{1,0:T(8,128)(2,1)S(1)}, bf16[256,1536]{1,0:T(8,128)(2,1)}, u32[]{:S(2)}) copy-start(bf16[256,1536]{1,0:T(8,128)(2,1)} %k_ref.5) | copy-start | bytes 2359300
  2.4 1.1 %copy-start.4 = (bf16[256,1536]{1,0:T(8,128)(2,1)S(1)}, bf16[256,1536]{1,0:T(8,128)(2,1)}, u32[]{:S(2)}) copy-start(bf16[256,1536]{1,0:T(8,128)(2,1)} %v_ref.3) | copy-start | bytes 2359300
  3.5 0.7 %copy-start.6 = (s32[256]{0:T(256)S(1)}, s32[256]{0:T(256)}, u32[]{:S(2)}) copy-start(s32[256]{0:T(256)} %param.11) | copy-start | bytes 3076
  4.2 0.7 %copy-start.8 = (s32[256]{0:T(256)S(1)}, s32[256]{0:T(256)}, u32[]{:S(2)}) copy-start(s32[256]{0:T(256)} %param.12) | copy-start | bytes 3076
  4.9 12.7 %copy-start.1 = (bf16[256,1536]{1,0:T(8,128)(2,1)S(1)}, bf16[256,1536]{1,0:T(8,128)(2,1)}, u32[]{:S(2)}) copy-start(bf16[256,1536]{1,0:T(8,128)(2,1)} %k_ref.5) | copy-start | bytes 2359300
  4.9 12.7 %copy-start.2 = (bf16[256,1536]{1,0:T(8,128)(2,1)S(1)}, bf16[256,1536]{1,0:T(8,128)(2,1)}, u32[]{:S(2)}) copy-start(bf16[256,1536]{1,0:T(8,128)(2,1)} %q_ref.3) | copy-start | bytes 2359300
  5.3 5.8 %collective-permute-start = (bf16[16,3072]{1,0:T(8,128)(2,1)S(1)}, bf16[16,3072]{1,0:T(8,128)(2,1)S(1)}, u32[]{:S(2)}, u32[]{:S(2)}) collective-permute-start(bf16[16,3072]{1,0:T(8,128)(2,1)S(1)} %get-tuple-element.17.refs_0_), channel_id=1, source_target_pairs={{0,8},{4,12},{8,0},{12,4},{1,9},{5,13},{9,1},{13,5},{2,10},{6,14},... | collective-permute-start | bytes 294920 | tf_op jit(solution)/shard_map/ppermute | solution.py:201
  8.3 3.8 %collective-permute-start.3 = (bf16[4,3072]{1,0:T(4,128)(2,1)S(1)}, bf16[4,3072]{1,0:T(4,128)(2,1)S(1)}, u32[]{:S(2)}, u32[]{:S(2)}) collective-permute-start(bf16[4,3072]{1,0:T(4,128)(2,1)S(1)} %get-tuple-element.18), channel_id=1, source_target_pairs={{0,1},{1,0},{2,3},{3,2},{4,5},{5,4},{6,7},{7,6},{8,9},{9,8},{10,11... | collective-permute-start | bytes 73736 | tf_op jit(solution)/shard_map/ppermute | solution.py:201
  9.8 7.7 %collective-permute-start.1 = (bf16[16,3072]{1,0:T(8,128)(2,1)S(1)}, bf16[16,3072]{1,0:T(8,128)(2,1)S(1)}, u32[]{:S(2)}, u32[]{:S(2)}) collective-permute-start(bf16[16,3072]{1,0:T(8,128)(2,1)S(1)} %get-tuple-element.17.refs_0_), channel_id=1, source_target_pairs={{0,4},{4,0},{8,12},{12,8},{1,5},{5,1},{9,13},{13,9},{2,6},{6,2},{1... | collective-permute-start | bytes 294920 | tf_op jit(solution)/shard_map/ppermute | solution.py:201
  11.1 6.5 %collective-permute-start.2 = (bf16[16,3072]{1,0:T(8,128)(2,1)S(1)}, bf16[16,3072]{1,0:T(8,128)(2,1)S(1)}, u32[]{:S(2)}, u32[]{:S(2)}) collective-permute-start(bf16[16,3072]{1,0:T(8,128)(2,1)S(1)} %collective-permute-done.refs_1_), channel_id=1, source_target_pairs={{0,4},{4,0},{8,12},{12,8},{1,5},{5,1},{9,13},{13,9},{2,6},{6,2},{1... | collective-permute-start | bytes 294920 | tf_op jit(solution)/shard_map/ppermute | solution.py:201
  12.1 5.4 %collective-permute-start.4 = (bf16[8,3072]{1,0:T(8,128)(2,1)S(1)}, bf16[8,3072]{1,0:T(8,128)(2,1)S(1)}, u32[]{:S(2)}, u32[]{:S(2)}) collective-permute-start(bf16[8,3072]{1,0:T(8,128)(2,1)S(1)} %pad_maximum_fusion.refs_4_), channel_id=1, source_target_pairs={{0,2},{1,3},{2,0},{3,1},{4,6},{5,7},{6,4},{7,5},{8,10},{9,11},{10,... | collective-permute-start | bytes 147464 | tf_op jit(solution)/shard_map/ppermute | solution.py:201
  17.6 1.1 %copy-start.3 = (bf16[256,1536]{1,0:T(8,128)(2,1)S(1)}, bf16[256,1536]{1,0:T(8,128)(2,1)}, u32[]{:S(2)}) copy-start(bf16[256,1536]{1,0:T(8,128)(2,1)} %g_ref.3) | copy-start | bytes 2359300
  18.7 1.1 %copy-start.5 = (bf16[256,1536]{1,0:T(8,128)(2,1)S(1)}, bf16[256,1536]{1,0:T(8,128)(2,1)}, u32[]{:S(2)}) copy-start(bf16[256,1536]{1,0:T(8,128)(2,1)} %v_ref.3) | copy-start | bytes 2359300
  24.1 5.1 %collective-permute-start.7 = (bf16[8,3072]{1,0:T(8,128)(2,1)S(1)}, bf16[8,3072]{1,0:T(8,128)(2,1)S(1)}, u32[]{:S(2)}, u32[]{:S(2)}) collective-permute-start(bf16[8,3072]{1,0:T(8,128)(2,1)S(1)} %get-tuple-element.28), channel_id=1, source_target_pairs={{0,2},{1,3},{2,0},{3,1},{4,6},{5,7},{6,4},{7,5},{8,10},{9,11},{10,... | collective-permute-start | bytes 147464 | tf_op jit(solution)/shard_map/ppermute | solution.py:201
  26.4 2.8 %collective-permute-start.5 = (bf16[32,3072]{1,0:T(8,128)(2,1)S(1)}, bf16[32,3072]{1,0:T(8,128)(2,1)S(1)}, u32[]{:S(2)}, u32[]{:S(2)}) collective-permute-start(bf16[32,3072]{1,0:T(8,128)(2,1)S(1)} %get-tuple-element.26), channel_id=1, source_target_pairs={{0,4},{4,0},{8,12},{12,8},{1,5},{5,1},{9,13},{13,9},{2,6},{6,2},{1... | collective-permute-start | bytes 589832 | tf_op jit(solution)/shard_map/ppermute | solution.py:201
  29.3 4.7 %collective-permute-start.6 = (bf16[16,3072]{1,0:T(8,128)(2,1)S(1)}, bf16[16,3072]{1,0:T(8,128)(2,1)S(1)}, u32[]{:S(2)}, u32[]{:S(2)}) collective-permute-start(bf16[16,3072]{1,0:T(8,128)(2,1)S(1)} %get-tuple-element.31), channel_id=1, source_target_pairs={{0,8},{4,12},{8,0},{12,4},{1,9},{5,13},{9,1},{13,5},{2,10},{6,14},... | collective-permute-start | bytes 294920 | tf_op jit(solution)/shard_map/ppermute | solution.py:201
  29.8 4.1 %collective-permute-start.8 = (bf16[4,3072]{1,0:T(4,128)(2,1)S(1)}, bf16[4,3072]{1,0:T(4,128)(2,1)S(1)}, u32[]{:S(2)}, u32[]{:S(2)}) collective-permute-start(bf16[4,3072]{1,0:T(4,128)(2,1)S(1)} %get-tuple-element.33), channel_id=1, source_target_pairs={{0,1},{1,0},{2,3},{3,2},{4,5},{5,4},{6,7},{7,6},{8,9},{9,8},{10,11... | collective-permute-start | bytes 73736 | tf_op jit(solution)/shard_map/ppermute | solution.py:201
  32.1 1.9 %copy-start.7 = (s32[256]{0:T(256)S(1)}, s32[256]{0:T(256)}, u32[]{:S(2)}) copy-start(s32[256]{0:T(256)} %param.11) | copy-start | bytes 3076
  32.1 1.9 %copy-start.9 = (s32[256]{0:T(256)S(1)}, s32[256]{0:T(256)}, u32[]{:S(2)}) copy-start(s32[256]{0:T(256)} %param.12) | copy-start | bytes 3076

commit v2 on v1

v2 whole, which is shorter than its diff:
```python
import functools
import math

import jax
import jax.numpy as jnp
from jax import lax
from jax.experimental import pallas as pl
from jax.experimental.pallas import tpu as pltpu
from jax.sharding import PartitionSpec as P

HD = 128
WIN = 64
WIN_FRAME = 4
KF = 16
KT = 4
PAIR = 2 * WIN
SPAN = WIN_FRAME * WIN
ROWS = KF + 8
CHUNK = 512

MASK_FILL = -1e30
FACTOR = HD ** (-0.5)
SCALE = FACTOR * math.log2(math.e)
LIMIT = 16 * 1024 * 1024
LOAD_LIMIT = 55000 * 1024
JOIN_FLOPS = 10**9

VMEM = pl.BlockSpec(memory_space=pltpu.VMEM)
HBM = pl.BlockSpec(memory_space=pltpu.HBM)
ANY = pl.BlockSpec(memory_space=pl.ANY)

NT = ((1,), (1,))
NN = ((1,), (0,))
TN = ((0,), (0,))


def dot(a, b, dims):
    return lax.dot_general(a, b, (dims, ((), ())), preferred_element_type=jnp.float32)


def call(kernel, outs, ins, flops, moved, scratch=(), out_specs=None, limit=LIMIT):
    return pl.pallas_call(
        kernel,
        out_shape=outs,
        in_specs=[spec for _, spec in ins],
        out_specs=out_specs or [VMEM] * len(outs),
        scratch_shapes=list(scratch),
        compiler_params=pltpu.CompilerParams(vmem_limit_bytes=limit),
        cost_estimate=pl.CostEstimate(
            flops=flops, bytes_accessed=moved, transcendentals=0
        ),
    )(*[array for array, _ in ins])


def load_kernel(
    code_ref, k_hbm, v_hbm, t_ref, f_ref, member_ref, valid_ref, k_ref, v_ref, sems
):
    copies = [
        pltpu.make_async_copy(k_hbm, k_ref, sems.at[0]),
        pltpu.make_async_copy(v_hbm, v_ref, sems.at[1]),
    ]
    for copy in copies:
        copy.start()
    length, features = k_ref.shape
    code = code_ref[...]
    label = lax.broadcasted_iota(jnp.int32, (ROWS, length), 0)
    ids = jnp.where(label < KF, code // KT, code % KT + KF)
    member = jnp.where((ids == label) & (code >= 0), 1.0, 0.0)
    member_ref[...] = member
    count = jnp.sum(member[:KF], axis=0, keepdims=True)
    count = jnp.sum(count, axis=1, keepdims=True) * (SPAN / length)
    valid_ref[...] = jnp.broadcast_to(count, valid_ref.shape)
    share = 1.0 / jnp.maximum(jnp.sum(member, axis=1, keepdims=True), 1.0)
    table = member.astype(jnp.bfloat16)
    for copy, ref, at in ((copies[0], k_ref, 0), (copies[1], v_ref, features)):
        copy.wait()
        pooled = dot(table, ref[...], NN) * share
        f_ref[:, at : at + features] = pooled[:KF].astype(jnp.bfloat16)
        t_ref[:, at : at + features] = pooled[KF : KF + KT].astype(jnp.bfloat16)


def join_kernel(a_ref, b_ref, out_ref):
    parts = [a_ref[...].astype(jnp.float32), b_ref[...].astype(jnp.float32)]
    out_ref[...] = jnp.concatenate(parts, axis=0).astype(jnp.bfloat16)


def window_kernel(
    valid_ref,
    q_ref,
    raw_ref,
    k_ref,
    v_ref,
    after_ref,
    g_ref,
    e_ref,
    d_ref,
    top_ref,
    sum_ref,
    dot_ref,
):
    del after_ref
    length, features = q_ref.shape
    valid = valid_ref[:1].astype(jnp.int32)
    live = lax.broadcasted_iota(jnp.int32, (length, HD), 0) % SPAN < valid
    lane = lax.broadcasted_iota(jnp.int32, (WIN, PAIR), 1)
    row = lax.broadcasted_iota(jnp.int32, (WIN, PAIR), 0)
    first = lane < WIN
    place = row + jnp.where(first, 0, WIN)
    for h in range(features // HD):
        at = slice(h * HD, (h + 1) * HD)
        g = jnp.where(live, raw_ref[:, at], 0)
        g_ref[:, at] = g
        for p in range(length // PAIR):
            rows = slice(p * PAIR, (p + 1) * PAIR)
            s = dot(k_ref[rows, at], q_ref[rows, at], NT)
            d = dot(v_ref[rows, at], g[rows], NT)
            s = jnp.where(first, s[:WIN], s[WIN:])
            s = jnp.where((place + p * PAIR) % SPAN < valid, s, MASK_FILL)
            d = jnp.where(first, d[:WIN], d[WIN:])
            top = jnp.max(s, axis=0, keepdims=True)
            e = jnp.exp2((s - top) * SCALE)
            e_ref[h, :, rows] = e
            d_ref[h, :, rows] = d
            top_ref[h : h + 1, rows] = top
            sum_ref[h : h + 1, rows] = jnp.sum(e, axis=0, keepdims=True)
            dot_ref[h : h + 1, rows] = jnp.sum(e * d, axis=0, keepdims=True)


def coarse_rows(refs, at):
    parts = [r[:, at : at + HD].astype(jnp.float32) for r in refs]
    return jnp.concatenate(parts, axis=0).astype(jnp.bfloat16)


def coarse_kernel(parts, q_ref, g_ref, top_ref, sum_ref, dot_ref, *refs):
    coarse = refs[:parts]
    ds_ref, weight_ref, delta_ref = refs[parts : parts + 3]
    term_refs = refs[parts + 3 :]
    features = q_ref.shape[1]
    for h in range(features // HD):
        at = h * HD
        row = slice(h, h + 1)
        q = q_ref[:, at : at + HD]
        g = g_ref[:, at : at + HD]
        s = dot(coarse_rows(coarse, at), q, NT)
        d = dot(coarse_rows(coarse, features + at), g, NT)
        window_top = top_ref[row]
        top = jnp.maximum(window_top, jnp.max(s, axis=0, keepdims=True))
        shrink = jnp.exp2((window_top - top) * SCALE)
        e = jnp.exp2((s - top) * SCALE)
        inv = 1.0 / (sum_ref[row] * shrink + jnp.sum(e, axis=0, keepdims=True))
        delta = (dot_ref[row] * shrink + jnp.sum(e * d, axis=0, keepdims=True)) * inv
        weight_ref[row] = shrink * inv
        delta_ref[row] = delta
        w = e * inv
        ds = ((FACTOR * w) * (d - delta)).astype(jnp.bfloat16)
        ds_ref[h] = ds
        for term, start in (
            (dot(ds, q, NN), at),
            (dot(w.astype(jnp.bfloat16), g, NN), features + at),
        ):
            begin = 0
            for ref in term_refs:
                end = begin + ref.shape[0]
                ref[:, start : start + HD] = term[begin:end].astype(jnp.bfloat16)
                begin = end


def local_kernel(
    q_ref, g_ref, e_ref, d_ref, weight_ref, delta_ref, ds_ref, dk_ref, dv_ref
):
    length, features = q_ref.shape
    first = lax.broadcasted_iota(jnp.int32, (WIN, PAIR), 1) < WIN

    def split(x):
        return jnp.concatenate(
            [jnp.where(first, x, 0.0), jnp.where(first, 0.0, x)], axis=0
        ).astype(jnp.bfloat16)

    for h in range(features // HD):
        at = slice(h * HD, (h + 1) * HD)
        for p in range(length // PAIR):
            rows = slice(p * PAIR, (p + 1) * PAIR)
            w = e_ref[h, :, rows] * weight_ref[h : h + 1, rows]
            ds = (FACTOR * w) * (d_ref[h, :, rows] - delta_ref[h : h + 1, rows])
            ds = split(ds)
            ds_ref[h, :, rows] = ds
            dk_ref[rows, at] = dot(ds, q_ref[rows, at], NN)
            dv_ref[rows, at] = dot(split(w), g_ref[rows, at], NN)


def query_kernel(parts, k_ref, ds_ref, dsc_ref, *refs):
    coarse = refs[:parts]
    dq_ref = refs[parts]
    length, features = k_ref.shape
    for h in range(features // HD):
        at = h * HD
        kc = coarse_rows(coarse, at)
        for p in range(length // PAIR):
            rows = slice(p * PAIR, (p + 1) * PAIR)
            keys = jnp.concatenate([k_ref[rows, at : at + HD], kc], axis=0)
            ds = jnp.concatenate([ds_ref[h, :, rows], dsc_ref[h, :, rows]], axis=0)
            dq_ref[rows, at : at + HD] = dot(ds, keys, TN).astype(jnp.bfloat16)


def spread_kernel(
    member_ref,
    dk_ref,
    dv_ref,
    f1_ref,
    f2_ref,
    t1_ref,
    t2_ref,
    kg_hbm,
    vg_hbm,
    kg_ref,
    vg_ref,
    sems,
):
    features = dk_ref.shape[1]
    member = member_ref[...]
    share = 1.0 / jnp.maximum(jnp.sum(member, axis=1, keepdims=True), 1.0)
    both = jnp.concatenate([member, member], axis=0).astype(jnp.bfloat16)
    pad = jnp.zeros((ROWS - KF - KT, CHUNK), jnp.float32)
    copies = []
    for grad, ref, target, begin in (
        (dk_ref, kg_ref, kg_hbm, 0),
        (dv_ref, vg_ref, vg_hbm, features),
    ):
        for start in range(0, features, CHUNK):
            part = slice(begin + start, begin + start + CHUNK)
            here = slice(start, start + CHUNK)
            f = f1_ref[:, part].astype(jnp.float32) + f2_ref[:, part].astype(
                jnp.float32
            )
            t = t1_ref[:, part].astype(jnp.float32) + t2_ref[:, part].astype(
                jnp.float32
            )
            grads = jnp.concatenate([f, t, pad], axis=0) * share
            high = grads.astype(jnp.bfloat16).astype(jnp.float32)
            terms = jnp.concatenate([high, grads - high], axis=0)
            back = dot(both, terms.astype(jnp.bfloat16), TN)
            ref[:, here] = (grad[:, here] + back).astype(jnp.bfloat16)
            copy = pltpu.make_async_copy(
                ref.at[:, here], target.at[:, here], sems.at[len(copies)]
            )
            copy.start()
            copies.append(copy)
    for copy in copies:
        copy.wait()


def swap(x, axis, size, mask):
    return lax.ppermute(x, axis, [(i, i ^ mask) for i in range(size)])


def add(a, b):
    return (a.astype(jnp.float32) + b.astype(jnp.float32)).astype(jnp.bfloat16)


def body(tm, space, query, key_in, value_in, grad_out, frame_ids, time_ids, tile_valid):
    length, features = query.shape
    heads = features // HD
    live = lax.iota(jnp.int32, length) % SPAN < tile_valid.reshape(())
    code = jnp.where(live, frame_ids * KT + time_ids, -1).reshape(1, length)
    bf16, f32 = jnp.bfloat16, jnp.float32
    shape = jax.ShapeDtypeStruct
    size = length * features
    block = shape((length, features), bf16)
    sums = shape((length, features), f32)
    stat = shape((heads, length), f32)

    own_t, own_f, member, valid = call(
        load_kernel,
        [
            shape((KT, 2 * features), bf16),
            shape((KF, 2 * features), bf16),
            shape((ROWS, length), f32),
            shape((8, PAIR), f32),
        ],
        [(code, VMEM), (key_in, HBM), (value_in, HBM)],
        4 * size * ROWS,
        4 * size,
        [
            pltpu.VMEM((length, features), bf16),
            pltpu.VMEM((length, features), bf16),
            pltpu.SemaphoreType.DMA((2,)),
        ],
        limit=LOAD_LIMIT,
    )
    masks = [space >> (i + 1) for i in range(space.bit_length() - 1)]
    have_t = own_t
    for mask in masks[:-1]:
        (have_t,) = call(
            join_kernel,
            [shape((2 * have_t.shape[0], 2 * features), bf16)],
            [(have_t, VMEM), (swap(have_t, "space", space, mask), VMEM)],
            JOIN_FLOPS,
            0,
        )
    got_t = swap(have_t, "space", space, masks[-1])
    from_2 = swap(own_f, "tm", tm, 2)
    from_1 = swap(own_f, "tm", tm, 1)
    from_3 = swap(from_2, "tm", tm, 1)
    coarse = [own_f, from_2, from_1, from_3, jnp.concatenate([have_t, got_t], axis=0)]
    total = tm * KF + space * KT
    coarse_in = [(x, VMEM) for x in coarse]

    g, e, d, top, window_sum, window_dot = call(
        window_kernel,
        [
            block,
            shape((heads, WIN, length), f32),
            shape((heads, WIN, length), f32),
            stat,
            stat,
            stat,
        ],
        [
            (valid, VMEM),
            (query, VMEM),
            (grad_out, VMEM),
            (key_in, VMEM),
            (value_in, VMEM),
            (have_t, ANY),
        ],
        4 * size * PAIR,
        16 * size,
    )

    half = shape((space * KT // 2, 2 * features), bf16)
    pair = shape((2 * KF, 2 * features), bf16)
    dsc, weight, delta, f_keep, f_send, t_keep, t_send = call(
        functools.partial(coarse_kernel, len(coarse)),
        [shape((heads, total, length), bf16), stat, stat, pair, pair, half, half],
        [(x, VMEM) for x in (query, g, top, window_sum, window_dot)] + coarse_in,
        8 * size * total,
        8 * size,
    )

    for mask in masks[:0:-1]:
        summed = add(t_keep, swap(t_send, "space", space, mask))
        t_keep, t_send = jnp.split(summed, 2)
    got_t = swap(t_send, "space", space, masks[0])
    summed = add(f_keep, swap(f_send, "tm", tm, 1))
    f_keep, f_send = summed[:KF], summed[KF:]
    got_f = swap(f_send, "tm", tm, 2)

    ds, dk, dv = call(
        local_kernel,
        [shape((heads, PAIR, length), bf16), sums, sums],
        [(x, VMEM) for x in (query, g, e, d, weight, delta)],
        4 * size * PAIR,
        16 * size,
    )
    (query_grad,) = call(
        functools.partial(query_kernel, len(coarse)),
        [block],
        [(x, VMEM) for x in (key_in, ds, dsc)] + coarse_in,
        2 * size * (PAIR + total),
        6 * size,
    )
    chunks = 2 * features // CHUNK
    key_grad, value_grad = call(
        spread_kernel,
        [block, block],
        [(x, VMEM) for x in (member, dk, dv, f_keep, got_f, t_keep, got_t)],
        8 * size * ROWS,
        12 * size,
        [
            pltpu.VMEM((length, features), bf16),
            pltpu.VMEM((length, features), bf16),
            pltpu.SemaphoreType.DMA((chunks,)),
        ],
        [HBM, HBM],
    )
    return query_grad, key_grad, value_grad


def solution(mesh):
    tm, space = mesh.shape["tm"], mesh.shape["space"]
    rows = P(("groups", "tm", "space"), None)
    ids = P(("groups", "tm", "space"))
    return jax.shard_map(
        functools.partial(body, tm, space),
        mesh=mesh,
        in_specs=(rows, rows, rows, rows, ids, ids, P(("groups", "tm"), "space")),
        out_specs=(rows, rows, rows),
        check_vma=False,
    )
```

time: 35.9 us -> 29.8 us (0.83)
  local copies, waits for them, and re-layouts: 5.93 us -> 0.05 us
  waiting for transfers between devices: 7.77 us -> 3.88 us
  starting transfers between devices: 12.3 us -> 14 us
  Pallas kernels: 8.08 us -> 9.52 us
  other arithmetic: 0.09 us -> 0.77 us
    unnamed x20 -> x8, local copies, waits for them, and re-layouts: 5.89 us -> 0.01 us
    ppermute x9, waiting for transfers between devices: 7.77 us -> 3.88 us  [swap(): return lax.ppermute(x, axis, [(i, i ^ mask) for i in range(size)])]
    ppermute x9, starting transfers between devices: 12.3 us -> 14 us  [swap(): return lax.ppermute(x, axis, [(i, i ^ mask) for i in range(size)])]
    pallas_call x4 -> x7, Pallas kernels: 8.08 us -> 9.52 us  [call(): pl.pallas_call(kernel, out_shape=outs, in_specs=[spec for _, spec in ins]...]
    select_n x0 -> x1, other arithmetic: none -> 0.7 us  [body(): code = jnp.where(live, frame_ids * KT + time_ids, -1).reshape(1, length)]
  transfers between devices with their start and end apart: 9 -> 9, of which waited for: 4 -> 4; matrix products, arithmetic and copies ran while one was open for 0% -> 0% of each run, Pallas kernels for 5% -> 11%
where the time goes in v2:
time: 29.8 us; the launch traced here: 29.6 us
  starting transfers between devices  14 us (47%)
  Pallas kernels  9.52 us (32%)
  waiting for transfers between devices  3.88 us (13%)
  between operations  1.38 us (5%)
  other arithmetic  0.77 us (3%)
    ppermute x9, starting transfers between devices, swap(): return lax.ppermute(x, axis, [(i, i ^ mask) for i in range(size)])  14 us
    pallas_call x7, Pallas kernels, call(): pl.pallas_call(kernel, out_shape=outs, in_specs=[spec for _, spec in ins]...  9.52 us
    ppermute x9, waiting for transfers between devices, swap(): return lax.ppermute(x, axis, [(i, i ^ mask) for i in range(size)])  3.88 us
    select_n x1, other arithmetic, body(): code = jnp.where(live, frame_ids * KT + time_ids, -1).reshape(1, length)  0.7 us
  transfers between devices with their start and end apart: 9, of which 4 were waited for; matrix products, arithmetic and copies ran while one was open for 0% of the time, Pallas kernels for 11%

profile of v2, /device:TPU:0, one launch (start us, length us, event | category | flops | bytes accessed | tf_op | source)
XLA Modules:
  0.0 29.6 jit_solution(6430669126827035602)
XLA Ops:
  1.3 0.7 %compare_select_fusion = s32[256]{0:T(256)S(1)} fusion(s32[256]{0:T(256)} %param.12, s32[256]{0:T(256)} %param.11, s32[]{:T(128)} %bitcast.2), kind=kLoop, calls=%fused_computation.3 | loop fusion | flops 2560 | bytes 3076 | tf_op jit(solution)/shard_map/jit(_where)/select_n | solution.py:264
  2.0 1.7 %shard_map.94 = (bf16[4,3072]{1,0:T(4,128)(2,1)S(1)}, bf16[16,3072]{1,0:T(8,128)(2,1)S(1)}, f32[24,256]{1,0:T(8,128)S(1)}, f32[8,128]{1,0:T(8,128)S(1)}) custom-call(s32[1,256]{1,0:T(1,128)S(1)} %bitcast.3, bf16[256,1536]{1,0:T(8,128)(2,1)} %k_ref.3, bf16[256,1536]{1,0:T(8,128)(2,1)} %v_ref.1), custom_call_target="tpu_custom_call" | custom-call | flops 37748736 | bytes 1572864 | tf_op jit(solution)/shard_map/pallas_call | solution.py:42
  3.6 4.1 %collective-permute-start = (bf16[4,3072]{1,0:T(4,128)(2,1)S(1)}, bf16[4,3072]{1,0:T(4,128)(2,1)S(1)}, u32[]{:S(2)}, u32[]{:S(2)}) collective-permute-start(bf16[4,3072]{1,0:T(4,128)(2,1)S(1)} %get-tuple-element.26.a_ref), channel_id=1, source_target_pairs={{0,2},{1,3},{2,0},{3,1},{4,6},{5,7},{6,4},{7,5},{8,10},{9,11},{10,... | collective-permute-start | bytes 73736 | tf_op jit(solution)/shard_map/ppermute | solution.py:253
  7.7 0.0 copy-start
  7.7 0.0 copy-start.1
  7.8 0.0 copy-start.2
  7.8 0.0 copy-start.3
  7.8 1.6 %collective-permute-start.1 = (bf16[16,3072]{1,0:T(8,128)(2,1)S(1)}, bf16[16,3072]{1,0:T(8,128)(2,1)S(1)}, u32[]{:S(2)}, u32[]{:S(2)}) collective-permute-start(bf16[16,3072]{1,0:T(8,128)(2,1)S(1)} %get-tuple-element.33.refs_0_), channel_id=1, source_target_pairs={{0,8},{4,12},{8,0},{12,4},{1,9},{5,13},{9,1},{13,5},{2,10},{6,14},... | collective-permute-start | bytes 294920 | tf_op jit(solution)/shard_map/ppermute | solution.py:253
  9.3 0.2 collective-permute-done.b_ref
  9.6 2.0 %collective-permute-start.4 = (bf16[8,3072]{1,0:T(8,128)(2,1)S(1)}, bf16[8,3072]{1,0:T(8,128)(2,1)S(1)}, u32[]{:S(2)}, u32[]{:S(2)}) collective-permute-start(bf16[8,3072]{1,0:T(8,128)(2,1)S(1)} %shard_map.95.after_ref), channel_id=1, source_target_pairs={{0,1},{1,0},{2,3},{3,2},{4,5},{5,4},{6,7},{7,6},{8,9},{9,8},{10,11... | collective-permute-start | bytes 147464 | tf_op jit(solution)/shard_map/ppermute | solution.py:253
  11.5 0.0 collective-permute-start.2
  11.5 0.0 copy-done
  11.5 0.0 copy-done.1
  11.6 0.0 copy-done.2
  11.6 0.0 copy-done.3
  11.6 1.2 %shard_map.96 = (bf16[256,1536]{1,0:T(8,128)(2,1)S(1)}, f32[12,64,256]{2,1,0:T(8,128)S(1)}, f32[12,64,256]{2,1,0:T(8,128)S(1)}, f32[12,256]{1,0:T(8,128)S(1)}, f...) custom-call(f32[8,128]{1,0:T(8,128)S(1)} %get-tuple-element.25.valid_ref, bf16[256,1536]{1,0:T(8,128)(2,1)S(1)} %copy-done, ...), custom_call_target="tpu_custom_call" | custom-call | flops 201326592 | bytes 6291456 | tf_op jit(solution)/shard_map/pallas_call | solution.py:42
  12.8 0.0 collective-permute-done.1.refs_1_
  12.8 0.6 %collective-permute-start.3 = (bf16[16,3072]{1,0:T(8,128)(2,1)S(1)}, bf16[16,3072]{1,0:T(8,128)(2,1)S(1)}, u32[]{:S(2)}, u32[]{:S(2)}) collective-permute-start(bf16[16,3072]{1,0:T(8,128)(2,1)S(1)} %collective-permute-done.1.refs_1_), channel_id=1, source_target_pairs={{0,4},{4,0},{8,12},{12,8},{1,5},{5,1},{9,13},{13,9},{2,6},{6,2},{1... | collective-permute-start | bytes 294920 | tf_op jit(solution)/shard_map/ppermute | solution.py:253
  13.3 0.4 %collective-permute-done.4 = bf16[8,3072]{1,0:T(8,128)(2,1)S(1)} collective-permute-done((bf16[8,3072]{1,0:T(8,128)(2,1)S(1)}, bf16[8,3072]{1,0:T(8,128)(2,1)S(1)}, u32[]{:S(2)}, u32[]{:S(2)}) %collective-permute-start.4) | collective-permute-done | bytes 49184 | tf_op jit(solution)/shard_map/ppermute | solution.py:253
  13.7 0.0 collective-permute-done.2.refs_2_
  13.8 0.5 %collective-permute-done.3.refs_3_ = bf16[16,3072]{1,0:T(8,128)(2,1)S(1)} collective-permute-done((bf16[16,3072]{1,0:T(8,128)(2,1)S(1)}, bf16[16,3072]{1,0:T(8,128)(2,1)S(1)}, u32[]{:S(2)}, u32[]{:S(2)}) %collective-permute-start.3) | collective-permute-done | bytes 98336 | tf_op jit(solution)/shard_map/ppermute | solution.py:253
  14.3 3.0 %shard_map.97 = (bf16[12,80,256]{2,1,0:T(8,128)(2,1)S(1)}, f32[12,256]{1,0:T(8,128)S(1)}, f32[12,256]{1,0:T(8,128)S(1)}, bf16[32,3072]{1,0:T(8,128)(2,1)S(1)}, b...) custom-call(bf16[256,1536]{1,0:T(8,128)(2,1)S(1)} %copy-done, ...), custom_call_target="tpu_custom_call" | custom-call | flops 251658240 | bytes 3145728 | tf_op jit(solution)/shard_map/pallas_call | solution.py:42
  17.3 1.5 %collective-permute-start.7 = (bf16[8,3072]{1,0:T(8,128)(2,1)S(1)}, bf16[8,3072]{1,0:T(8,128)(2,1)S(1)}, u32[]{:S(2)}, u32[]{:S(2)}) collective-permute-start(bf16[8,3072]{1,0:T(8,128)(2,1)S(1)} %get-tuple-element.44), channel_id=1, source_target_pairs={{0,1},{1,0},{2,3},{3,2},{4,5},{5,4},{6,7},{7,6},{8,9},{9,8},{10,11... | collective-permute-start | bytes 147464 | tf_op jit(solution)/shard_map/ppermute | solution.py:253
  18.7 0.0 collective-permute-start.5
  18.8 2.7 %collective-permute-done.7 = bf16[8,3072]{1,0:T(8,128)(2,1)S(1)} collective-permute-done((bf16[8,3072]{1,0:T(8,128)(2,1)S(1)}, bf16[8,3072]{1,0:T(8,128)(2,1)S(1)}, u32[]{:S(2)}, u32[]{:S(2)}) %collective-permute-start.7) | collective-permute-done | bytes 49184 | tf_op jit(solution)/shard_map/ppermute | solution.py:253
  21.5 0.0 collective-permute-done.5
  21.6 1.6 %collective-permute-start.6 = (bf16[16,3072]{1,0:T(8,128)(2,1)S(1)}, bf16[16,3072]{1,0:T(8,128)(2,1)S(1)}, u32[]{:S(2)}, u32[]{:S(2)}) collective-permute-start(bf16[16,3072]{1,0:T(8,128)(2,1)S(1)} %get-tuple-element.47), channel_id=1, source_target_pairs={{0,8},{4,12},{8,0},{12,4},{1,9},{5,13},{9,1},{13,5},{2,10},{6,14},... | collective-permute-start | bytes 294920 | tf_op jit(solution)/shard_map/ppermute | solution.py:253
  23.1 2.8 %collective-permute-start.8 = (bf16[4,3072]{1,0:T(4,128)(2,1)S(1)}, bf16[4,3072]{1,0:T(4,128)(2,1)S(1)}, u32[]{:S(2)}, u32[]{:S(2)}) collective-permute-start(bf16[4,3072]{1,0:T(4,128)(2,1)S(1)} %get-tuple-element.49), channel_id=1, source_target_pairs={{0,2},{1,3},{2,0},{3,1},{4,6},{5,7},{6,4},{7,5},{8,10},{9,11},{10,... | collective-permute-start | bytes 73736 | tf_op jit(solution)/shard_map/ppermute | solution.py:253
  25.9 0.7 %shard_map.98 = (bf16[12,128,256]{2,1,0:T(8,128)(2,1)S(1)}, f32[256,1536]{1,0:T(8,128)S(1)}, f32[256,1536]{1,0:T(8,128)S(1)}) custom-call(bf16[256,1536]{1,0:T(8,128)(2,1)S(1)} %copy-done, bf16[256,1536]{1,0:T(8,128)(2,1)S(1)} %get-tuple-element.27.g_ref, f32[12,64,256]{2,1,0:T(8,128)S(1)} %get-tuple-element.28.e_ref, ...), custom_call_target="tpu_custom_call" | custom-call | flops 201326592 | bytes 6291456 | tf_op jit(solution)/shard_map/pallas_call | solution.py:42
  26.6 1.5 %shard_map.99 = bf16[256,1536]{1,0:T(8,128)(2,1)} custom-call(bf16[256,1536]{1,0:T(8,128)(2,1)S(1)} %copy-done.1, bf16[12,128,256]{2,1,0:T(8,128)(2,1)S(1)} %get-tuple-element.36.ds_ref, bf16[12,80,256]{2,1,0:T(8,128)(2,1)S(1)} %get-tuple-element.37.dsc_ref, bf16[16,3072]{1,0:T(8,128)(2,1)S(1)} %get-tuple-element.33.refs_0_, ...), custom_call_target="tpu_custom_call" | custom-call | flops 163577856 | bytes 2359296 | tf_op jit(solution)/shard_map/pallas_call | solution.py:42
  28.1 0.0 collective-permute-done.8.t2_ref
  28.1 0.0 collective-permute-done.6.f2_ref
  28.1 1.5 %shard_map.100 = (bf16[256,1536]{1,0:T(8,128)(2,1)}, bf16[256,1536]{1,0:T(8,128)(2,1)}) custom-call(f32[24,256]{1,0:T(8,128)S(1)} %get-tuple-element.38.member_ref, f32[256,1536]{1,0:T(8,128)S(1)} %get-tuple-element.39.dk_ref, f32[256,1536]{1,0:T(8,128)S(1)} %get-tuple-element.40.dv_ref, bf16[16,3072]{1,0:T(8,128)(2,1)S(1)} %get-tuple-element.48.f1_ref, ...), custom_call_target="tpu_custom_call" | custom-call | flops 75497472 | bytes 4718592 | tf_op jit(solution)/shard_map/pallas_call | solution.py:42
  (6 shorter events, 0.1 us)
Async XLA Ops:
  3.6 5.9 %collective-permute-start = (bf16[4,3072]{1,0:T(4,128)(2,1)S(1)}, bf16[4,3072]{1,0:T(4,128)(2,1)S(1)}, u32[]{:S(2)}, u32[]{:S(2)}) collective-permute-start(bf16[4,3072]{1,0:T(4,128)(2,1)S(1)} %get-tuple-element.26.a_ref), channel_id=1, source_target_pairs={{0,2},{1,3},{2,0},{3,1},{4,6},{5,7},{6,4},{7,5},{8,10},{9,11},{10,... | collective-permute-start | bytes 73736 | tf_op jit(solution)/shard_map/ppermute | solution.py:253
  7.7 3.8 %copy-start = (bf16[256,1536]{1,0:T(8,128)(2,1)S(1)}, bf16[256,1536]{1,0:T(8,128)(2,1)}, u32[]{:S(2)}) copy-start(bf16[256,1536]{1,0:T(8,128)(2,1)} %q_ref.5) | copy-start | bytes 2359300
  7.7 3.8 %copy-start.1 = (bf16[256,1536]{1,0:T(8,128)(2,1)S(1)}, bf16[256,1536]{1,0:T(8,128)(2,1)}, u32[]{:S(2)}) copy-start(bf16[256,1536]{1,0:T(8,128)(2,1)} %k_ref.3) | copy-start | bytes 2359300
  7.8 3.8 %copy-start.2 = (bf16[256,1536]{1,0:T(8,128)(2,1)S(1)}, bf16[256,1536]{1,0:T(8,128)(2,1)}, u32[]{:S(2)}) copy-start(bf16[256,1536]{1,0:T(8,128)(2,1)} %v_ref.1) | copy-start | bytes 2359300
  7.8 3.8 %copy-start.3 = (bf16[256,1536]{1,0:T(8,128)(2,1)S(1)}, bf16[256,1536]{1,0:T(8,128)(2,1)}, u32[]{:S(2)}) copy-start(bf16[256,1536]{1,0:T(8,128)(2,1)} %raw_ref.1) | copy-start | bytes 2359300
  7.8 5.0 %collective-permute-start.1 = (bf16[16,3072]{1,0:T(8,128)(2,1)S(1)}, bf16[16,3072]{1,0:T(8,128)(2,1)S(1)}, u32[]{:S(2)}, u32[]{:S(2)}) collective-permute-start(bf16[16,3072]{1,0:T(8,128)(2,1)S(1)} %get-tuple-element.33.refs_0_), channel_id=1, source_target_pairs={{0,8},{4,12},{8,0},{12,4},{1,9},{5,13},{9,1},{13,5},{2,10},{6,14},... | collective-permute-start | bytes 294920 | tf_op jit(solution)/shard_map/ppermute | solution.py:253
  9.6 4.2 %collective-permute-start.4 = (bf16[8,3072]{1,0:T(8,128)(2,1)S(1)}, bf16[8,3072]{1,0:T(8,128)(2,1)S(1)}, u32[]{:S(2)}, u32[]{:S(2)}) collective-permute-start(bf16[8,3072]{1,0:T(8,128)(2,1)S(1)} %shard_map.95.after_ref), channel_id=1, source_target_pairs={{0,1},{1,0},{2,3},{3,2},{4,5},{5,4},{6,7},{7,6},{8,9},{9,8},{10,11... | collective-permute-start | bytes 147464 | tf_op jit(solution)/shard_map/ppermute | solution.py:253
  11.5 2.2 %collective-permute-start.2 = (bf16[16,3072]{1,0:T(8,128)(2,1)S(1)}, bf16[16,3072]{1,0:T(8,128)(2,1)S(1)}, u32[]{:S(2)}, u32[]{:S(2)}) collective-permute-start(bf16[16,3072]{1,0:T(8,128)(2,1)S(1)} %get-tuple-element.33.refs_0_), channel_id=1, source_target_pairs={{0,4},{4,0},{8,12},{12,8},{1,5},{5,1},{9,13},{13,9},{2,6},{6,2},{1... | collective-permute-start | bytes 294920 | tf_op jit(solution)/shard_map/ppermute | solution.py:253
  12.8 1.5 %collective-permute-start.3 = (bf16[16,3072]{1,0:T(8,128)(2,1)S(1)}, bf16[16,3072]{1,0:T(8,128)(2,1)S(1)}, u32[]{:S(2)}, u32[]{:S(2)}) collective-permute-start(bf16[16,3072]{1,0:T(8,128)(2,1)S(1)} %collective-permute-done.1.refs_1_), channel_id=1, source_target_pairs={{0,4},{4,0},{8,12},{12,8},{1,5},{5,1},{9,13},{13,9},{2,6},{6,2},{1... | collective-permute-start | bytes 294920 | tf_op jit(solution)/shard_map/ppermute | solution.py:253
  17.3 4.2 %collective-permute-start.7 = (bf16[8,3072]{1,0:T(8,128)(2,1)S(1)}, bf16[8,3072]{1,0:T(8,128)(2,1)S(1)}, u32[]{:S(2)}, u32[]{:S(2)}) collective-permute-start(bf16[8,3072]{1,0:T(8,128)(2,1)S(1)} %get-tuple-element.44), channel_id=1, source_target_pairs={{0,1},{1,0},{2,3},{3,2},{4,5},{5,4},{6,7},{7,6},{8,9},{9,8},{10,11... | collective-permute-start | bytes 147464 | tf_op jit(solution)/shard_map/ppermute | solution.py:253
  18.7 2.7 %collective-permute-start.5 = (bf16[32,3072]{1,0:T(8,128)(2,1)S(1)}, bf16[32,3072]{1,0:T(8,128)(2,1)S(1)}, u32[]{:S(2)}, u32[]{:S(2)}) collective-permute-start(bf16[32,3072]{1,0:T(8,128)(2,1)S(1)} %get-tuple-element.42), channel_id=1, source_target_pairs={{0,4},{4,0},{8,12},{12,8},{1,5},{5,1},{9,13},{13,9},{2,6},{6,2},{1... | collective-permute-start | bytes 589832 | tf_op jit(solution)/shard_map/ppermute | solution.py:253
  21.6 6.6 %collective-permute-start.6 = (bf16[16,3072]{1,0:T(8,128)(2,1)S(1)}, bf16[16,3072]{1,0:T(8,128)(2,1)S(1)}, u32[]{:S(2)}, u32[]{:S(2)}) collective-permute-start(bf16[16,3072]{1,0:T(8,128)(2,1)S(1)} %get-tuple-element.47), channel_id=1, source_target_pairs={{0,8},{4,12},{8,0},{12,4},{1,9},{5,13},{9,1},{13,5},{2,10},{6,14},... | collective-permute-start | bytes 294920 | tf_op jit(solution)/shard_map/ppermute | solution.py:253
  23.1 5.0 %collective-permute-start.8 = (bf16[4,3072]{1,0:T(4,128)(2,1)S(1)}, bf16[4,3072]{1,0:T(4,128)(2,1)S(1)}, u32[]{:S(2)}, u32[]{:S(2)}) collective-permute-start(bf16[4,3072]{1,0:T(4,128)(2,1)S(1)} %get-tuple-element.49), channel_id=1, source_target_pairs={{0,2},{1,3},{2,0},{3,1},{4,6},{5,7},{6,4},{7,5},{8,10},{9,11},{10,... | collective-permute-start | bytes 73736 | tf_op jit(solution)/shard_map/ppermute | solution.py:253

commit v3 on v2

--- a/solution.py
+++ b/solution.py
@@ -22,7 +22,6 @@
 FACTOR = HD ** (-0.5)
 SCALE = FACTOR * math.log2(math.e)
 LIMIT = 16 * 1024 * 1024
-LOAD_LIMIT = 55000 * 1024
 JOIN_FLOPS = 10**9
 
 VMEM = pl.BlockSpec(memory_space=pltpu.VMEM)
@@ -52,15 +51,11 @@
     )(*[array for array, _ in ins])
 
 
-def load_kernel(
-    code_ref, k_hbm, v_hbm, t_ref, f_ref, member_ref, valid_ref, k_ref, v_ref, sems
-):
-    copies = [
-        pltpu.make_async_copy(k_hbm, k_ref, sems.at[0]),
-        pltpu.make_async_copy(v_hbm, v_ref, sems.at[1]),
-    ]
-    for copy in copies:
-        copy.start()
+def start_kernel(out_ref):
+    out_ref[...] = jnp.zeros_like(out_ref)
+
+
+def pool_kernel(code_ref, k_ref, v_ref, t_ref, f_ref, member_ref, valid_ref):
     length, features = k_ref.shape
     code = code_ref[...]
     label = lax.broadcasted_iota(jnp.int32, (ROWS, length), 0)
@@ -72,8 +67,7 @@
     valid_ref[...] = jnp.broadcast_to(count, valid_ref.shape)
     share = 1.0 / jnp.maximum(jnp.sum(member, axis=1, keepdims=True), 1.0)
     table = member.astype(jnp.bfloat16)
-    for copy, ref, at in ((copies[0], k_ref, 0), (copies[1], v_ref, features)):
-        copy.wait()
+    for ref, at in ((k_ref, 0), (v_ref, features)):
         pooled = dot(table, ref[...], NN) * share
         f_ref[:, at : at + features] = pooled[:KF].astype(jnp.bfloat16)
         t_ref[:, at : at + features] = pooled[KF : KF + KT].astype(jnp.bfloat16)
@@ -84,8 +78,17 @@
     out_ref[...] = jnp.concatenate(parts, axis=0).astype(jnp.bfloat16)
 
 
+def halve_kernel(a_ref, b_ref, *refs):
+    keep_ref, send_ref = refs[-2:]
+    total = a_ref[...].astype(jnp.float32) + b_ref[...].astype(jnp.float32)
+    amount = keep_ref.shape[0]
+    keep_ref[...] = total[:amount].astype(jnp.bfloat16)
+    send_ref[...] = total[amount:].astype(jnp.bfloat16)
+
+
 def window_kernel(
     valid_ref,
+    member_ref,
     q_ref,
     raw_ref,
     k_ref,
@@ -97,9 +100,17 @@
     top_ref,
     sum_ref,
     dot_ref,
+    table_ref,
+    share_ref,
 ):
     del after_ref
     length, features = q_ref.shape
+    member = member_ref[...]
+    share = 1.0 / jnp.maximum(jnp.sum(member, axis=1, keepdims=True), 1.0)
+    share_ref[...] = jnp.broadcast_to(share, share_ref.shape)
+    blank = jnp.zeros((HD - 2 * ROWS, length), jnp.float32)
+    table = jnp.concatenate([member, member, blank], axis=0)
+    table_ref[...] = table.T[:, : 2 * ROWS].astype(jnp.bfloat16)
     valid = valid_ref[:1].astype(jnp.int32)
     live = lax.broadcasted_iota(jnp.int32, (length, HD), 0) % SPAN < valid
     lane = lax.broadcasted_iota(jnp.int32, (WIN, PAIR), 1)
@@ -136,13 +147,18 @@
     ds_ref, weight_ref, delta_ref = refs[parts : parts + 3]
     term_refs = refs[parts + 3 :]
     features = q_ref.shape[1]
-    for h in range(features // HD):
+    heads = features // HD
+
+    def products(h):
         at = h * HD
-        row = slice(h, h + 1)
         q = q_ref[:, at : at + HD]
         g = g_ref[:, at : at + HD]
         s = dot(coarse_rows(coarse, at), q, NT)
         d = dot(coarse_rows(coarse, features + at), g, NT)
+        return q, g, s, d
+
+    def weigh(h, s, d):
+        row = slice(h, h + 1)
         window_top = top_ref[row]
         top = jnp.maximum(window_top, jnp.max(s, axis=0, keepdims=True))
         shrink = jnp.exp2((window_top - top) * SCALE)
@@ -154,15 +170,27 @@
         w = e * inv
         ds = ((FACTOR * w) * (d - delta)).astype(jnp.bfloat16)
         ds_ref[h] = ds
-        for term, start in (
-            (dot(ds, q, NN), at),
-            (dot(w.astype(jnp.bfloat16), g, NN), features + at),
-        ):
+        return ds, w.astype(jnp.bfloat16)
+
+    def gradients(h, ds, w, q, g):
+        at = h * HD
+        for term, start in ((dot(ds, q, NN), at), (dot(w, g, NN), features + at)):
             begin = 0
             for ref in term_refs:
                 end = begin + ref.shape[0]
                 ref[:, start : start + HD] = term[begin:end].astype(jnp.bfloat16)
                 begin = end
+
+    ahead, behind = products(0), None
+    for h in range(heads):
+        q, g, s, d = ahead
+        if h + 1 < heads:
+            ahead = products(h + 1)
+        if behind:
+            gradients(*behind)
+        ds, w = weigh(h, s, d)
+        behind = (h, ds, w, q, g)
+    gradients(*behind)
 
 
 def local_kernel(
@@ -202,66 +230,56 @@
             dq_ref[rows, at : at + HD] = dot(ds, keys, TN).astype(jnp.bfloat16)
 
 
-def spread_kernel(
-    member_ref,
-    dk_ref,
-    dv_ref,
-    f1_ref,
-    f2_ref,
-    t1_ref,
-    t2_ref,
-    kg_hbm,
-    vg_hbm,
-    kg_ref,
-    vg_ref,
-    sems,
-):
+def spread_kernel(f_parts, t_parts, table_ref, share_ref, dk_ref, dv_ref, *refs):
+    f_refs = refs[:f_parts]
+    t_refs = refs[f_parts : f_parts + t_parts]
+    kg_hbm, vg_hbm, kg_ref, vg_ref, sems = refs[f_parts + t_parts :]
     features = dk_ref.shape[1]
-    member = member_ref[...]
-    share = 1.0 / jnp.maximum(jnp.sum(member, axis=1, keepdims=True), 1.0)
-    both = jnp.concatenate([member, member], axis=0).astype(jnp.bfloat16)
+    table = table_ref[...]
+    share = share_ref[:, :1]
     pad = jnp.zeros((ROWS - KF - KT, CHUNK), jnp.float32)
+
+    def back(begin):
+        part = slice(begin, begin + CHUNK)
+        f, t = (
+            functools.reduce(
+                lambda a, b: a + b, [r[:, part].astype(jnp.float32) for r in refs]
+            )
+            for refs in (f_refs, t_refs)
+        )
+        grads = jnp.concatenate([f, t, pad], axis=0) * share
+        high = grads.astype(jnp.bfloat16).astype(jnp.float32)
+        terms = jnp.concatenate([high, grads - high], axis=0)
+        return dot(table, terms.astype(jnp.bfloat16), NN)
+
     copies = []
-    for grad, ref, target, begin in (
-        (dk_ref, kg_ref, kg_hbm, 0),
-        (dv_ref, vg_ref, vg_hbm, features),
-    ):
-        for start in range(0, features, CHUNK):
-            part = slice(begin + start, begin + start + CHUNK)
-            here = slice(start, start + CHUNK)
-            f = f1_ref[:, part].astype(jnp.float32) + f2_ref[:, part].astype(
-                jnp.float32
-            )
-            t = t1_ref[:, part].astype(jnp.float32) + t2_ref[:, part].astype(
-                jnp.float32
-            )
-            grads = jnp.concatenate([f, t, pad], axis=0) * share
-            high = grads.astype(jnp.bfloat16).astype(jnp.float32)
-            terms = jnp.concatenate([high, grads - high], axis=0)
-            back = dot(both, terms.astype(jnp.bfloat16), TN)
-            ref[:, here] = (grad[:, here] + back).astype(jnp.bfloat16)
-            copy = pltpu.make_async_copy(
-                ref.at[:, here], target.at[:, here], sems.at[len(copies)]
-            )
-            copy.start()
-            copies.append(copy)
+    ahead = back(0)
+    for begin in range(0, 2 * features, CHUNK):
+        now = ahead
+        if begin + CHUNK < 2 * features:
+            ahead = back(begin + CHUNK)
+        if begin < features:
+            grad, ref, target = dk_ref, kg_ref, kg_hbm
+        else:
+            grad, ref, target = dv_ref, vg_ref, vg_hbm
+        here = slice(begin % features, begin % features + CHUNK)
+        ref[:, here] = (grad[:, here] + now).astype(jnp.bfloat16)
+        copy = pltpu.make_async_copy(
+            ref.at[:, here], target.at[:, here], sems.at[len(copies)]
+        )
+        copy.start()
+        copies.append(copy)
     for copy in copies:
         copy.wait()
 
 
 def swap(x, axis, size, mask):
     return lax.ppermute(x, axis, [(i, i ^ mask) for i in range(size)])
-
-
-def add(a, b):
-    return (a.astype(jnp.float32) + b.astype(jnp.float32)).astype(jnp.bfloat16)
 
 
 def body(tm, space, query, key_in, value_in, grad_out, frame_ids, time_ids, tile_valid):
     length, features = query.shape
     heads = features // HD
-    live = lax.iota(jnp.int32, length) % SPAN < tile_valid.reshape(())
-    code = jnp.where(live, frame_ids * KT + time_ids, -1).reshape(1, length)
     bf16, f32 = jnp.bfloat16, jnp.float32
     shape = jax.ShapeDtypeStruct
     size = length * features
@@ -269,24 +287,22 @@
     sums = shape((length, features), f32)
     stat = shape((heads, length), f32)
 
+    (zero,) = call(start_kernel, [shape((1, length), jnp.int32)], [], JOIN_FLOPS, 0)
+    live = lax.iota(jnp.int32, length) % SPAN < tile_valid.reshape(())
+    code = jnp.where(live, frame_ids * KT + time_ids, -1).reshape(1, length) + zero
     own_t, own_f, member, valid = call(
-        load_kernel,
+        pool_kernel,
         [
             shape((KT, 2 * features), bf16),
             shape((KF, 2 * features), bf16),
             shape((ROWS, length), f32),
             shape((8, PAIR), f32),
         ],
-        [(code, VMEM), (key_in, HBM), (value_in, HBM)],
+        [(code, VMEM), (key_in, VMEM), (value_in, VMEM)],
         4 * size * ROWS,
         4 * size,
-        [
-            pltpu.VMEM((length, features), bf16),
-            pltpu.VMEM((length, features), bf16),
-            pltpu.SemaphoreType.DMA((2,)),
-        ],
-        limit=LOAD_LIMIT,
-    )
+    )
+
     masks = [space >> (i + 1) for i in range(space.bit_length() - 1)]
     have_t = own_t
     for mask in masks[:-1]:
@@ -305,7 +321,7 @@
     total = tm * KF + space * KT
     coarse_in = [(x, VMEM) for x in coarse]
 
-    g, e, d, top, window_sum, window_dot = call(
+    g, e, d, top, window_sum, window_dot, table, share = call(
         window_kernel,
         [
             block,
@@ -314,9 +330,12 @@
             stat,
             stat,
             stat,
+            shape((length, 2 * ROWS), bf16),
+            shape((ROWS, HD), f32),
         ],
         [
             (valid, VMEM),
+            (member, VMEM),
             (query, VMEM),
             (grad_out, VMEM),
             (key_in, VMEM),
@@ -337,14 +356,6 @@
         8 * size,
     )
 
-    for mask in masks[:0:-1]:
-        summed = add(t_keep, swap(t_send, "space", space, mask))
-        t_keep, t_send = jnp.split(summed, 2)
-    got_t = swap(t_send, "space", space, masks[0])
-    summed = add(f_keep, swap(f_send, "tm", tm, 1))
-    f_keep, f_send = summed[:KF], summed[KF:]
-    got_f = swap(f_send, "tm", tm, 2)
-
     ds, dk, dv = call(
         local_kernel,
         [shape((heads, PAIR, length), bf16), sums, sums],
@@ -352,6 +363,19 @@
         4 * size * PAIR,
         16 * size,
     )
+    def halve(keep, got, flops, after=()):
+        part = shape((keep.shape[0] // 2, 2 * features), bf16)
+        ins = [(keep, VMEM), (got, VMEM)] + [(x, ANY) for x in after]
+        return call(halve_kernel, [part, part], ins, flops, 0)
+
+    for mask in masks[:0:-1]:
+        t_keep, t_send = halve(
+            t_keep, swap(t_send, "space", space, mask), JOIN_FLOPS, [dk]
+        )
+    got_t = swap(t_send, "space", space, masks[0])
+    f_keep, f_send = halve(f_keep, swap(f_send, "tm", tm, 1), 0)
+    got_f = swap(f_send, "tm", tm, 2)
+
     (query_grad,) = call(
         functools.partial(query_kernel, len(coarse)),
         [block],
@@ -361,9 +385,9 @@
     )
     chunks = 2 * features // CHUNK
     key_grad, value_grad = call(
-        spread_kernel,
+        functools.partial(spread_kernel, 2, 2),
         [block, block],
-        [(x, VMEM) for x in (member, dk, dv, f_keep, got_f, t_keep, got_t)],
+        [(x, VMEM) for x in (table, share, dk, dv, f_keep, got_f, t_keep, got_t)],
         8 * size * ROWS,
         12 * size,
         [

time: 29.8 us -> 25.3 us (0.85)
  Pallas kernels: 9.52 us -> 6.65 us
  waiting for transfers between devices: 3.88 us -> 2.41 us
  other arithmetic: 0.77 us -> 0.02 us
  local copies, waits for them, and re-layouts: 0.05 us -> 0.58 us
    pallas_call x7 -> x10, Pallas kernels: 9.52 us -> 6.65 us  [call(): pl.pallas_call(kernel, out_shape=outs, in_specs=[spec for _, spec in ins]...]
    ppermute x9, waiting for transfers between devices: 3.88 us -> 2.41 us  [swap(): return lax.ppermute(x, axis, [(i, i ^ mask) for i in range(size)])]
    select_n x1, other arithmetic: 0.7 us -> 0.01 us  [body(): jnp.where(live, frame_ids * KT + time_ids, -1).reshape(1, length) + zero]
    unnamed x8 -> x12, local copies, waits for them, and re-layouts: 0.01 us -> 0.58 us
  transfers between devices with their start and end apart: 9 -> 9, of which waited for: 4 -> 5; matrix products, arithmetic and copies ran while one was open for 0% -> 0% of each run, Pallas kernels for 11% -> 14%
where the time goes in v3:
time: 25.3 us; the launch traced here: 25.2 us
  starting transfers between devices  14 us (55%)
  Pallas kernels  6.65 us (26%)
  waiting for transfers between devices  2.41 us (10%)
  between operations  1.53 us (6%)
  local copies, waits for them, and re-layouts  0.58 us (2%)
    ppermute x9, starting transfers between devices, swap(): return lax.ppermute(x, axis, [(i, i ^ mask) for i in range(size)])  14 us
    pallas_call x10, Pallas kernels, call(): pl.pallas_call(kernel, out_shape=outs, in_specs=[spec for _, spec in ins]...  6.65 us
    ppermute x9, waiting for transfers between devices, swap(): return lax.ppermute(x, axis, [(i, i ^ mask) for i in range(size)])  2.41 us
    unnamed x12, local copies, waits for them, and re-layouts  0.58 us
  transfers between devices with their start and end apart: 9, of which 5 were waited for; matrix products, arithmetic and copies ran while one was open for 0% of the time, Pallas kernels for 14%

profile of v3, /device:TPU:0, one launch (start us, length us, event | category | flops | bytes accessed | tf_op | source)
XLA Modules:
  0.0 25.2 jit_solution(2710159050591561637)
XLA Ops:
  0.6 0.0 copy-start.4
  0.6 0.0 copy-start.5
  0.7 0.0 copy-start.1
  0.7 0.0 copy-start.2
  1.4 0.0 copy-done.4
  1.5 0.0 copy-done.5
  1.5 0.3 %copy-done.1 = bf16[256,1536]{1,0:T(8,128)(2,1)S(1)} copy-done((bf16[256,1536]{1,0:T(8,128)(2,1)S(1)}, bf16[256,1536]{1,0:T(8,128)(2,1)}, u32[]{:S(2)}) %copy-start.1) | copy-done | bytes 786456
  1.8 0.2 copy-done.2
  2.0 0.4 %shard_map.95 = (bf16[4,3072]{1,0:T(4,128)(2,1)S(1)}, bf16[16,3072]{1,0:T(8,128)(2,1)S(1)}, f32[24,256]{1,0:T(8,128)S(1)}, f32[8,128]{1,0:T(8,128)S(1)}) custom-call(s32[1,256]{1,0:T(1,128)S(1)} %add.14.code_ref, bf16[256,1536]{1,0:T(8,128)(2,1)S(1)} %copy-done.1, bf16[256,1536]{1,0:T(8,128)(2,1)S(1)} %copy-done.2), custom_call_target="tpu_custom_call" | custom-call | flops 37748736 | bytes 1572864 | tf_op jit(solution)/shard_map/pallas_call | solution.py:41
  2.4 4.1 %collective-permute-start = (bf16[4,3072]{1,0:T(4,128)(2,1)S(1)}, bf16[4,3072]{1,0:T(4,128)(2,1)S(1)}, u32[]{:S(2)}, u32[]{:S(2)}) collective-permute-start(bf16[4,3072]{1,0:T(4,128)(2,1)S(1)} %get-tuple-element.33.a_ref), channel_id=1, source_target_pairs={{0,2},{1,3},{2,0},{3,1},{4,6},{5,7},{6,4},{7,5},{8,10},{9,11},{10,... | collective-permute-start | bytes 73736 | tf_op jit(solution)/shard_map/ppermute | solution.py:277
  6.5 0.0 copy-start
  6.5 0.0 copy-start.3
  6.5 1.5 %collective-permute-start.1 = (bf16[16,3072]{1,0:T(8,128)(2,1)S(1)}, bf16[16,3072]{1,0:T(8,128)(2,1)S(1)}, u32[]{:S(2)}, u32[]{:S(2)}) collective-permute-start(bf16[16,3072]{1,0:T(8,128)(2,1)S(1)} %get-tuple-element.40.refs_0_), channel_id=1, source_target_pairs={{0,8},{4,12},{8,0},{12,4},{1,9},{5,13},{9,1},{13,5},{2,10},{6,14},... | collective-permute-start | bytes 294920 | tf_op jit(solution)/shard_map/ppermute | solution.py:277
  8.0 0.3 %collective-permute-done.b_ref = bf16[4,3072]{1,0:T(4,128)(2,1)S(1)} collective-permute-done((bf16[4,3072]{1,0:T(4,128)(2,1)S(1)}, bf16[4,3072]{1,0:T(4,128)(2,1)S(1)}, u32[]{:S(2)}, u32[]{:S(2)}) %collective-permute-start) | collective-permute-done | bytes 24608 | tf_op jit(solution)/shard_map/ppermute | solution.py:277
  8.3 2.0 %collective-permute-start.4 = (bf16[8,3072]{1,0:T(8,128)(2,1)S(1)}, bf16[8,3072]{1,0:T(8,128)(2,1)S(1)}, u32[]{:S(2)}, u32[]{:S(2)}) collective-permute-start(bf16[8,3072]{1,0:T(8,128)(2,1)S(1)} %shard_map.96.after_ref), channel_id=1, source_target_pairs={{0,1},{1,0},{2,3},{3,2},{4,5},{5,4},{6,7},{7,6},{8,9},{9,8},{10,11... | collective-permute-start | bytes 147464 | tf_op jit(solution)/shard_map/ppermute | solution.py:277
  10.3 0.0 collective-permute-start.2
  10.3 0.0 copy-done
  10.3 0.0 copy-done.3
  10.3 1.2 %shard_map.97 = (bf16[256,1536]{1,0:T(8,128)(2,1)S(1)}, f32[12,64,256]{2,1,0:T(8,128)S(1)}, f32[12,64,256]{2,1,0:T(8,128)S(1)}, f32[12,256]{1,0:T(8,128)S(1)}, f...) custom-call(f32[8,128]{1,0:T(8,128)S(1)} %get-tuple-element.31.valid_ref, ...), custom_call_target="tpu_custom_call" | custom-call | flops 201326592 | bytes 6291456 | tf_op jit(solution)/shard_map/pallas_call | solution.py:41
  11.5 0.0 collective-permute-done.1.refs_1_
  11.5 0.6 %collective-permute-start.3 = (bf16[16,3072]{1,0:T(8,128)(2,1)S(1)}, bf16[16,3072]{1,0:T(8,128)(2,1)S(1)}, u32[]{:S(2)}, u32[]{:S(2)}) collective-permute-start(bf16[16,3072]{1,0:T(8,128)(2,1)S(1)} %collective-permute-done.1.refs_1_), channel_id=1, source_target_pairs={{0,4},{4,0},{8,12},{12,8},{1,5},{5,1},{9,13},{13,9},{2,6},{6,2},{1... | collective-permute-start | bytes 294920 | tf_op jit(solution)/shard_map/ppermute | solution.py:277
  12.1 0.4 %collective-permute-done.4 = bf16[8,3072]{1,0:T(8,128)(2,1)S(1)} collective-permute-done((bf16[8,3072]{1,0:T(8,128)(2,1)S(1)}, bf16[8,3072]{1,0:T(8,128)(2,1)S(1)}, u32[]{:S(2)}, u32[]{:S(2)}) %collective-permute-start.4) | collective-permute-done | bytes 49184 | tf_op jit(solution)/shard_map/ppermute | solution.py:277
  12.5 0.0 collective-permute-done.2.refs_2_
  12.5 0.5 %collective-permute-done.3.refs_3_ = bf16[16,3072]{1,0:T(8,128)(2,1)S(1)} collective-permute-done((bf16[16,3072]{1,0:T(8,128)(2,1)S(1)}, bf16[16,3072]{1,0:T(8,128)(2,1)S(1)}, u32[]{:S(2)}, u32[]{:S(2)}) %collective-permute-start.3) | collective-permute-done | bytes 98336 | tf_op jit(solution)/shard_map/ppermute | solution.py:277
  13.0 1.4 %shard_map.98 = (bf16[12,80,256]{2,1,0:T(8,128)(2,1)S(1)}, f32[12,256]{1,0:T(8,128)S(1)}, f32[12,256]{1,0:T(8,128)S(1)}, bf16[32,3072]{1,0:T(8,128)(2,1)S(1)}, b...) custom-call(bf16[256,1536]{1,0:T(8,128)(2,1)S(1)} %copy-done, ...), custom_call_target="tpu_custom_call" | custom-call | flops 251658240 | bytes 3145728 | tf_op jit(solution)/shard_map/pallas_call | solution.py:41
  14.4 0.4 %collective-permute-start.5 = (bf16[32,3072]{1,0:T(8,128)(2,1)S(1)}, bf16[32,3072]{1,0:T(8,128)(2,1)S(1)}, u32[]{:S(2)}, u32[]{:S(2)}) collective-permute-start(bf16[32,3072]{1,0:T(8,128)(2,1)S(1)} %get-tuple-element.50), channel_id=1, source_target_pairs={{0,4},{4,0},{8,12},{12,8},{1,5},{5,1},{9,13},{13,9},{2,6},{6,2},{1... | collective-permute-start | bytes 589832 | tf_op jit(solution)/shard_map/ppermute | solution.py:277
  14.8 1.1 %collective-permute-start.7 = (bf16[8,3072]{1,0:T(8,128)(2,1)S(1)}, bf16[8,3072]{1,0:T(8,128)(2,1)S(1)}, u32[]{:S(2)}, u32[]{:S(2)}) collective-permute-start(bf16[8,3072]{1,0:T(8,128)(2,1)S(1)} %get-tuple-element.54), channel_id=1, source_target_pairs={{0,1},{1,0},{2,3},{3,2},{4,5},{5,4},{6,7},{7,6},{8,9},{9,8},{10,11... | collective-permute-start | bytes 147464 | tf_op jit(solution)/shard_map/ppermute | solution.py:277
  15.9 0.7 %shard_map.99 = (bf16[12,128,256]{2,1,0:T(8,128)(2,1)S(1)}, f32[256,1536]{1,0:T(8,128)S(1)}, f32[256,1536]{1,0:T(8,128)S(1)}) custom-call(bf16[256,1536]{1,0:T(8,128)(2,1)S(1)} %copy-done, bf16[256,1536]{1,0:T(8,128)(2,1)S(1)} %get-tuple-element.34.g_ref, f32[12,64,256]{2,1,0:T(8,128)S(1)} %get-tuple-element.35.e_ref, ...), custom_call_target="tpu_custom_call" | custom-call | flops 201326592 | bytes 6291456 | tf_op jit(solution)/shard_map/pallas_call | solution.py:41
  16.6 0.0 collective-permute-done.5.b_ref
  16.7 1.6 %collective-permute-start.6 = (bf16[16,3072]{1,0:T(8,128)(2,1)S(1)}, bf16[16,3072]{1,0:T(8,128)(2,1)S(1)}, u32[]{:S(2)}, u32[]{:S(2)}) collective-permute-start(bf16[16,3072]{1,0:T(8,128)(2,1)S(1)} %get-tuple-element.52), channel_id=1, source_target_pairs={{0,8},{4,12},{8,0},{12,4},{1,9},{5,13},{9,1},{13,5},{2,10},{6,14},... | collective-permute-start | bytes 294920 | tf_op jit(solution)/shard_map/ppermute | solution.py:277
  18.2 0.7 %collective-permute-done.7.b_ref = bf16[8,3072]{1,0:T(8,128)(2,1)S(1)} collective-permute-done((bf16[8,3072]{1,0:T(8,128)(2,1)S(1)}, bf16[8,3072]{1,0:T(8,128)(2,1)S(1)}, u32[]{:S(2)}, u32[]{:S(2)}) %collective-permute-start.7) | collective-permute-done | bytes 49184 | tf_op jit(solution)/shard_map/ppermute | solution.py:277
  18.9 2.8 %collective-permute-start.8 = (bf16[4,3072]{1,0:T(4,128)(2,1)S(1)}, bf16[4,3072]{1,0:T(4,128)(2,1)S(1)}, u32[]{:S(2)}, u32[]{:S(2)}) collective-permute-start(bf16[4,3072]{1,0:T(4,128)(2,1)S(1)} %get-tuple-element.56), channel_id=1, source_target_pairs={{0,2},{1,3},{2,0},{3,1},{4,6},{5,7},{6,4},{7,5},{8,10},{9,11},{10,... | collective-permute-start | bytes 73736 | tf_op jit(solution)/shard_map/ppermute | solution.py:277
  21.7 1.5 %shard_map.100 = bf16[256,1536]{1,0:T(8,128)(2,1)} custom-call(bf16[256,1536]{1,0:T(8,128)(2,1)S(1)} %copy-done.1, bf16[12,128,256]{2,1,0:T(8,128)(2,1)S(1)} %get-tuple-element.43.ds_ref, bf16[12,80,256]{2,1,0:T(8,128)(2,1)S(1)} %get-tuple-element.44.dsc_ref, bf16[16,3072]{1,0:T(8,128)(2,1)S(1)} %get-tuple-element.40.refs_0_, ...), custom_call_target="tpu_custom_call" | custom-call | flops 163577856 | bytes 2359296 | tf_op jit(solution)/shard_map/pallas_call | solution.py:41
  23.2 0.5 %collective-permute-done.8.refs_3_ = bf16[4,3072]{1,0:T(4,128)(2,1)S(1)} collective-permute-done((bf16[4,3072]{1,0:T(4,128)(2,1)S(1)}, bf16[4,3072]{1,0:T(4,128)(2,1)S(1)}, u32[]{:S(2)}, u32[]{:S(2)}) %collective-permute-start.8) | collective-permute-done | bytes 24608 | tf_op jit(solution)/shard_map/ppermute | solution.py:277
  23.7 0.0 collective-permute-done.6.refs_1_
  23.7 1.5 %shard_map.103 = (bf16[256,1536]{1,0:T(8,128)(2,1)}, bf16[256,1536]{1,0:T(8,128)(2,1)}) custom-call(bf16[256,48]{1,0:T(8,128)(2,1)S(1)} %get-tuple-element.45.table_ref, f32[24,128]{1,0:T(8,128)S(1)} %get-tuple-element.46.share_ref, f32[256,1536]{1,0:T(8,128)S(1)} %get-tuple-element.47.refs_0_.dk_ref, f32[256,1536]{1,0:T(8,128)S(1)} %get-tuple-element.48.dv_ref, ...), custom_call_target="tpu_custom_call" | custom-call | flops 75497472 | bytes 4718592 | tf_op jit(solution)/shard_map/pallas_call | solution.py:41
  (7 shorter events, 0.1 us)
Async XLA Ops:
  0.6 0.8 %copy-start.4 = (s32[256]{0:T(256)S(1)}, s32[256]{0:T(256)}, u32[]{:S(2)}) copy-start(s32[256]{0:T(256)} %param.12) | copy-start | bytes 3076
  0.6 0.8 %copy-start.5 = (s32[256]{0:T(256)S(1)}, s32[256]{0:T(256)}, u32[]{:S(2)}) copy-start(s32[256]{0:T(256)} %param.11) | copy-start | bytes 3076
  0.7 1.2 %copy-start.1 = (bf16[256,1536]{1,0:T(8,128)(2,1)S(1)}, bf16[256,1536]{1,0:T(8,128)(2,1)}, u32[]{:S(2)}) copy-start(bf16[256,1536]{1,0:T(8,128)(2,1)} %k_ref.5) | copy-start | bytes 2359300
  0.7 1.4 %copy-start.2 = (bf16[256,1536]{1,0:T(8,128)(2,1)S(1)}, bf16[256,1536]{1,0:T(8,128)(2,1)}, u32[]{:S(2)}) copy-start(bf16[256,1536]{1,0:T(8,128)(2,1)} %v_ref.3) | copy-start | bytes 2359300
  2.4 5.9 %collective-permute-start = (bf16[4,3072]{1,0:T(4,128)(2,1)S(1)}, bf16[4,3072]{1,0:T(4,128)(2,1)S(1)}, u32[]{:S(2)}, u32[]{:S(2)}) collective-permute-start(bf16[4,3072]{1,0:T(4,128)(2,1)S(1)} %get-tuple-element.33.a_ref), channel_id=1, source_target_pairs={{0,2},{1,3},{2,0},{3,1},{4,6},{5,7},{6,4},{7,5},{8,10},{9,11},{10,... | collective-permute-start | bytes 73736 | tf_op jit(solution)/shard_map/ppermute | solution.py:277
  6.5 3.8 %copy-start = (bf16[256,1536]{1,0:T(8,128)(2,1)S(1)}, bf16[256,1536]{1,0:T(8,128)(2,1)}, u32[]{:S(2)}) copy-start(bf16[256,1536]{1,0:T(8,128)(2,1)} %q_ref.5) | copy-start | bytes 2359300
  6.5 3.8 %copy-start.3 = (bf16[256,1536]{1,0:T(8,128)(2,1)S(1)}, bf16[256,1536]{1,0:T(8,128)(2,1)}, u32[]{:S(2)}) copy-start(bf16[256,1536]{1,0:T(8,128)(2,1)} %raw_ref.1) | copy-start | bytes 2359300
  6.5 5.0 %collective-permute-start.1 = (bf16[16,3072]{1,0:T(8,128)(2,1)S(1)}, bf16[16,3072]{1,0:T(8,128)(2,1)S(1)}, u32[]{:S(2)}, u32[]{:S(2)}) collective-permute-start(bf16[16,3072]{1,0:T(8,128)(2,1)S(1)} %get-tuple-element.40.refs_0_), channel_id=1, source_target_pairs={{0,8},{4,12},{8,0},{12,4},{1,9},{5,13},{9,1},{13,5},{2,10},{6,14},... | collective-permute-start | bytes 294920 | tf_op jit(solution)/shard_map/ppermute | solution.py:277
  8.3 4.2 %collective-permute-start.4 = (bf16[8,3072]{1,0:T(8,128)(2,1)S(1)}, bf16[8,3072]{1,0:T(8,128)(2,1)S(1)}, u32[]{:S(2)}, u32[]{:S(2)}) collective-permute-start(bf16[8,3072]{1,0:T(8,128)(2,1)S(1)} %shard_map.96.after_ref), channel_id=1, source_target_pairs={{0,1},{1,0},{2,3},{3,2},{4,5},{5,4},{6,7},{7,6},{8,9},{9,8},{10,11... | collective-permute-start | bytes 147464 | tf_op jit(solution)/shard_map/ppermute | solution.py:277
  10.3 2.2 %collective-permute-start.2 = (bf16[16,3072]{1,0:T(8,128)(2,1)S(1)}, bf16[16,3072]{1,0:T(8,128)(2,1)S(1)}, u32[]{:S(2)}, u32[]{:S(2)}) collective-permute-start(bf16[16,3072]{1,0:T(8,128)(2,1)S(1)} %get-tuple-element.40.refs_0_), channel_id=1, source_target_pairs={{0,4},{4,0},{8,12},{12,8},{1,5},{5,1},{9,13},{13,9},{2,6},{6,2},{1... | collective-permute-start | bytes 294920 | tf_op jit(solution)/shard_map/ppermute | solution.py:277
  11.5 1.5 %collective-permute-start.3 = (bf16[16,3072]{1,0:T(8,128)(2,1)S(1)}, bf16[16,3072]{1,0:T(8,128)(2,1)S(1)}, u32[]{:S(2)}, u32[]{:S(2)}) collective-permute-start(bf16[16,3072]{1,0:T(8,128)(2,1)S(1)} %collective-permute-done.1.refs_1_), channel_id=1, source_target_pairs={{0,4},{4,0},{8,12},{12,8},{1,5},{5,1},{9,13},{13,9},{2,6},{6,2},{1... | collective-permute-start | bytes 294920 | tf_op jit(solution)/shard_map/ppermute | solution.py:277
  14.4 2.2 %collective-permute-start.5 = (bf16[32,3072]{1,0:T(8,128)(2,1)S(1)}, bf16[32,3072]{1,0:T(8,128)(2,1)S(1)}, u32[]{:S(2)}, u32[]{:S(2)}) collective-permute-start(bf16[32,3072]{1,0:T(8,128)(2,1)S(1)} %get-tuple-element.50), channel_id=1, source_target_pairs={{0,4},{4,0},{8,12},{12,8},{1,5},{5,1},{9,13},{13,9},{2,6},{6,2},{1... | collective-permute-start | bytes 589832 | tf_op jit(solution)/shard_map/ppermute | solution.py:277
  14.8 4.1 %collective-permute-start.7 = (bf16[8,3072]{1,0:T(8,128)(2,1)S(1)}, bf16[8,3072]{1,0:T(8,128)(2,1)S(1)}, u32[]{:S(2)}, u32[]{:S(2)}) collective-permute-start(bf16[8,3072]{1,0:T(8,128)(2,1)S(1)} %get-tuple-element.54), channel_id=1, source_target_pairs={{0,1},{1,0},{2,3},{3,2},{4,5},{5,4},{6,7},{7,6},{8,9},{9,8},{10,11... | collective-permute-start | bytes 147464 | tf_op jit(solution)/shard_map/ppermute | solution.py:277
  16.7 7.0 %collective-permute-start.6 = (bf16[16,3072]{1,0:T(8,128)(2,1)S(1)}, bf16[16,3072]{1,0:T(8,128)(2,1)S(1)}, u32[]{:S(2)}, u32[]{:S(2)}) collective-permute-start(bf16[16,3072]{1,0:T(8,128)(2,1)S(1)} %get-tuple-element.52), channel_id=1, source_target_pairs={{0,8},{4,12},{8,0},{12,4},{1,9},{5,13},{9,1},{13,5},{2,10},{6,14},... | collective-permute-start | bytes 294920 | tf_op jit(solution)/shard_map/ppermute | solution.py:277
  18.9 4.8 %collective-permute-start.8 = (bf16[4,3072]{1,0:T(4,128)(2,1)S(1)}, bf16[4,3072]{1,0:T(4,128)(2,1)S(1)}, u32[]{:S(2)}, u32[]{:S(2)}) collective-permute-start(bf16[4,3072]{1,0:T(4,128)(2,1)S(1)} %get-tuple-element.56), channel_id=1, source_target_pairs={{0,2},{1,3},{2,0},{3,1},{4,6},{5,7},{6,4},{7,5},{8,10},{9,11},{10,... | collective-permute-start | bytes 73736 | tf_op jit(solution)/shard_map/ppermute | solution.py:277

commit v4 on v3

--- a/solution.py
+++ b/solution.py
@@ -73,7 +73,8 @@
         t_ref[:, at : at + features] = pooled[KF : KF + KT].astype(jnp.bfloat16)
 
 
-def join_kernel(a_ref, b_ref, out_ref):
+def join_kernel(a_ref, b_ref, *refs):
+    out_ref = refs[-1]
     parts = [a_ref[...].astype(jnp.float32), b_ref[...].astype(jnp.float32)]
     out_ref[...] = jnp.concatenate(parts, axis=0).astype(jnp.bfloat16)
 
@@ -86,25 +87,11 @@
     send_ref[...] = total[amount:].astype(jnp.bfloat16)
 
 
-def window_kernel(
-    valid_ref,
-    member_ref,
-    q_ref,
-    raw_ref,
-    k_ref,
-    v_ref,
-    after_ref,
-    g_ref,
-    e_ref,
-    d_ref,
-    top_ref,
-    sum_ref,
-    dot_ref,
-    table_ref,
-    share_ref,
+def value_kernel(
+    valid_ref, member_ref, raw_ref, v_ref, after_ref, g_ref, d_ref, table_ref, share_ref
 ):
     del after_ref
-    length, features = q_ref.shape
+    length, features = raw_ref.shape
     member = member_ref[...]
     share = 1.0 / jnp.maximum(jnp.sum(member, axis=1, keepdims=True), 1.0)
     share_ref[...] = jnp.broadcast_to(share, share_ref.shape)
@@ -113,28 +100,48 @@
     table_ref[...] = table.T[:, : 2 * ROWS].astype(jnp.bfloat16)
     valid = valid_ref[:1].astype(jnp.int32)
     live = lax.broadcasted_iota(jnp.int32, (length, HD), 0) % SPAN < valid
-    lane = lax.broadcasted_iota(jnp.int32, (WIN, PAIR), 1)
-    row = lax.broadcasted_iota(jnp.int32, (WIN, PAIR), 0)
-    first = lane < WIN
-    place = row + jnp.where(first, 0, WIN)
+    first = lax.broadcasted_iota(jnp.int32, (WIN, PAIR), 1) < WIN
     for h in range(features // HD):
         at = slice(h * HD, (h + 1) * HD)
         g = jnp.where(live, raw_ref[:, at], 0)
         g_ref[:, at] = g
         for p in range(length // PAIR):
             rows = slice(p * PAIR, (p + 1) * PAIR)
-            s = dot(k_ref[rows, at], q_ref[rows, at], NT)
             d = dot(v_ref[rows, at], g[rows], NT)
-            s = jnp.where(first, s[:WIN], s[WIN:])
-            s = jnp.where((place + p * PAIR) % SPAN < valid, s, MASK_FILL)
-            d = jnp.where(first, d[:WIN], d[WIN:])
-            top = jnp.max(s, axis=0, keepdims=True)
-            e = jnp.exp2((s - top) * SCALE)
-            e_ref[h, :, rows] = e
-            d_ref[h, :, rows] = d
-            top_ref[h : h + 1, rows] = top
-            sum_ref[h : h + 1, rows] = jnp.sum(e, axis=0, keepdims=True)
-            dot_ref[h : h + 1, rows] = jnp.sum(e * d, axis=0, keepdims=True)
+            d_ref[h, :, rows] = jnp.where(first, d[:WIN], d[WIN:])
+
+
+def window_kernel(
+    valid_ref, q_ref, k_ref, d_ref, after_ref, e_ref, top_ref, sum_ref, dot_ref
+):
+    del after_ref
+    length, features = q_ref.shape
+    valid = valid_ref[:1].astype(jnp.int32)
+    lane = lax.broadcasted_iota(jnp.int32, (WIN, PAIR), 1)
+    row = lax.broadcasted_iota(jnp.int32, (WIN, PAIR), 0)
+    first = lane < WIN
+    place = row + jnp.where(first, 0, WIN)
+    steps = [(h, p) for h in range(features // HD) for p in range(length // PAIR)]
+
+    def products(h, p):
+        rows = slice(p * PAIR, (p + 1) * PAIR)
+        at = slice(h * HD, (h + 1) * HD)
+        return dot(k_ref[rows, at], q_ref[rows, at], NT)
+
+    ahead = products(*steps[0])
+    for step, (h, p) in enumerate(steps):
+        s = ahead
+        if step + 1 < len(steps):
+            ahead = products(*steps[step + 1])
+        rows = slice(p * PAIR, (p + 1) * PAIR)
+        s = jnp.where(first, s[:WIN], s[WIN:])
+        s = jnp.where((place + p * PAIR) % SPAN < valid, s, MASK_FILL)
+        top = jnp.max(s, axis=0, keepdims=True)
+        e = jnp.exp2((s - top) * SCALE)
+        e_ref[h, :, rows] = e
+        top_ref[h : h + 1, rows] = top
+        sum_ref[h : h + 1, rows] = jnp.sum(e, axis=0, keepdims=True)
+        dot_ref[h : h + 1, rows] = jnp.sum(e * d_ref[h, :, rows], axis=0, keepdims=True)
 
 
 def coarse_rows(refs, at):
@@ -303,49 +310,39 @@
         4 * size,
     )
 
+    def join(a, b, flops, after=()):
+        ins = [(a, VMEM), (b, VMEM)] + [(x, ANY) for x in after]
+        both = shape((a.shape[0] + b.shape[0], 2 * features), bf16)
+        return call(join_kernel, [both], ins, flops, 0)[0]
+
     masks = [space >> (i + 1) for i in range(space.bit_length() - 1)]
     have_t = own_t
     for mask in masks[:-1]:
-        (have_t,) = call(
-            join_kernel,
-            [shape((2 * have_t.shape[0], 2 * features), bf16)],
-            [(have_t, VMEM), (swap(have_t, "space", space, mask), VMEM)],
-            JOIN_FLOPS,
-            0,
-        )
+        have_t = join(have_t, swap(have_t, "space", space, mask), JOIN_FLOPS)
     got_t = swap(have_t, "space", space, masks[-1])
     from_2 = swap(own_f, "tm", tm, 2)
     from_1 = swap(own_f, "tm", tm, 1)
     from_3 = swap(from_2, "tm", tm, 1)
-    coarse = [own_f, from_2, from_1, from_3, jnp.concatenate([have_t, got_t], axis=0)]
     total = tm * KF + space * KT
+
+    wide = shape((heads, WIN, length), f32)
+    g, d, table, share = call(
+        value_kernel,
+        [block, wide, shape((length, 2 * ROWS), bf16), shape((ROWS, HD), f32)],
+        [(x, VMEM) for x in (valid, member, grad_out, value_in)] + [(have_t, ANY)],
+        2 * size * PAIR,
+        8 * size,
+    )
+    e, top, window_sum, window_dot = call(
+        window_kernel,
+        [wide, stat, stat, stat],
+        [(x, VMEM) for x in (valid, query, key_in, d)] + [(from_2, ANY)],
+        2 * size * PAIR,
+        8 * size,
+    )
+
+    coarse = [own_f, from_2, from_1, from_3, join(have_t, got_t, JOIN_FLOPS, [top])]
     coarse_in = [(x, VMEM) for x in coarse]
-
-    g, e, d, top, window_sum, window_dot, table, share = call(
-        window_kernel,
-        [
-            block,
-            shape((heads, WIN, length), f32),
-            shape((heads, WIN, length), f32),
-            stat,
-            stat,
-            stat,
-            shape((length, 2 * ROWS), bf16),
-            shape((ROWS, HD), f32),
-        ],
-        [
-            (valid, VMEM),
-            (member, VMEM),
-            (query, VMEM),
-            (grad_out, VMEM),
-            (key_in, VMEM),
-            (value_in, VMEM),
-            (have_t, ANY),
-        ],
-        4 * size * PAIR,
-        16 * size,
-    )
-
     half = shape((space * KT // 2, 2 * features), bf16)
     pair = shape((2 * KF, 2 * features), bf16)
     dsc, weight, delta, f_keep, f_send, t_keep, t_send = call(

time: 25.3 us -> 24.9 us (0.984)
  waiting for transfers between devices: 2.41 us -> 1.29 us
  starting transfers between devices: 14 us -> 14.4 us
    ppermute x9, waiting for transfers between devices: 2.41 us -> 1.29 us  [swap(): return lax.ppermute(x, axis, [(i, i ^ mask) for i in range(size)])]
    ppermute x9, starting transfers between devices: 14 us -> 14.4 us  [swap(): return lax.ppermute(x, axis, [(i, i ^ mask) for i in range(size)])]
    pallas_call x10 -> x12, Pallas kernels: 6.65 us -> 6.89 us  [call(): pl.pallas_call(kernel, out_shape=outs, in_specs=[spec for _, spec in ins]...]
  transfers between devices with their start and end apart: 9 -> 9, of which waited for: 5 -> 5; matrix products, arithmetic and copies ran while one was open for 0% -> 0% of each run, Pallas kernels for 14% -> 15%
where the time goes in v4:
time: 24.9 us; the launch traced here: 24.7 us
  starting transfers between devices  14.4 us (58%)
  Pallas kernels  6.89 us (28%)
  between operations  1.53 us (6%)
  waiting for transfers between devices  1.29 us (5%)
  local copies, waits for them, and re-layouts  0.58 us (2%)
    ppermute x9, starting transfers between devices, swap(): return lax.ppermute(x, axis, [(i, i ^ mask) for i in range(size)])  14.4 us
    pallas_call x12, Pallas kernels, call(): pl.pallas_call(kernel, out_shape=outs, in_specs=[spec for _, spec in ins]...  6.89 us
    ppermute x9, waiting for transfers between devices, swap(): return lax.ppermute(x, axis, [(i, i ^ mask) for i in range(size)])  1.29 us
    unnamed x12, local copies, waits for them, and re-layouts  0.58 us
  transfers between devices with their start and end apart: 9, of which 5 were waited for; matrix products, arithmetic and copies ran while one was open for 0% of the time, Pallas kernels for 15%

profile of v4, /device:TPU:0, one launch (start us, length us, event | category | flops | bytes accessed | tf_op | source)
XLA Modules:
  0.0 24.7 jit_solution(12300037231740253026)
XLA Ops:
  0.6 0.0 copy-start.4
  0.6 0.0 copy-start.5
  0.7 0.0 copy-start.1
  0.7 0.0 copy-start.2
  1.4 0.0 copy-done.4
  1.5 0.0 copy-done.5
  1.5 0.3 %copy-done.1 = bf16[256,1536]{1,0:T(8,128)(2,1)S(1)} copy-done((bf16[256,1536]{1,0:T(8,128)(2,1)S(1)}, bf16[256,1536]{1,0:T(8,128)(2,1)}, u32[]{:S(2)}) %copy-start.1) | copy-done | bytes 786456
  1.8 0.2 copy-done.2
  2.0 0.4 %shard_map.95 = (bf16[4,3072]{1,0:T(4,128)(2,1)S(1)}, bf16[16,3072]{1,0:T(8,128)(2,1)S(1)}, f32[24,256]{1,0:T(8,128)S(1)}, f32[8,128]{1,0:T(8,128)S(1)}) custom-call(s32[1,256]{1,0:T(1,128)S(1)} %add.14.code_ref, bf16[256,1536]{1,0:T(8,128)(2,1)S(1)} %copy-done.1, bf16[256,1536]{1,0:T(8,128)(2,1)S(1)} %copy-done.2), custom_call_target="tpu_custom_call" | custom-call | flops 37748736 | bytes 1572864 | tf_op jit(solution)/shard_map/pallas_call | solution.py:41
  2.4 4.1 %collective-permute-start = (bf16[4,3072]{1,0:T(4,128)(2,1)S(1)}, bf16[4,3072]{1,0:T(4,128)(2,1)S(1)}, u32[]{:S(2)}, u32[]{:S(2)}) collective-permute-start(bf16[4,3072]{1,0:T(4,128)(2,1)S(1)} %get-tuple-element.33.a_ref), channel_id=1, source_target_pairs={{0,2},{1,3},{2,0},{3,1},{4,6},{5,7},{6,4},{7,5},{8,10},{9,11},{10,... | collective-permute-start | bytes 73736 | tf_op jit(solution)/shard_map/ppermute | solution.py:284
  6.5 0.0 copy-start.3
  6.5 1.5 %collective-permute-start.1 = (bf16[16,3072]{1,0:T(8,128)(2,1)S(1)}, bf16[16,3072]{1,0:T(8,128)(2,1)S(1)}, u32[]{:S(2)}, u32[]{:S(2)}) collective-permute-start(bf16[16,3072]{1,0:T(8,128)(2,1)S(1)} %get-tuple-element.36.refs_0_), channel_id=1, source_target_pairs={{0,8},{4,12},{8,0},{12,4},{1,9},{5,13},{9,1},{13,5},{2,10},{6,14},... | collective-permute-start | bytes 294920 | tf_op jit(solution)/shard_map/ppermute | solution.py:284
  8.0 0.3 %collective-permute-done.b_ref = bf16[4,3072]{1,0:T(4,128)(2,1)S(1)} collective-permute-done((bf16[4,3072]{1,0:T(4,128)(2,1)S(1)}, bf16[4,3072]{1,0:T(4,128)(2,1)S(1)}, u32[]{:S(2)}, u32[]{:S(2)}) %collective-permute-start) | collective-permute-done | bytes 24608 | tf_op jit(solution)/shard_map/ppermute | solution.py:284
  8.3 0.0 copy-start
  8.3 2.0 %collective-permute-start.4 = (bf16[8,3072]{1,0:T(8,128)(2,1)S(1)}, bf16[8,3072]{1,0:T(8,128)(2,1)S(1)}, u32[]{:S(2)}, u32[]{:S(2)}) collective-permute-start(bf16[8,3072]{1,0:T(8,128)(2,1)S(1)} %shard_map.96.after_ref.a_ref), channel_id=1, source_target_pairs={{0,1},{1,0},{2,3},{3,2},{4,5},{5,4},{6,7},{7,6},{8,9},{9,8},{10,11... | collective-permute-start | bytes 147464 | tf_op jit(solution)/shard_map/ppermute | solution.py:284
  10.3 0.0 collective-permute-start.2
  10.3 0.0 copy-done.3
  10.3 0.7 %shard_map.97 = (bf16[256,1536]{1,0:T(8,128)(2,1)S(1)}, f32[12,64,256]{2,1,0:T(8,128)S(1)}, bf16[256,48]{1,0:T(8,128)(2,1)S(1)}, f32[24,128]{1,0:T(8,128)S(1)}) custom-call(f32[8,128]{1,0:T(8,128)S(1)} %get-tuple-element.31.valid_ref, f32[24,256]{1,0:T(8,128)S(1)} %get-tuple-element.32.member_ref, bf16[256,1536]{1,0:T(8,128)(2,1)S(1)} %copy-done.3, ...), custom_call_target="tpu_custom_call" | custom-call | flops 100663296 | bytes 3145728 | tf_op jit(solution)/shard_map/pallas_call | solution.py:41
  11.0 0.1 collective-permute-done.1.after_ref.refs_1_
  11.1 0.5 %collective-permute-start.3 = (bf16[16,3072]{1,0:T(8,128)(2,1)S(1)}, bf16[16,3072]{1,0:T(8,128)(2,1)S(1)}, u32[]{:S(2)}, u32[]{:S(2)}) collective-permute-start(bf16[16,3072]{1,0:T(8,128)(2,1)S(1)} %collective-permute-done.1.after_ref.refs_1_), channel_id=1, source_target_pairs={{0,4},{4,0},{8,12},{12,8},{1,5},{5,1},{9,13},{13,9},{2,6},{6,2},{1... | collective-permute-start | bytes 294920 | tf_op jit(solution)/shard_map/ppermute | solution.py:284
  11.6 0.0 copy-done
  11.6 0.7 %shard_map.98 = (f32[12,64,256]{2,1,0:T(8,128)S(1)}, f32[12,256]{1,0:T(8,128)S(1)}, f32[12,256]{1,0:T(8,128)S(1)}, f32[12,256]{1,0:T(8,128)S(1)}) custom-call(f32[8,128]{1,0:T(8,128)S(1)} %get-tuple-element.31.valid_ref, bf16[256,1536]{1,0:T(8,128)(2,1)S(1)} %copy-done, bf16[256,1536]{1,0:T(8,128)(2,1)S(1)} %copy-done.1, ...), custom_call_target="tpu_custom_call" | custom-call | flops 100663296 | bytes 3145728 | tf_op jit(solution)/shard_map/pallas_call | solution.py:41
  12.3 0.2 collective-permute-done.4.b_ref
  12.5 0.0 collective-permute-done.2.refs_2_
  12.5 0.0 collective-permute-done.3.refs_3_
  12.5 1.4 %shard_map.100 = (bf16[12,80,256]{2,1,0:T(8,128)(2,1)S(1)}, f32[12,256]{1,0:T(8,128)S(1)}, f32[12,256]{1,0:T(8,128)S(1)}, bf16[32,3072]{1,0:T(8,128)(2,1)S(1)}, ...) custom-call(bf16[256,1536]{1,0:T(8,128)(2,1)S(1)} %copy-done, ...), custom_call_target="tpu_custom_call" | custom-call | flops 251658240 | bytes 3145728 | tf_op jit(solution)/shard_map/pallas_call | solution.py:41
  13.9 0.4 %collective-permute-start.5 = (bf16[32,3072]{1,0:T(8,128)(2,1)S(1)}, bf16[32,3072]{1,0:T(8,128)(2,1)S(1)}, u32[]{:S(2)}, u32[]{:S(2)}) collective-permute-start(bf16[32,3072]{1,0:T(8,128)(2,1)S(1)} %get-tuple-element.50), channel_id=1, source_target_pairs={{0,4},{4,0},{8,12},{12,8},{1,5},{5,1},{9,13},{13,9},{2,6},{6,2},{1... | collective-permute-start | bytes 589832 | tf_op jit(solution)/shard_map/ppermute | solution.py:284
  14.3 1.6 %collective-permute-start.7 = (bf16[8,3072]{1,0:T(8,128)(2,1)S(1)}, bf16[8,3072]{1,0:T(8,128)(2,1)S(1)}, u32[]{:S(2)}, u32[]{:S(2)}) collective-permute-start(bf16[8,3072]{1,0:T(8,128)(2,1)S(1)} %get-tuple-element.54), channel_id=1, source_target_pairs={{0,1},{1,0},{2,3},{3,2},{4,5},{5,4},{6,7},{7,6},{8,9},{9,8},{10,11... | collective-permute-start | bytes 147464 | tf_op jit(solution)/shard_map/ppermute | solution.py:284
  15.9 0.7 %shard_map.101 = (bf16[12,128,256]{2,1,0:T(8,128)(2,1)S(1)}, f32[256,1536]{1,0:T(8,128)S(1)}, f32[256,1536]{1,0:T(8,128)S(1)}) custom-call(bf16[256,1536]{1,0:T(8,128)(2,1)S(1)} %copy-done, bf16[256,1536]{1,0:T(8,128)(2,1)S(1)} %get-tuple-element.34.g_ref, f32[12,64,256]{2,1,0:T(8,128)S(1)} %get-tuple-element.37.e_ref, ...), custom_call_target="tpu_custom_call" | custom-call | flops 201326592 | bytes 6291456 | tf_op jit(solution)/shard_map/pallas_call | solution.py:41
  16.6 0.0 collective-permute-done.5.b_ref
  16.6 0.1 shard_map.103
  16.7 1.6 %collective-permute-start.6 = (bf16[16,3072]{1,0:T(8,128)(2,1)S(1)}, bf16[16,3072]{1,0:T(8,128)(2,1)S(1)}, u32[]{:S(2)}, u32[]{:S(2)}) collective-permute-start(bf16[16,3072]{1,0:T(8,128)(2,1)S(1)} %get-tuple-element.52), channel_id=1, source_target_pairs={{0,8},{4,12},{8,0},{12,4},{1,9},{5,13},{9,1},{13,5},{2,10},{6,14},... | collective-permute-start | bytes 294920 | tf_op jit(solution)/shard_map/ppermute | solution.py:284
  18.3 0.2 collective-permute-done.7.b_ref
  18.4 2.8 %collective-permute-start.8 = (bf16[4,3072]{1,0:T(4,128)(2,1)S(1)}, bf16[4,3072]{1,0:T(4,128)(2,1)S(1)}, u32[]{:S(2)}, u32[]{:S(2)}) collective-permute-start(bf16[4,3072]{1,0:T(4,128)(2,1)S(1)} %get-tuple-element.56), channel_id=1, source_target_pairs={{0,2},{1,3},{2,0},{3,1},{4,6},{5,7},{6,4},{7,5},{8,10},{9,11},{10,... | collective-permute-start | bytes 73736 | tf_op jit(solution)/shard_map/ppermute | solution.py:284
  21.3 1.5 %shard_map.102 = bf16[256,1536]{1,0:T(8,128)(2,1)} custom-call(bf16[256,1536]{1,0:T(8,128)(2,1)S(1)} %copy-done.1, bf16[12,128,256]{2,1,0:T(8,128)(2,1)S(1)} %get-tuple-element.43.ds_ref, bf16[12,80,256]{2,1,0:T(8,128)(2,1)S(1)} %get-tuple-element.44.dsc_ref, bf16[16,3072]{1,0:T(8,128)(2,1)S(1)} %get-tuple-element.36.refs_0_, ...), custom_call_target="tpu_custom_call" | custom-call | flops 163577856 | bytes 2359296 | tf_op jit(solution)/shard_map/pallas_call | solution.py:41
  22.8 0.5 %collective-permute-done.8.refs_3_ = bf16[4,3072]{1,0:T(4,128)(2,1)S(1)} collective-permute-done((bf16[4,3072]{1,0:T(4,128)(2,1)S(1)}, bf16[4,3072]{1,0:T(4,128)(2,1)S(1)}, u32[]{:S(2)}, u32[]{:S(2)}) %collective-permute-start.8) | collective-permute-done | bytes 24608 | tf_op jit(solution)/shard_map/ppermute | solution.py:284
  23.2 0.0 collective-permute-done.6.refs_1_
  23.2 1.5 %shard_map.105 = (bf16[256,1536]{1,0:T(8,128)(2,1)}, bf16[256,1536]{1,0:T(8,128)(2,1)}) custom-call(bf16[256,48]{1,0:T(8,128)(2,1)S(1)} %get-tuple-element.45.table_ref, f32[24,128]{1,0:T(8,128)S(1)} %get-tuple-element.46.share_ref, f32[256,1536]{1,0:T(8,128)S(1)} %get-tuple-element.47.refs_0_.dk_ref, f32[256,1536]{1,0:T(8,128)S(1)} %get-tuple-element.48.dv_ref, ...), custom_call_target="tpu_custom_call" | custom-call | flops 75497472 | bytes 4718592 | tf_op jit(solution)/shard_map/pallas_call | solution.py:41
  (6 shorter events, 0.1 us)
Async XLA Ops:
  0.6 0.8 %copy-start.4 = (s32[256]{0:T(256)S(1)}, s32[256]{0:T(256)}, u32[]{:S(2)}) copy-start(s32[256]{0:T(256)} %param.12) | copy-start | bytes 3076
  0.6 0.8 %copy-start.5 = (s32[256]{0:T(256)S(1)}, s32[256]{0:T(256)}, u32[]{:S(2)}) copy-start(s32[256]{0:T(256)} %param.11) | copy-start | bytes 3076
  0.7 1.2 %copy-start.1 = (bf16[256,1536]{1,0:T(8,128)(2,1)S(1)}, bf16[256,1536]{1,0:T(8,128)(2,1)}, u32[]{:S(2)}) copy-start(bf16[256,1536]{1,0:T(8,128)(2,1)} %k_ref.5) | copy-start | bytes 2359300
  0.7 1.4 %copy-start.2 = (bf16[256,1536]{1,0:T(8,128)(2,1)S(1)}, bf16[256,1536]{1,0:T(8,128)(2,1)}, u32[]{:S(2)}) copy-start(bf16[256,1536]{1,0:T(8,128)(2,1)} %v_ref.3) | copy-start | bytes 2359300
  2.4 5.9 %collective-permute-start = (bf16[4,3072]{1,0:T(4,128)(2,1)S(1)}, bf16[4,3072]{1,0:T(4,128)(2,1)S(1)}, u32[]{:S(2)}, u32[]{:S(2)}) collective-permute-start(bf16[4,3072]{1,0:T(4,128)(2,1)S(1)} %get-tuple-element.33.a_ref), channel_id=1, source_target_pairs={{0,2},{1,3},{2,0},{3,1},{4,6},{5,7},{6,4},{7,5},{8,10},{9,11},{10,... | collective-permute-start | bytes 73736 | tf_op jit(solution)/shard_map/ppermute | solution.py:284
  6.5 3.8 %copy-start.3 = (bf16[256,1536]{1,0:T(8,128)(2,1)S(1)}, bf16[256,1536]{1,0:T(8,128)(2,1)}, u32[]{:S(2)}) copy-start(bf16[256,1536]{1,0:T(8,128)(2,1)} %raw_ref.1) | copy-start | bytes 2359300
  6.5 4.6 %collective-permute-start.1 = (bf16[16,3072]{1,0:T(8,128)(2,1)S(1)}, bf16[16,3072]{1,0:T(8,128)(2,1)S(1)}, u32[]{:S(2)}, u32[]{:S(2)}) collective-permute-start(bf16[16,3072]{1,0:T(8,128)(2,1)S(1)} %get-tuple-element.36.refs_0_), channel_id=1, source_target_pairs={{0,8},{4,12},{8,0},{12,4},{1,9},{5,13},{9,1},{13,5},{2,10},{6,14},... | collective-permute-start | bytes 294920 | tf_op jit(solution)/shard_map/ppermute | solution.py:284
  8.3 3.3 %copy-start = (bf16[256,1536]{1,0:T(8,128)(2,1)S(1)}, bf16[256,1536]{1,0:T(8,128)(2,1)}, u32[]{:S(2)}) copy-start(bf16[256,1536]{1,0:T(8,128)(2,1)} %q_ref.5) | copy-start | bytes 2359300
  8.3 4.2 %collective-permute-start.4 = (bf16[8,3072]{1,0:T(8,128)(2,1)S(1)}, bf16[8,3072]{1,0:T(8,128)(2,1)S(1)}, u32[]{:S(2)}, u32[]{:S(2)}) collective-permute-start(bf16[8,3072]{1,0:T(8,128)(2,1)S(1)} %shard_map.96.after_ref.a_ref), channel_id=1, source_target_pairs={{0,1},{1,0},{2,3},{3,2},{4,5},{5,4},{6,7},{7,6},{8,9},{9,8},{10,11... | collective-permute-start | bytes 147464 | tf_op jit(solution)/shard_map/ppermute | solution.py:284
  10.3 2.2 %collective-permute-start.2 = (bf16[16,3072]{1,0:T(8,128)(2,1)S(1)}, bf16[16,3072]{1,0:T(8,128)(2,1)S(1)}, u32[]{:S(2)}, u32[]{:S(2)}) collective-permute-start(bf16[16,3072]{1,0:T(8,128)(2,1)S(1)} %get-tuple-element.36.refs_0_), channel_id=1, source_target_pairs={{0,4},{4,0},{8,12},{12,8},{1,5},{5,1},{9,13},{13,9},{2,6},{6,2},{1... | collective-permute-start | bytes 294920 | tf_op jit(solution)/shard_map/ppermute | solution.py:284
  11.1 1.4 %collective-permute-start.3 = (bf16[16,3072]{1,0:T(8,128)(2,1)S(1)}, bf16[16,3072]{1,0:T(8,128)(2,1)S(1)}, u32[]{:S(2)}, u32[]{:S(2)}) collective-permute-start(bf16[16,3072]{1,0:T(8,128)(2,1)S(1)} %collective-permute-done.1.after_ref.refs_1_), channel_id=1, source_target_pairs={{0,4},{4,0},{8,12},{12,8},{1,5},{5,1},{9,13},{13,9},{2,6},{6,2},{1... | collective-permute-start | bytes 294920 | tf_op jit(solution)/shard_map/ppermute | solution.py:284
  13.9 2.7 %collective-permute-start.5 = (bf16[32,3072]{1,0:T(8,128)(2,1)S(1)}, bf16[32,3072]{1,0:T(8,128)(2,1)S(1)}, u32[]{:S(2)}, u32[]{:S(2)}) collective-permute-start(bf16[32,3072]{1,0:T(8,128)(2,1)S(1)} %get-tuple-element.50), channel_id=1, source_target_pairs={{0,4},{4,0},{8,12},{12,8},{1,5},{5,1},{9,13},{13,9},{2,6},{6,2},{1... | collective-permute-start | bytes 589832 | tf_op jit(solution)/shard_map/ppermute | solution.py:284
  14.3 4.1 %collective-permute-start.7 = (bf16[8,3072]{1,0:T(8,128)(2,1)S(1)}, bf16[8,3072]{1,0:T(8,128)(2,1)S(1)}, u32[]{:S(2)}, u32[]{:S(2)}) collective-permute-start(bf16[8,3072]{1,0:T(8,128)(2,1)S(1)} %get-tuple-element.54), channel_id=1, source_target_pairs={{0,1},{1,0},{2,3},{3,2},{4,5},{5,4},{6,7},{7,6},{8,9},{9,8},{10,11... | collective-permute-start | bytes 147464 | tf_op jit(solution)/shard_map/ppermute | solution.py:284
  16.7 6.5 %collective-permute-start.6 = (bf16[16,3072]{1,0:T(8,128)(2,1)S(1)}, bf16[16,3072]{1,0:T(8,128)(2,1)S(1)}, u32[]{:S(2)}, u32[]{:S(2)}) collective-permute-start(bf16[16,3072]{1,0:T(8,128)(2,1)S(1)} %get-tuple-element.52), channel_id=1, source_target_pairs={{0,8},{4,12},{8,0},{12,4},{1,9},{5,13},{9,1},{13,5},{2,10},{6,14},... | collective-permute-start | bytes 294920 | tf_op jit(solution)/shard_map/ppermute | solution.py:284
  18.4 4.8 %collective-permute-start.8 = (bf16[4,3072]{1,0:T(4,128)(2,1)S(1)}, bf16[4,3072]{1,0:T(4,128)(2,1)S(1)}, u32[]{:S(2)}, u32[]{:S(2)}) collective-permute-start(bf16[4,3072]{1,0:T(4,128)(2,1)S(1)} %get-tuple-element.56), channel_id=1, source_target_pairs={{0,2},{1,3},{2,0},{3,1},{4,6},{5,7},{6,4},{7,5},{8,10},{9,11},{10,... | collective-permute-start | bytes 73736 | tf_op jit(solution)/shard_map/ppermute | solution.py:284

commit v5 on v4

--- a/solution.py
+++ b/solution.py
@@ -55,8 +55,10 @@
     out_ref[...] = jnp.zeros_like(out_ref)
 
 
-def pool_kernel(code_ref, k_ref, v_ref, t_ref, f_ref, member_ref, valid_ref):
-    length, features = k_ref.shape
+def pool_key_kernel(
+    code_ref, k_ref, t_ref, f_ref, member_ref, valid_ref, share_ref
+):
+    length = k_ref.shape[0]
     code = code_ref[...]
     label = lax.broadcasted_iota(jnp.int32, (ROWS, length), 0)
     ids = jnp.where(label < KF, code // KT, code % KT + KF)
@@ -66,11 +68,19 @@
     count = jnp.sum(count, axis=1, keepdims=True) * (SPAN / length)
     valid_ref[...] = jnp.broadcast_to(count, valid_ref.shape)
     share = 1.0 / jnp.maximum(jnp.sum(member, axis=1, keepdims=True), 1.0)
-    table = member.astype(jnp.bfloat16)
-    for ref, at in ((k_ref, 0), (v_ref, features)):
-        pooled = dot(table, ref[...], NN) * share
-        f_ref[:, at : at + features] = pooled[:KF].astype(jnp.bfloat16)
-        t_ref[:, at : at + features] = pooled[KF : KF + KT].astype(jnp.bfloat16)
+    share_ref[...] = jnp.broadcast_to(share, share_ref.shape)
+    pooled = dot(member.astype(jnp.bfloat16), k_ref[...], NN) * share
+    f_ref[...] = pooled[:KF].astype(jnp.bfloat16)
+    t_ref[...] = pooled[KF : KF + KT].astype(jnp.bfloat16)
+
+
+def pool_value_kernel(member_ref, share_ref, tk_ref, fk_ref, v_ref, t_ref, f_ref):
+    features = v_ref.shape[1]
+    t_ref[:, :features] = tk_ref[...]
+    f_ref[:, :features] = fk_ref[...]
+    pooled = dot(member_ref[...].astype(jnp.bfloat16), v_ref[...], NN) * share_ref[:, :1]
+    f_ref[:, features:] = pooled[:KF].astype(jnp.bfloat16)
+    t_ref[:, features:] = pooled[KF : KF + KT].astype(jnp.bfloat16)
 
 
 def join_kernel(a_ref, b_ref, *refs):
@@ -88,13 +98,11 @@
 
 
 def value_kernel(
-    valid_ref, member_ref, raw_ref, v_ref, after_ref, g_ref, d_ref, table_ref, share_ref
+    valid_ref, member_ref, raw_ref, v_ref, after_ref, g_ref, d_ref, table_ref
 ):
     del after_ref
     length, features = raw_ref.shape
     member = member_ref[...]
-    share = 1.0 / jnp.maximum(jnp.sum(member, axis=1, keepdims=True), 1.0)
-    share_ref[...] = jnp.broadcast_to(share, share_ref.shape)
     blank = jnp.zeros((HD - 2 * ROWS, length), jnp.float32)
     table = jnp.concatenate([member, member, blank], axis=0)
     table_ref[...] = table.T[:, : 2 * ROWS].astype(jnp.bfloat16)
@@ -188,11 +196,11 @@
                 ref[:, start : start + HD] = term[begin:end].astype(jnp.bfloat16)
                 begin = end
 
-    ahead, behind = products(0), None
+    ahead, behind = [products(h) for h in range(min(2, heads))], None
     for h in range(heads):
-        q, g, s, d = ahead
-        if h + 1 < heads:
-            ahead = products(h + 1)
+        q, g, s, d = ahead.pop(0)
+        if h + 2 < heads:
+            ahead.append(products(h + 2))
         if behind:
             gradients(*behind)
         ds, w = weigh(h, s, d)
@@ -297,17 +305,25 @@
     (zero,) = call(start_kernel, [shape((1, length), jnp.int32)], [], JOIN_FLOPS, 0)
     live = lax.iota(jnp.int32, length) % SPAN < tile_valid.reshape(())
     code = jnp.where(live, frame_ids * KT + time_ids, -1).reshape(1, length) + zero
-    own_t, own_f, member, valid = call(
-        pool_kernel,
+    tk, fk, member, valid, share = call(
+        pool_key_kernel,
         [
-            shape((KT, 2 * features), bf16),
-            shape((KF, 2 * features), bf16),
+            shape((KT, features), bf16),
+            shape((KF, features), bf16),
             shape((ROWS, length), f32),
             shape((8, PAIR), f32),
+            shape((ROWS, HD), f32),
         ],
-        [(code, VMEM), (key_in, VMEM), (value_in, VMEM)],
-        4 * size * ROWS,
-        4 * size,
+        [(x, VMEM) for x in (code, key_in)],
+        2 * size * ROWS,
+        2 * size,
+    )
+    own_t, own_f = call(
+        pool_value_kernel,
+        [shape((KT, 2 * features), bf16), shape((KF, 2 * features), bf16)],
+        [(x, VMEM) for x in (member, share, tk, fk, value_in)],
+        2 * size * ROWS,
+        2 * size,
     )
 
     def join(a, b, flops, after=()):
@@ -326,9 +342,9 @@
     total = tm * KF + space * KT
 
     wide = shape((heads, WIN, length), f32)
-    g, d, table, share = call(
+    g, d, table = call(
         value_kernel,
-        [block, wide, shape((length, 2 * ROWS), bf16), shape((ROWS, HD), f32)],
+        [block, wide, shape((length, 2 * ROWS), bf16)],
         [(x, VMEM) for x in (valid, member, grad_out, value_in)] + [(have_t, ANY)],
         2 * size * PAIR,
         8 * size,

time: 24.9 us -> 24.5 us (0.984)
    pallas_call x12 -> x13, Pallas kernels: 6.89 us -> 6.78 us  [call(): pl.pallas_call(kernel, out_shape=outs, in_specs=[spec for _, spec in ins]...]
where the time goes in v5:
time: 24.5 us; the launch traced here: 24.4 us
  starting transfers between devices  14.4 us (59%)
  Pallas kernels  6.78 us (28%)
  between operations  1.53 us (6%)
  waiting for transfers between devices  1.29 us (5%)
  local copies, waits for them, and re-layouts  0.35 us (1%)
    ppermute x9, starting transfers between devices, swap(): return lax.ppermute(x, axis, [(i, i ^ mask) for i in range(size)])  14.4 us
    pallas_call x13, Pallas kernels, call(): pl.pallas_call(kernel, out_shape=outs, in_specs=[spec for _, spec in ins]...  6.78 us
    ppermute x9, waiting for transfers between devices, swap(): return lax.ppermute(x, axis, [(i, i ^ mask) for i in range(size)])  1.29 us
  transfers between devices with their start and end apart: 9, of which 5 were waited for; matrix products, arithmetic and copies ran while one was open for 0% of the time, Pallas kernels for 15%

profile of v5, /device:TPU:0, one launch (start us, length us, event | category | flops | bytes accessed | tf_op | source)
XLA Modules:
  0.0 24.4 jit_solution(7559138498345539434)
XLA Ops:
  0.6 0.0 copy-start.4
  0.6 0.0 copy-start.5
  0.7 0.0 copy-start.1
  0.7 0.0 copy-start.2
  1.4 0.0 copy-done.4
  1.5 0.0 copy-done.5
  1.5 0.3 %copy-done.1 = bf16[256,1536]{1,0:T(8,128)(2,1)S(1)} copy-done((bf16[256,1536]{1,0:T(8,128)(2,1)S(1)}, bf16[256,1536]{1,0:T(8,128)(2,1)}, u32[]{:S(2)}) %copy-start.1) | copy-done | bytes 786456
  1.8 0.2 shard_map.95
  2.0 0.0 copy-done.2
  2.1 0.2 shard_map.96
  2.3 4.1 %collective-permute-start = (bf16[4,3072]{1,0:T(4,128)(2,1)S(1)}, bf16[4,3072]{1,0:T(4,128)(2,1)S(1)}, u32[]{:S(2)}, u32[]{:S(2)}) collective-permute-start(bf16[4,3072]{1,0:T(4,128)(2,1)S(1)} %get-tuple-element.38.a_ref), channel_id=1, source_target_pairs={{0,2},{1,3},{2,0},{3,1},{4,6},{5,7},{6,4},{7,5},{8,10},{9,11},{10,... | collective-permute-start | bytes 73736 | tf_op jit(solution)/shard_map/ppermute | solution.py:292
  6.4 0.0 copy-start.3
  6.4 1.5 %collective-permute-start.1 = (bf16[16,3072]{1,0:T(8,128)(2,1)S(1)}, bf16[16,3072]{1,0:T(8,128)(2,1)S(1)}, u32[]{:S(2)}, u32[]{:S(2)}) collective-permute-start(bf16[16,3072]{1,0:T(8,128)(2,1)S(1)} %get-tuple-element.41.refs_0_), channel_id=1, source_target_pairs={{0,8},{4,12},{8,0},{12,4},{1,9},{5,13},{9,1},{13,5},{2,10},{6,14},... | collective-permute-start | bytes 294920 | tf_op jit(solution)/shard_map/ppermute | solution.py:292
  7.9 0.3 %collective-permute-done.b_ref = bf16[4,3072]{1,0:T(4,128)(2,1)S(1)} collective-permute-done((bf16[4,3072]{1,0:T(4,128)(2,1)S(1)}, bf16[4,3072]{1,0:T(4,128)(2,1)S(1)}, u32[]{:S(2)}, u32[]{:S(2)}) %collective-permute-start) | collective-permute-done | bytes 24608 | tf_op jit(solution)/shard_map/ppermute | solution.py:292
  8.2 0.0 copy-start
  8.2 2.0 %collective-permute-start.4 = (bf16[8,3072]{1,0:T(8,128)(2,1)S(1)}, bf16[8,3072]{1,0:T(8,128)(2,1)S(1)}, u32[]{:S(2)}, u32[]{:S(2)}) collective-permute-start(bf16[8,3072]{1,0:T(8,128)(2,1)S(1)} %shard_map.97.after_ref.a_ref), channel_id=1, source_target_pairs={{0,1},{1,0},{2,3},{3,2},{4,5},{5,4},{6,7},{7,6},{8,9},{9,8},{10,11... | collective-permute-start | bytes 147464 | tf_op jit(solution)/shard_map/ppermute | solution.py:292
  10.2 0.0 collective-permute-start.2
  10.2 0.0 copy-done.3
  10.2 0.7 %shard_map.98 = (bf16[256,1536]{1,0:T(8,128)(2,1)S(1)}, f32[12,64,256]{2,1,0:T(8,128)S(1)}, bf16[256,48]{1,0:T(8,128)(2,1)S(1)}) custom-call(f32[8,128]{1,0:T(8,128)S(1)} %get-tuple-element.33.valid_ref, f32[24,256]{1,0:T(8,128)S(1)} %get-tuple-element.34.member_ref, bf16[256,1536]{1,0:T(8,128)(2,1)S(1)} %copy-done.3, bf16[256,1536]{1,0:T(8,128)(2,1)S(1)} %copy-done.2, ...), custom_call_target="tpu_custom_call" | custom-call | flops 100663296 | bytes 3145728 | tf_op jit(solution)/shard_map/pallas_call | solution.py:41
  10.9 0.1 collective-permute-done.1.after_ref.refs_1_
  11.0 0.5 %collective-permute-start.3 = (bf16[16,3072]{1,0:T(8,128)(2,1)S(1)}, bf16[16,3072]{1,0:T(8,128)(2,1)S(1)}, u32[]{:S(2)}, u32[]{:S(2)}) collective-permute-start(bf16[16,3072]{1,0:T(8,128)(2,1)S(1)} %collective-permute-done.1.after_ref.refs_1_), channel_id=1, source_target_pairs={{0,4},{4,0},{8,12},{12,8},{1,5},{5,1},{9,13},{13,9},{2,6},{6,2},{1... | collective-permute-start | bytes 294920 | tf_op jit(solution)/shard_map/ppermute | solution.py:292
  11.5 0.0 copy-done
  11.5 0.7 %shard_map.99 = (f32[12,64,256]{2,1,0:T(8,128)S(1)}, f32[12,256]{1,0:T(8,128)S(1)}, f32[12,256]{1,0:T(8,128)S(1)}, f32[12,256]{1,0:T(8,128)S(1)}) custom-call(f32[8,128]{1,0:T(8,128)S(1)} %get-tuple-element.33.valid_ref, bf16[256,1536]{1,0:T(8,128)(2,1)S(1)} %copy-done, bf16[256,1536]{1,0:T(8,128)(2,1)S(1)} %copy-done.1, ...), custom_call_target="tpu_custom_call" | custom-call | flops 100663296 | bytes 3145728 | tf_op jit(solution)/shard_map/pallas_call | solution.py:41
  12.2 0.2 collective-permute-done.4.b_ref
  12.4 0.0 collective-permute-done.2.refs_2_
  12.4 0.0 collective-permute-done.3.refs_3_
  12.4 1.2 %shard_map.101 = (bf16[12,80,256]{2,1,0:T(8,128)(2,1)S(1)}, f32[12,256]{1,0:T(8,128)S(1)}, f32[12,256]{1,0:T(8,128)S(1)}, bf16[32,3072]{1,0:T(8,128)(2,1)S(1)}, ...) custom-call(bf16[256,1536]{1,0:T(8,128)(2,1)S(1)} %copy-done, ...), custom_call_target="tpu_custom_call" | custom-call | flops 251658240 | bytes 3145728 | tf_op jit(solution)/shard_map/pallas_call | solution.py:41
  13.6 0.4 %collective-permute-start.5 = (bf16[32,3072]{1,0:T(8,128)(2,1)S(1)}, bf16[32,3072]{1,0:T(8,128)(2,1)S(1)}, u32[]{:S(2)}, u32[]{:S(2)}) collective-permute-start(bf16[32,3072]{1,0:T(8,128)(2,1)S(1)} %get-tuple-element.54), channel_id=1, source_target_pairs={{0,4},{4,0},{8,12},{12,8},{1,5},{5,1},{9,13},{13,9},{2,6},{6,2},{1... | collective-permute-start | bytes 589832 | tf_op jit(solution)/shard_map/ppermute | solution.py:292
  14.0 1.6 %collective-permute-start.7 = (bf16[8,3072]{1,0:T(8,128)(2,1)S(1)}, bf16[8,3072]{1,0:T(8,128)(2,1)S(1)}, u32[]{:S(2)}, u32[]{:S(2)}) collective-permute-start(bf16[8,3072]{1,0:T(8,128)(2,1)S(1)} %get-tuple-element.58), channel_id=1, source_target_pairs={{0,1},{1,0},{2,3},{3,2},{4,5},{5,4},{6,7},{7,6},{8,9},{9,8},{10,11... | collective-permute-start | bytes 147464 | tf_op jit(solution)/shard_map/ppermute | solution.py:292
  15.6 0.7 %shard_map.102 = (bf16[12,128,256]{2,1,0:T(8,128)(2,1)S(1)}, f32[256,1536]{1,0:T(8,128)S(1)}, f32[256,1536]{1,0:T(8,128)S(1)}) custom-call(bf16[256,1536]{1,0:T(8,128)(2,1)S(1)} %copy-done, bf16[256,1536]{1,0:T(8,128)(2,1)S(1)} %get-tuple-element.39.g_ref, f32[12,64,256]{2,1,0:T(8,128)S(1)} %get-tuple-element.42.e_ref, ...), custom_call_target="tpu_custom_call" | custom-call | flops 201326592 | bytes 6291456 | tf_op jit(solution)/shard_map/pallas_call | solution.py:41
  16.3 0.0 collective-permute-done.5.b_ref
  16.3 0.1 shard_map.104
  16.4 1.5 %collective-permute-start.6 = (bf16[16,3072]{1,0:T(8,128)(2,1)S(1)}, bf16[16,3072]{1,0:T(8,128)(2,1)S(1)}, u32[]{:S(2)}, u32[]{:S(2)}) collective-permute-start(bf16[16,3072]{1,0:T(8,128)(2,1)S(1)} %get-tuple-element.56), channel_id=1, source_target_pairs={{0,8},{4,12},{8,0},{12,4},{1,9},{5,13},{9,1},{13,5},{2,10},{6,14},... | collective-permute-start | bytes 294920 | tf_op jit(solution)/shard_map/ppermute | solution.py:292
  17.9 0.2 collective-permute-done.7.b_ref
  18.1 2.8 %collective-permute-start.8 = (bf16[4,3072]{1,0:T(4,128)(2,1)S(1)}, bf16[4,3072]{1,0:T(4,128)(2,1)S(1)}, u32[]{:S(2)}, u32[]{:S(2)}) collective-permute-start(bf16[4,3072]{1,0:T(4,128)(2,1)S(1)} %get-tuple-element.60), channel_id=1, source_target_pairs={{0,2},{1,3},{2,0},{3,1},{4,6},{5,7},{6,4},{7,5},{8,10},{9,11},{10,... | collective-permute-start | bytes 73736 | tf_op jit(solution)/shard_map/ppermute | solution.py:292
  20.9 1.5 %shard_map.103 = bf16[256,1536]{1,0:T(8,128)(2,1)} custom-call(bf16[256,1536]{1,0:T(8,128)(2,1)S(1)} %copy-done.1, bf16[12,128,256]{2,1,0:T(8,128)(2,1)S(1)} %get-tuple-element.48.ds_ref, bf16[12,80,256]{2,1,0:T(8,128)(2,1)S(1)} %get-tuple-element.49.dsc_ref, bf16[16,3072]{1,0:T(8,128)(2,1)S(1)} %get-tuple-element.41.refs_0_, ...), custom_call_target="tpu_custom_call" | custom-call | flops 163577856 | bytes 2359296 | tf_op jit(solution)/shard_map/pallas_call | solution.py:41
  22.4 0.5 %collective-permute-done.8.refs_3_ = bf16[4,3072]{1,0:T(4,128)(2,1)S(1)} collective-permute-done((bf16[4,3072]{1,0:T(4,128)(2,1)S(1)}, bf16[4,3072]{1,0:T(4,128)(2,1)S(1)}, u32[]{:S(2)}, u32[]{:S(2)}) %collective-permute-start.8) | collective-permute-done | bytes 24608 | tf_op jit(solution)/shard_map/ppermute | solution.py:292
  22.9 0.0 collective-permute-done.6.refs_1_
  22.9 1.5 %shard_map.106 = (bf16[256,1536]{1,0:T(8,128)(2,1)}, bf16[256,1536]{1,0:T(8,128)(2,1)}) custom-call(bf16[256,48]{1,0:T(8,128)(2,1)S(1)} %get-tuple-element.50.table_ref, f32[24,128]{1,0:T(8,128)S(1)} %get-tuple-element.35.share_ref, f32[256,1536]{1,0:T(8,128)S(1)} %get-tuple-element.51.refs_0_.dk_ref, f32[256,1536]{1,0:T(8,128)S(1)} %get-tuple-element.52.dv_ref, ...), custom_call_target="tpu_custom_call" | custom-call | flops 75497472 | bytes 4718592 | tf_op jit(solution)/shard_map/pallas_call | solution.py:41
  (6 shorter events, 0.1 us)
Async XLA Ops:
  0.6 0.8 %copy-start.4 = (s32[256]{0:T(256)S(1)}, s32[256]{0:T(256)}, u32[]{:S(2)}) copy-start(s32[256]{0:T(256)} %param.12) | copy-start | bytes 3076
  0.6 0.8 %copy-start.5 = (s32[256]{0:T(256)S(1)}, s32[256]{0:T(256)}, u32[]{:S(2)}) copy-start(s32[256]{0:T(256)} %param.11) | copy-start | bytes 3076
  0.7 1.2 %copy-start.1 = (bf16[256,1536]{1,0:T(8,128)(2,1)S(1)}, bf16[256,1536]{1,0:T(8,128)(2,1)}, u32[]{:S(2)}) copy-start(bf16[256,1536]{1,0:T(8,128)(2,1)} %k_ref.5) | copy-start | bytes 2359300
  0.7 1.4 %copy-start.2 = (bf16[256,1536]{1,0:T(8,128)(2,1)S(1)}, bf16[256,1536]{1,0:T(8,128)(2,1)}, u32[]{:S(2)}) copy-start(bf16[256,1536]{1,0:T(8,128)(2,1)} %v_ref.3) | copy-start | bytes 2359300
  2.3 5.9 %collective-permute-start = (bf16[4,3072]{1,0:T(4,128)(2,1)S(1)}, bf16[4,3072]{1,0:T(4,128)(2,1)S(1)}, u32[]{:S(2)}, u32[]{:S(2)}) collective-permute-start(bf16[4,3072]{1,0:T(4,128)(2,1)S(1)} %get-tuple-element.38.a_ref), channel_id=1, source_target_pairs={{0,2},{1,3},{2,0},{3,1},{4,6},{5,7},{6,4},{7,5},{8,10},{9,11},{10,... | collective-permute-start | bytes 73736 | tf_op jit(solution)/shard_map/ppermute | solution.py:292
  6.4 3.8 %copy-start.3 = (bf16[256,1536]{1,0:T(8,128)(2,1)S(1)}, bf16[256,1536]{1,0:T(8,128)(2,1)}, u32[]{:S(2)}) copy-start(bf16[256,1536]{1,0:T(8,128)(2,1)} %raw_ref.1) | copy-start | bytes 2359300
  6.4 4.6 %collective-permute-start.1 = (bf16[16,3072]{1,0:T(8,128)(2,1)S(1)}, bf16[16,3072]{1,0:T(8,128)(2,1)S(1)}, u32[]{:S(2)}, u32[]{:S(2)}) collective-permute-start(bf16[16,3072]{1,0:T(8,128)(2,1)S(1)} %get-tuple-element.41.refs_0_), channel_id=1, source_target_pairs={{0,8},{4,12},{8,0},{12,4},{1,9},{5,13},{9,1},{13,5},{2,10},{6,14},... | collective-permute-start | bytes 294920 | tf_op jit(solution)/shard_map/ppermute | solution.py:292
  8.2 3.3 %copy-start = (bf16[256,1536]{1,0:T(8,128)(2,1)S(1)}, bf16[256,1536]{1,0:T(8,128)(2,1)}, u32[]{:S(2)}) copy-start(bf16[256,1536]{1,0:T(8,128)(2,1)} %q_ref.5) | copy-start | bytes 2359300
  8.2 4.2 %collective-permute-start.4 = (bf16[8,3072]{1,0:T(8,128)(2,1)S(1)}, bf16[8,3072]{1,0:T(8,128)(2,1)S(1)}, u32[]{:S(2)}, u32[]{:S(2)}) collective-permute-start(bf16[8,3072]{1,0:T(8,128)(2,1)S(1)} %shard_map.97.after_ref.a_ref), channel_id=1, source_target_pairs={{0,1},{1,0},{2,3},{3,2},{4,5},{5,4},{6,7},{7,6},{8,9},{9,8},{10,11... | collective-permute-start | bytes 147464 | tf_op jit(solution)/shard_map/ppermute | solution.py:292
  10.2 2.2 %collective-permute-start.2 = (bf16[16,3072]{1,0:T(8,128)(2,1)S(1)}, bf16[16,3072]{1,0:T(8,128)(2,1)S(1)}, u32[]{:S(2)}, u32[]{:S(2)}) collective-permute-start(bf16[16,3072]{1,0:T(8,128)(2,1)S(1)} %get-tuple-element.41.refs_0_), channel_id=1, source_target_pairs={{0,4},{4,0},{8,12},{12,8},{1,5},{5,1},{9,13},{13,9},{2,6},{6,2},{1... | collective-permute-start | bytes 294920 | tf_op jit(solution)/shard_map/ppermute | solution.py:292
  11.0 1.4 %collective-permute-start.3 = (bf16[16,3072]{1,0:T(8,128)(2,1)S(1)}, bf16[16,3072]{1,0:T(8,128)(2,1)S(1)}, u32[]{:S(2)}, u32[]{:S(2)}) collective-permute-start(bf16[16,3072]{1,0:T(8,128)(2,1)S(1)} %collective-permute-done.1.after_ref.refs_1_), channel_id=1, source_target_pairs={{0,4},{4,0},{8,12},{12,8},{1,5},{5,1},{9,13},{13,9},{2,6},{6,2},{1... | collective-permute-start | bytes 294920 | tf_op jit(solution)/shard_map/ppermute | solution.py:292
  13.6 2.7 %collective-permute-start.5 = (bf16[32,3072]{1,0:T(8,128)(2,1)S(1)}, bf16[32,3072]{1,0:T(8,128)(2,1)S(1)}, u32[]{:S(2)}, u32[]{:S(2)}) collective-permute-start(bf16[32,3072]{1,0:T(8,128)(2,1)S(1)} %get-tuple-element.54), channel_id=1, source_target_pairs={{0,4},{4,0},{8,12},{12,8},{1,5},{5,1},{9,13},{13,9},{2,6},{6,2},{1... | collective-permute-start | bytes 589832 | tf_op jit(solution)/shard_map/ppermute | solution.py:292
  14.0 4.1 %collective-permute-start.7 = (bf16[8,3072]{1,0:T(8,128)(2,1)S(1)}, bf16[8,3072]{1,0:T(8,128)(2,1)S(1)}, u32[]{:S(2)}, u32[]{:S(2)}) collective-permute-start(bf16[8,3072]{1,0:T(8,128)(2,1)S(1)} %get-tuple-element.58), channel_id=1, source_target_pairs={{0,1},{1,0},{2,3},{3,2},{4,5},{5,4},{6,7},{7,6},{8,9},{9,8},{10,11... | collective-permute-start | bytes 147464 | tf_op jit(solution)/shard_map/ppermute | solution.py:292
  16.4 6.5 %collective-permute-start.6 = (bf16[16,3072]{1,0:T(8,128)(2,1)S(1)}, bf16[16,3072]{1,0:T(8,128)(2,1)S(1)}, u32[]{:S(2)}, u32[]{:S(2)}) collective-permute-start(bf16[16,3072]{1,0:T(8,128)(2,1)S(1)} %get-tuple-element.56), channel_id=1, source_target_pairs={{0,8},{4,12},{8,0},{12,4},{1,9},{5,13},{9,1},{13,5},{2,10},{6,14},... | collective-permute-start | bytes 294920 | tf_op jit(solution)/shard_map/ppermute | solution.py:292
  18.1 4.8 %collective-permute-start.8 = (bf16[4,3072]{1,0:T(4,128)(2,1)S(1)}, bf16[4,3072]{1,0:T(4,128)(2,1)S(1)}, u32[]{:S(2)}, u32[]{:S(2)}) collective-permute-start(bf16[4,3072]{1,0:T(4,128)(2,1)S(1)} %get-tuple-element.60), channel_id=1, source_target_pairs={{0,2},{1,3},{2,0},{3,1},{4,6},{5,7},{6,4},{7,5},{8,10},{9,11},{10,... | collective-permute-start | bytes 73736 | tf_op jit(solution)/shard_map/ppermute | solution.py:292

commit v6 on v5

--- a/solution.py
+++ b/solution.py
@@ -17,6 +17,7 @@
 SPAN = WIN_FRAME * WIN
 ROWS = KF + 8
 CHUNK = 512
+EARLY = 6
 
 MASK_FILL = -1e30
 FACTOR = HD ** (-0.5)
@@ -97,30 +98,41 @@
     send_ref[...] = total[amount:].astype(jnp.bfloat16)
 
 
-def value_kernel(
-    valid_ref, member_ref, raw_ref, v_ref, after_ref, g_ref, d_ref, table_ref
-):
+def value_products(h, g_ref, v_ref):
+    at = slice(h * HD, (h + 1) * HD)
+    first = lax.broadcasted_iota(jnp.int32, (WIN, PAIR), 1) < WIN
+    for p in range(v_ref.shape[0] // PAIR):
+        rows = slice(p * PAIR, (p + 1) * PAIR)
+        d = dot(v_ref[rows, at], g_ref[rows, at], NT)
+        yield rows, jnp.where(first, d[:WIN], d[WIN:])
+
+
+def value_kernel(valid_ref, raw_ref, v_ref, after_ref, g_ref, d_ref):
     del after_ref
     length, features = raw_ref.shape
-    member = member_ref[...]
-    blank = jnp.zeros((HD - 2 * ROWS, length), jnp.float32)
-    table = jnp.concatenate([member, member, blank], axis=0)
-    table_ref[...] = table.T[:, : 2 * ROWS].astype(jnp.bfloat16)
     valid = valid_ref[:1].astype(jnp.int32)
     live = lax.broadcasted_iota(jnp.int32, (length, HD), 0) % SPAN < valid
-    first = lax.broadcasted_iota(jnp.int32, (WIN, PAIR), 1) < WIN
     for h in range(features // HD):
         at = slice(h * HD, (h + 1) * HD)
-        g = jnp.where(live, raw_ref[:, at], 0)
-        g_ref[:, at] = g
-        for p in range(length // PAIR):
-            rows = slice(p * PAIR, (p + 1) * PAIR)
-            d = dot(v_ref[rows, at], g[rows], NT)
-            d_ref[h, :, rows] = jnp.where(first, d[:WIN], d[WIN:])
+        g_ref[:, at] = jnp.where(live, raw_ref[:, at], 0)
+    for h in range(d_ref.shape[0]):
+        for rows, d in value_products(h, g_ref, v_ref):
+            d_ref[h, :, rows] = d
 
 
 def window_kernel(
-    valid_ref, q_ref, k_ref, d_ref, after_ref, e_ref, top_ref, sum_ref, dot_ref
+    valid_ref,
+    q_ref,
+    k_ref,
+    g_ref,
+    v_ref,
+    d_early,
+    after_ref,
+    d_late,
+    e_ref,
+    top_ref,
+    sum_ref,
+    dot_ref,
 ):
     del after_ref
     length, features = q_ref.shape
@@ -129,27 +141,36 @@
     row = lax.broadcasted_iota(jnp.int32, (WIN, PAIR), 0)
     first = lane < WIN
     place = row + jnp.where(first, 0, WIN)
-    steps = [(h, p) for h in range(features // HD) for p in range(length // PAIR)]
-
-    def products(h, p):
-        rows = slice(p * PAIR, (p + 1) * PAIR)
+    early = d_early.shape[0]
+
+    def products(h):
         at = slice(h * HD, (h + 1) * HD)
-        return dot(k_ref[rows, at], q_ref[rows, at], NT)
-
-    ahead = products(*steps[0])
-    for step, (h, p) in enumerate(steps):
-        s = ahead
-        if step + 1 < len(steps):
-            ahead = products(*steps[step + 1])
-        rows = slice(p * PAIR, (p + 1) * PAIR)
-        s = jnp.where(first, s[:WIN], s[WIN:])
-        s = jnp.where((place + p * PAIR) % SPAN < valid, s, MASK_FILL)
-        top = jnp.max(s, axis=0, keepdims=True)
-        e = jnp.exp2((s - top) * SCALE)
-        e_ref[h, :, rows] = e
-        top_ref[h : h + 1, rows] = top
-        sum_ref[h : h + 1, rows] = jnp.sum(e, axis=0, keepdims=True)
-        dot_ref[h : h + 1, rows] = jnp.sum(e * d_ref[h, :, rows], axis=0, keepdims=True)
+        if h < early:
+            ds = [
+                (slice(p * PAIR, (p + 1) * PAIR), d_early[h, :, p * PAIR : (p + 1) * PAIR])
+                for p in range(length // PAIR)
+            ]
+        else:
+            ds = list(value_products(h, g_ref, v_ref))
+            for rows, d in ds:
+                d_late[h - early, :, rows] = d
+        return [(rows, dot(k_ref[rows, at], q_ref[rows, at], NT), d) for rows, d in ds]
+
+    heads = features // HD
+    ahead = products(0)
+    for h in range(heads):
+        now = ahead
+        if h + 1 < heads:
+            ahead = products(h + 1)
+        for rows, s, d in now:
+            s = jnp.where(first, s[:WIN], s[WIN:])
+            s = jnp.where((place + rows.start) % SPAN < valid, s, MASK_FILL)
+            top = jnp.max(s, axis=0, keepdims=True)
+            e = jnp.exp2((s - top) * SCALE)
+            e_ref[h, :, rows] = e
+            top_ref[h : h + 1, rows] = top
+            sum_ref[h : h + 1, rows] = jnp.sum(e, axis=0, keepdims=True)
+            dot_ref[h : h + 1, rows] = jnp.sum(e * d, axis=0, keepdims=True)
 
 
 def coarse_rows(refs, at):
@@ -209,7 +230,7 @@
 
 
 def local_kernel(
-    q_ref, g_ref, e_ref, d_ref, weight_ref, delta_ref, ds_ref, dk_ref, dv_ref
+    q_ref, g_ref, e_ref, d_early, d_late, weight_ref, delta_ref, ds_ref, dk_ref, dv_ref
 ):
     length, features = q_ref.shape
     first = lax.broadcasted_iota(jnp.int32, (WIN, PAIR), 1) < WIN
@@ -219,22 +240,28 @@
             [jnp.where(first, x, 0.0), jnp.where(first, 0.0, x)], axis=0
         ).astype(jnp.bfloat16)
 
+    early = d_early.shape[0]
     for h in range(features // HD):
         at = slice(h * HD, (h + 1) * HD)
+        d_ref, i = (d_early, h) if h < early else (d_late, h - early)
         for p in range(length // PAIR):
             rows = slice(p * PAIR, (p + 1) * PAIR)
             w = e_ref[h, :, rows] * weight_ref[h : h + 1, rows]
-            ds = (FACTOR * w) * (d_ref[h, :, rows] - delta_ref[h : h + 1, rows])
+            ds = (FACTOR * w) * (d_ref[i, :, rows] - delta_ref[h : h + 1, rows])
             ds = split(ds)
             ds_ref[h, :, rows] = ds
             dk_ref[rows, at] = dot(ds, q_ref[rows, at], NN)
             dv_ref[rows, at] = dot(split(w), g_ref[rows, at], NN)
 
 
-def query_kernel(parts, k_ref, ds_ref, dsc_ref, *refs):
+def query_kernel(parts, member_ref, k_ref, ds_ref, dsc_ref, *refs):
     coarse = refs[:parts]
-    dq_ref = refs[parts]
+    dq_ref, table_ref = refs[parts:]
     length, features = k_ref.shape
+    member = member_ref[...]
+    blank = jnp.zeros((HD - 2 * ROWS, length), jnp.float32)
+    table = jnp.concatenate([member, member, blank], axis=0)
+    table_ref[...] = table.T[:, : 2 * ROWS].astype(jnp.bfloat16)
     for h in range(features // HD):
         at = h * HD
         kc = coarse_rows(coarse, at)
@@ -342,17 +369,18 @@
     total = tm * KF + space * KT
 
     wide = shape((heads, WIN, length), f32)
-    g, d, table = call(
+    early = heads * EARLY // 12
+    g, d_early = call(
         value_kernel,
-        [block, wide, shape((length, 2 * ROWS), bf16)],
-        [(x, VMEM) for x in (valid, member, grad_out, value_in)] + [(have_t, ANY)],
+        [block, shape((early, WIN, length), f32)],
+        [(x, VMEM) for x in (valid, grad_out, value_in)] + [(have_t, ANY)],
         2 * size * PAIR,
         8 * size,
     )
-    e, top, window_sum, window_dot = call(
+    d_late, e, top, window_sum, window_dot = call(
         window_kernel,
-        [wide, stat, stat, stat],
-        [(x, VMEM) for x in (valid, query, key_in, d)] + [(from_2, ANY)],
+        [shape((heads - early, WIN, length), f32), wide, stat, stat, stat],
+        [(x, VMEM) for x in (valid, query, key_in, g, value_in, d_early)] + [(from_2, ANY)],
         2 * size * PAIR,
         8 * size,
     )
@@ -372,7 +400,7 @@
     ds, dk, dv = call(
         local_kernel,
         [shape((heads, PAIR, length), bf16), sums, sums],
-        [(x, VMEM) for x in (query, g, e, d, weight, delta)],
+        [(x, VMEM) for x in (query, g, e, d_early, d_late, weight, delta)],
         4 * size * PAIR,
         16 * size,
     )
@@ -383,16 +411,16 @@
 
     for mask in masks[:0:-1]:
         t_keep, t_send = halve(
-            t_keep, swap(t_send, "space", space, mask), JOIN_FLOPS, [dk]
+            t_keep, swap(t_send, "space", space, mask), 3 * 10**8, [dk]
         )
     got_t = swap(t_send, "space", space, masks[0])
     f_keep, f_send = halve(f_keep, swap(f_send, "tm", tm, 1), 0)
     got_f = swap(f_send, "tm", tm, 2)
 
-    (query_grad,) = call(
+    query_grad, table = call(
         functools.partial(query_kernel, len(coarse)),
-        [block],
-        [(x, VMEM) for x in (key_in, ds, dsc)] + coarse_in,
+        [block, shape((length, 2 * ROWS), bf16)],
+        [(x, VMEM) for x in (member, key_in, ds, dsc)] + coarse_in,
         2 * size * (PAIR + total),
         6 * size,
     )

time: 24.5 us -> 24.4 us (level)
  transfers between devices with their start and end apart: 9 -> 9, of which waited for: 5 -> 4; matrix products, arithmetic and copies ran while one was open for 0% -> 0% of each run, Pallas kernels for 15% -> 15%
where the time goes in v6:
time: 24.4 us; the launch traced here: 24.3 us
  starting transfers between devices  14.2 us (58%)
  Pallas kernels  6.84 us (28%)
  between operations  1.54 us (6%)
  waiting for transfers between devices  1.3 us (5%)
  local copies, waits for them, and re-layouts  0.35 us (1%)
    ppermute x9, starting transfers between devices, swap(): return lax.ppermute(x, axis, [(i, i ^ mask) for i in range(size)])  14.2 us
    pallas_call x13, Pallas kernels, call(): pl.pallas_call(kernel, out_shape=outs, in_specs=[spec for _, spec in ins]...  6.84 us
    ppermute x9, waiting for transfers between devices, swap(): return lax.ppermute(x, axis, [(i, i ^ mask) for i in range(size)])  1.3 us
  transfers between devices with their start and end apart: 9, of which 4 were waited for; matrix products, arithmetic and copies ran while one was open for 0% of the time, Pallas kernels for 15%

profile of v6, /device:TPU:0, one launch (start us, length us, event | category | flops | bytes accessed | tf_op | source)
XLA Modules:
  0.0 24.3 jit_solution(3323058067249849177)
XLA Ops:
  0.6 0.0 copy-start.4
  0.6 0.0 copy-start.5
  0.7 0.0 copy-start.2
  0.7 0.0 copy-start
  1.4 0.0 copy-done.4
  1.5 0.0 copy-done.5
  1.5 0.3 %copy-done.2 = bf16[256,1536]{1,0:T(8,128)(2,1)S(1)} copy-done((bf16[256,1536]{1,0:T(8,128)(2,1)S(1)}, bf16[256,1536]{1,0:T(8,128)(2,1)}, u32[]{:S(2)}) %copy-start.2) | copy-done | bytes 786456
  1.8 0.2 shard_map.95
  2.0 0.0 copy-done
  2.1 0.2 shard_map.96
  2.3 4.1 %collective-permute-start = (bf16[4,3072]{1,0:T(4,128)(2,1)S(1)}, bf16[4,3072]{1,0:T(4,128)(2,1)S(1)}, u32[]{:S(2)}, u32[]{:S(2)}) collective-permute-start(bf16[4,3072]{1,0:T(4,128)(2,1)S(1)} %get-tuple-element.40.a_ref), channel_id=1, source_target_pairs={{0,2},{1,3},{2,0},{3,1},{4,6},{5,7},{6,4},{7,5},{8,10},{9,11},{10,... | collective-permute-start | bytes 73736 | tf_op jit(solution)/shard_map/ppermute | solution.py:319
  6.4 0.0 copy-start.3
  6.4 1.5 %collective-permute-start.1 = (bf16[16,3072]{1,0:T(8,128)(2,1)S(1)}, bf16[16,3072]{1,0:T(8,128)(2,1)S(1)}, u32[]{:S(2)}, u32[]{:S(2)}) collective-permute-start(bf16[16,3072]{1,0:T(8,128)(2,1)S(1)} %get-tuple-element.43.refs_0_), channel_id=1, source_target_pairs={{0,8},{4,12},{8,0},{12,4},{1,9},{5,13},{9,1},{13,5},{2,10},{6,14},... | collective-permute-start | bytes 294920 | tf_op jit(solution)/shard_map/ppermute | solution.py:319
  7.9 0.3 %collective-permute-done.b_ref = bf16[4,3072]{1,0:T(4,128)(2,1)S(1)} collective-permute-done((bf16[4,3072]{1,0:T(4,128)(2,1)S(1)}, bf16[4,3072]{1,0:T(4,128)(2,1)S(1)}, u32[]{:S(2)}, u32[]{:S(2)}) %collective-permute-start) | collective-permute-done | bytes 24608 | tf_op jit(solution)/shard_map/ppermute | solution.py:319
  8.2 0.0 copy-start.1
  8.2 2.0 %collective-permute-start.4 = (bf16[8,3072]{1,0:T(8,128)(2,1)S(1)}, bf16[8,3072]{1,0:T(8,128)(2,1)S(1)}, u32[]{:S(2)}, u32[]{:S(2)}) collective-permute-start(bf16[8,3072]{1,0:T(8,128)(2,1)S(1)} %shard_map.97.after_ref.a_ref), channel_id=1, source_target_pairs={{0,1},{1,0},{2,3},{3,2},{4,5},{5,4},{6,7},{7,6},{8,9},{9,8},{10,11... | collective-permute-start | bytes 147464 | tf_op jit(solution)/shard_map/ppermute | solution.py:319
  10.2 0.0 collective-permute-start.2
  10.2 0.0 copy-done.3
  10.2 0.5 %shard_map.98 = (bf16[256,1536]{1,0:T(8,128)(2,1)S(1)}, f32[6,64,256]{2,1,0:T(8,128)S(1)}) custom-call(f32[8,128]{1,0:T(8,128)S(1)} %get-tuple-element.36.valid_ref, bf16[256,1536]{1,0:T(8,128)(2,1)S(1)} %copy-done.3, bf16[256,1536]{1,0:T(8,128)(2,1)S(1)} %copy-done, bf16[8,3072]{1,0:T(8,128)(2,1)S(1)} %shard_map.97.after_ref.a_ref), custom_call_target="tpu_custom_call" | custom-call | flops 100663296 | bytes 3145728 | tf_op jit(solution)/shard_map/pallas_call | solution.py:42
  10.7 0.3 %collective-permute-done.1.after_ref.refs_1_ = bf16[16,3072]{1,0:T(8,128)(2,1)S(1)} collective-permute-done((bf16[16,3072]{1,0:T(8,128)(2,1)S(1)}, bf16[16,3072]{1,0:T(8,128)(2,1)S(1)}, u32[]{:S(2)}, u32[]{:S(2)}) %collective-permute-start.1) | collective-permute-done | bytes 98336 | tf_op jit(solution)/shard_map/ppermute | solution.py:319
  11.0 0.3 %collective-permute-start.3 = (bf16[16,3072]{1,0:T(8,128)(2,1)S(1)}, bf16[16,3072]{1,0:T(8,128)(2,1)S(1)}, u32[]{:S(2)}, u32[]{:S(2)}) collective-permute-start(bf16[16,3072]{1,0:T(8,128)(2,1)S(1)} %collective-permute-done.1.after_ref.refs_1_), channel_id=1, source_target_pairs={{0,4},{4,0},{8,12},{12,8},{1,5},{5,1},{9,13},{13,9},{2,6},{6,2},{1... | collective-permute-start | bytes 294920 | tf_op jit(solution)/shard_map/ppermute | solution.py:319
  11.3 0.0 copy-done.1
  11.3 1.0 %shard_map.99 = (f32[6,64,256]{2,1,0:T(8,128)S(1)}, f32[12,64,256]{2,1,0:T(8,128)S(1)}, f32[12,256]{1,0:T(8,128)S(1)}, f32[12,256]{1,0:T(8,128)S(1)}, f32[12,256]{1,0:T(8,128)S(1)}) custom-call(f32[8,128]{1,0:T(8,128)S(1)} %get-tuple-element.36.valid_ref, bf16[256,1536]{1,0:T(8,128)(2,1)S(1)} %copy-done.1, bf16[256,1536]{1,0:T(8,128)(2,1)S(1)} %copy-done.2, ...), custom_call_target="tpu_custom_call" | custom-call | flops 100663296 | bytes 3145728 | tf_op jit(solution)/shard_map/pallas_call | solution.py:42
  12.2 0.1 collective-permute-done.4.b_ref
  12.4 0.0 collective-permute-done.2.refs_2_
  12.4 0.0 collective-permute-done.3.refs_3_
  12.4 1.2 %shard_map.101 = (bf16[12,80,256]{2,1,0:T(8,128)(2,1)S(1)}, f32[12,256]{1,0:T(8,128)S(1)}, f32[12,256]{1,0:T(8,128)S(1)}, bf16[32,3072]{1,0:T(8,128)(2,1)S(1)}, ...) custom-call(bf16[256,1536]{1,0:T(8,128)(2,1)S(1)} %copy-done.1, ...), custom_call_target="tpu_custom_call" | custom-call | flops 251658240 | bytes 3145728 | tf_op jit(solution)/shard_map/pallas_call | solution.py:42
  13.6 0.2 collective-permute-start.5
  13.8 1.8 %collective-permute-start.7 = (bf16[8,3072]{1,0:T(8,128)(2,1)S(1)}, bf16[8,3072]{1,0:T(8,128)(2,1)S(1)}, u32[]{:S(2)}, u32[]{:S(2)}) collective-permute-start(bf16[8,3072]{1,0:T(8,128)(2,1)S(1)} %get-tuple-element.62), channel_id=1, source_target_pairs={{0,1},{1,0},{2,3},{3,2},{4,5},{5,4},{6,7},{7,6},{8,9},{9,8},{10,11... | collective-permute-start | bytes 147464 | tf_op jit(solution)/shard_map/ppermute | solution.py:319
  15.6 0.0 collective-permute-done.5.b_ref
  15.6 0.1 shard_map.104
  15.7 1.5 %collective-permute-start.6 = (bf16[16,3072]{1,0:T(8,128)(2,1)S(1)}, bf16[16,3072]{1,0:T(8,128)(2,1)S(1)}, u32[]{:S(2)}, u32[]{:S(2)}) collective-permute-start(bf16[16,3072]{1,0:T(8,128)(2,1)S(1)} %get-tuple-element.60), channel_id=1, source_target_pairs={{0,8},{4,12},{8,0},{12,4},{1,9},{5,13},{9,1},{13,5},{2,10},{6,14},... | collective-permute-start | bytes 294920 | tf_op jit(solution)/shard_map/ppermute | solution.py:319
  17.2 0.7 %shard_map.102 = (bf16[12,128,256]{2,1,0:T(8,128)(2,1)S(1)}, f32[256,1536]{1,0:T(8,128)S(1)}, f32[256,1536]{1,0:T(8,128)S(1)}) custom-call(bf16[256,1536]{1,0:T(8,128)(2,1)S(1)} %copy-done.1, bf16[256,1536]{1,0:T(8,128)(2,1)S(1)} %get-tuple-element.41.g_ref, f32[12,64,256]{2,1,0:T(8,128)S(1)} %get-tuple-element.44.e_ref, ...), custom_call_target="tpu_custom_call" | custom-call | flops 201326592 | bytes 6291456 | tf_op jit(solution)/shard_map/pallas_call | solution.py:42
  17.9 0.0 collective-permute-done.7.b_ref
  18.0 2.8 %collective-permute-start.8 = (bf16[4,3072]{1,0:T(4,128)(2,1)S(1)}, bf16[4,3072]{1,0:T(4,128)(2,1)S(1)}, u32[]{:S(2)}, u32[]{:S(2)}) collective-permute-start(bf16[4,3072]{1,0:T(4,128)(2,1)S(1)} %get-tuple-element.64), channel_id=1, source_target_pairs={{0,2},{1,3},{2,0},{3,1},{4,6},{5,7},{6,4},{7,5},{8,10},{9,11},{10,... | collective-permute-start | bytes 73736 | tf_op jit(solution)/shard_map/ppermute | solution.py:319
  20.8 1.5 %shard_map.103 = (bf16[256,1536]{1,0:T(8,128)(2,1)}, bf16[256,48]{1,0:T(8,128)(2,1)S(1)}) custom-call(f32[24,256]{1,0:T(8,128)S(1)} %get-tuple-element.35.member_ref, bf16[256,1536]{1,0:T(8,128)(2,1)S(1)} %copy-done.2, bf16[12,128,256]{2,1,0:T(8,128)(2,1)S(1)} %get-tuple-element.51.ds_ref, bf16[12,80,256]{2,1,0:T(8,128)(2,1)S(1)} %get-tuple-element.52.dsc_ref, ...), custom_call_target="tpu_custom_call" | custom-call | flops 163577856 | bytes 2359296 | tf_op jit(solution)/shard_map/pallas_call | solution.py:42
  22.3 0.5 %collective-permute-done.8.refs_3_ = bf16[4,3072]{1,0:T(4,128)(2,1)S(1)} collective-permute-done((bf16[4,3072]{1,0:T(4,128)(2,1)S(1)}, bf16[4,3072]{1,0:T(4,128)(2,1)S(1)}, u32[]{:S(2)}, u32[]{:S(2)}) %collective-permute-start.8) | collective-permute-done | bytes 24608 | tf_op jit(solution)/shard_map/ppermute | solution.py:319
  22.8 0.0 collective-permute-done.6.refs_1_
  22.8 1.5 %shard_map.106 = (bf16[256,1536]{1,0:T(8,128)(2,1)}, bf16[256,1536]{1,0:T(8,128)(2,1)}) custom-call(bf16[256,48]{1,0:T(8,128)(2,1)S(1)} %get-tuple-element.54.table_ref, f32[24,128]{1,0:T(8,128)S(1)} %get-tuple-element.37.share_ref, f32[256,1536]{1,0:T(8,128)S(1)} %get-tuple-element.55.refs_0_.dk_ref, f32[256,1536]{1,0:T(8,128)S(1)} %get-tuple-element.56.dv_ref, ...), custom_call_target="tpu_custom_call" | custom-call | flops 75497472 | bytes 4718592 | tf_op jit(solution)/shard_map/pallas_call | solution.py:42
  (6 shorter events, 0.1 us)
Async XLA Ops:
  0.6 0.8 %copy-start.4 = (s32[256]{0:T(256)S(1)}, s32[256]{0:T(256)}, u32[]{:S(2)}) copy-start(s32[256]{0:T(256)} %param.12) | copy-start | bytes 3076
  0.6 0.8 %copy-start.5 = (s32[256]{0:T(256)S(1)}, s32[256]{0:T(256)}, u32[]{:S(2)}) copy-start(s32[256]{0:T(256)} %param.11) | copy-start | bytes 3076
  0.7 1.2 %copy-start.2 = (bf16[256,1536]{1,0:T(8,128)(2,1)S(1)}, bf16[256,1536]{1,0:T(8,128)(2,1)}, u32[]{:S(2)}) copy-start(bf16[256,1536]{1,0:T(8,128)(2,1)} %k_ref.5) | copy-start | bytes 2359300
  0.7 1.4 %copy-start = (bf16[256,1536]{1,0:T(8,128)(2,1)S(1)}, bf16[256,1536]{1,0:T(8,128)(2,1)}, u32[]{:S(2)}) copy-start(bf16[256,1536]{1,0:T(8,128)(2,1)} %v_ref.5) | copy-start | bytes 2359300
  2.3 5.9 %collective-permute-start = (bf16[4,3072]{1,0:T(4,128)(2,1)S(1)}, bf16[4,3072]{1,0:T(4,128)(2,1)S(1)}, u32[]{:S(2)}, u32[]{:S(2)}) collective-permute-start(bf16[4,3072]{1,0:T(4,128)(2,1)S(1)} %get-tuple-element.40.a_ref), channel_id=1, source_target_pairs={{0,2},{1,3},{2,0},{3,1},{4,6},{5,7},{6,4},{7,5},{8,10},{9,11},{10,... | collective-permute-start | bytes 73736 | tf_op jit(solution)/shard_map/ppermute | solution.py:319
  6.4 3.8 %copy-start.3 = (bf16[256,1536]{1,0:T(8,128)(2,1)S(1)}, bf16[256,1536]{1,0:T(8,128)(2,1)}, u32[]{:S(2)}) copy-start(bf16[256,1536]{1,0:T(8,128)(2,1)} %raw_ref.1) | copy-start | bytes 2359300
  6.4 4.6 %collective-permute-start.1 = (bf16[16,3072]{1,0:T(8,128)(2,1)S(1)}, bf16[16,3072]{1,0:T(8,128)(2,1)S(1)}, u32[]{:S(2)}, u32[]{:S(2)}) collective-permute-start(bf16[16,3072]{1,0:T(8,128)(2,1)S(1)} %get-tuple-element.43.refs_0_), channel_id=1, source_target_pairs={{0,8},{4,12},{8,0},{12,4},{1,9},{5,13},{9,1},{13,5},{2,10},{6,14},... | collective-permute-start | bytes 294920 | tf_op jit(solution)/shard_map/ppermute | solution.py:319
  8.2 3.1 %copy-start.1 = (bf16[256,1536]{1,0:T(8,128)(2,1)S(1)}, bf16[256,1536]{1,0:T(8,128)(2,1)}, u32[]{:S(2)}) copy-start(bf16[256,1536]{1,0:T(8,128)(2,1)} %q_ref.5) | copy-start | bytes 2359300
  8.2 4.2 %collective-permute-start.4 = (bf16[8,3072]{1,0:T(8,128)(2,1)S(1)}, bf16[8,3072]{1,0:T(8,128)(2,1)S(1)}, u32[]{:S(2)}, u32[]{:S(2)}) collective-permute-start(bf16[8,3072]{1,0:T(8,128)(2,1)S(1)} %shard_map.97.after_ref.a_ref), channel_id=1, source_target_pairs={{0,1},{1,0},{2,3},{3,2},{4,5},{5,4},{6,7},{7,6},{8,9},{9,8},{10,11... | collective-permute-start | bytes 147464 | tf_op jit(solution)/shard_map/ppermute | solution.py:319
  10.2 2.2 %collective-permute-start.2 = (bf16[16,3072]{1,0:T(8,128)(2,1)S(1)}, bf16[16,3072]{1,0:T(8,128)(2,1)S(1)}, u32[]{:S(2)}, u32[]{:S(2)}) collective-permute-start(bf16[16,3072]{1,0:T(8,128)(2,1)S(1)} %get-tuple-element.43.refs_0_), channel_id=1, source_target_pairs={{0,4},{4,0},{8,12},{12,8},{1,5},{5,1},{9,13},{13,9},{2,6},{6,2},{1... | collective-permute-start | bytes 294920 | tf_op jit(solution)/shard_map/ppermute | solution.py:319
  11.0 1.4 %collective-permute-start.3 = (bf16[16,3072]{1,0:T(8,128)(2,1)S(1)}, bf16[16,3072]{1,0:T(8,128)(2,1)S(1)}, u32[]{:S(2)}, u32[]{:S(2)}) collective-permute-start(bf16[16,3072]{1,0:T(8,128)(2,1)S(1)} %collective-permute-done.1.after_ref.refs_1_), channel_id=1, source_target_pairs={{0,4},{4,0},{8,12},{12,8},{1,5},{5,1},{9,13},{13,9},{2,6},{6,2},{1... | collective-permute-start | bytes 294920 | tf_op jit(solution)/shard_map/ppermute | solution.py:319
  13.6 2.0 %collective-permute-start.5 = (bf16[32,3072]{1,0:T(8,128)(2,1)S(1)}, bf16[32,3072]{1,0:T(8,128)(2,1)S(1)}, u32[]{:S(2)}, u32[]{:S(2)}) collective-permute-start(bf16[32,3072]{1,0:T(8,128)(2,1)S(1)} %get-tuple-element.58), channel_id=1, source_target_pairs={{0,4},{4,0},{8,12},{12,8},{1,5},{5,1},{9,13},{13,9},{2,6},{6,2},{1... | collective-permute-start | bytes 589832 | tf_op jit(solution)/shard_map/ppermute | solution.py:319
  13.8 4.2 %collective-permute-start.7 = (bf16[8,3072]{1,0:T(8,128)(2,1)S(1)}, bf16[8,3072]{1,0:T(8,128)(2,1)S(1)}, u32[]{:S(2)}, u32[]{:S(2)}) collective-permute-start(bf16[8,3072]{1,0:T(8,128)(2,1)S(1)} %get-tuple-element.62), channel_id=1, source_target_pairs={{0,1},{1,0},{2,3},{3,2},{4,5},{5,4},{6,7},{7,6},{8,9},{9,8},{10,11... | collective-permute-start | bytes 147464 | tf_op jit(solution)/shard_map/ppermute | solution.py:319
  15.7 7.1 %collective-permute-start.6 = (bf16[16,3072]{1,0:T(8,128)(2,1)S(1)}, bf16[16,3072]{1,0:T(8,128)(2,1)S(1)}, u32[]{:S(2)}, u32[]{:S(2)}) collective-permute-start(bf16[16,3072]{1,0:T(8,128)(2,1)S(1)} %get-tuple-element.60), channel_id=1, source_target_pairs={{0,8},{4,12},{8,0},{12,4},{1,9},{5,13},{9,1},{13,5},{2,10},{6,14},... | collective-permute-start | bytes 294920 | tf_op jit(solution)/shard_map/ppermute | solution.py:319
  18.0 4.8 %collective-permute-start.8 = (bf16[4,3072]{1,0:T(4,128)(2,1)S(1)}, bf16[4,3072]{1,0:T(4,128)(2,1)S(1)}, u32[]{:S(2)}, u32[]{:S(2)}) collective-permute-start(bf16[4,3072]{1,0:T(4,128)(2,1)S(1)} %get-tuple-element.64), channel_id=1, source_target_pairs={{0,2},{1,3},{2,0},{3,1},{4,6},{5,7},{6,4},{7,5},{8,10},{9,11},{10,... | collective-permute-start | bytes 73736 | tf_op jit(solution)/shard_map/ppermute | solution.py:319
